TPU v7x, 512 devices: a whole 4x8x8 slice. The times are simulated.
512 devices in a mesh: dp: 64 (over z, y_hi, core), tensor: 8 (over y_lo, x).
Axes of the slice: x: 4, y: 8 (y_hi: 4, y_lo: 2; y = y_hi * 2 + y_lo), z: 8, core: 2. Of those that a mesh axis runs over, the one named last changes fastest.
Arguments:
- activations: bfloat16 [8192, 8192], P('dp'), may hold values from -6 to 6
- norm_gain: bfloat16 [8192], replicated, may hold values from 0.099609375 to 1.8984375
- gate_w: bfloat16 [8192, 14336], P('dp', 'tensor'), may hold values from -0.0625 to 0.0625
- up_w: bfloat16 [8192, 14336], P('dp', 'tensor'), may hold values from -0.0625 to 0.0625
- down_w: bfloat16 [14336, 8192], P('tensor', 'dp'), may hold values from -0.1875 to 0.1875
- mask_gain: bfloat16 [14336], P('tensor'), may hold values from 0.29882812 to 3
- kept_blocks: int32 [8, 2], replicated, may hold values from 0 to 13, as said below
- kept_counts: int32 [8], replicated, may hold values from 0 to 2, as said below
- cotangent: bfloat16 [8192, 8192], P(('dp', 'tensor')), may hold values from -6 to 6
Outputs:
- input_grad: bfloat16 [8192, 8192], P(('dp', 'tensor'))
- gain_grad: float32 [16, 128], P('tensor', 'dp')
Inputs may be any that keep to these rules, and one draw needn't show every extreme that they name: `kept_blocks`: in each row the first 2 entries are distinct; entries past the row's count are padding. `kept_counts`: the counts add up to 8; some shard has 2 and some has 0.
All inputs are finite; a program needn't handle non-finite values.
Results may differ from a plain program's by a relative error of at most 0.015.
Values may be sent and summed in bfloat16 or wider, within the bound.
No kernel may reach another device: no remote copies, remote signals or barrier semaphores. Data moves between devices by JAX's collectives and lax.ppermute only.
A program may use at most 64 MiB of HBM per device.

v0:
```python
import math

import jax
import jax.numpy as jnp
from jax import lax
from jax.sharding import PartitionSpec as P

BLOCK = 128


def per_device(
    activations, norm_gain, gate_w, up_w, down_w, mask_gain, kept_blocks, kept_counts, cotangent
):
    tok_rows, width = activations.shape
    dslice, ff_local = gate_w.shape
    nblocks = ff_local // BLOCK
    tensors = lax.axis_size("tensor")
    mine = lax.axis_index("tensor")
    keep = kept_blocks.shape[1]
    act_float = activations.astype(jnp.float32)
    inv_rms = lax.rsqrt(jnp.mean(act_float * act_float, axis=-1, keepdims=True) + 1e-05)
    normalized = act_float * inv_rms
    gain_float = norm_gain.astype(jnp.float32)
    normed = (normalized * gain_float).astype(jnp.bfloat16)
    gate_blocks = gate_w.reshape(dslice, nblocks, BLOCK)
    up_blocks = up_w.reshape(dslice, nblocks, BLOCK)
    down_blocks = down_w.reshape(nblocks, BLOCK, dslice)
    gain_blocks = mask_gain.reshape(nblocks, BLOCK)
    kept_mine = lax.dynamic_index_in_dim(kept_blocks, mine, 0, keepdims=False)
    count_mine = lax.dynamic_index_in_dim(kept_counts, mine, 0, keepdims=False)
    slot_gate = jnp.take(gate_blocks, kept_mine, axis=1)
    slot_up = jnp.take(up_blocks, kept_mine, axis=1)
    slot_down = jnp.take(down_blocks, kept_mine, axis=0)
    full_gate, full_up, full_down = (
        lax.all_gather(slot_gate, "dp", axis=0, tiled=True),
        lax.all_gather(slot_up, "dp", axis=0, tiled=True),
        lax.all_gather(slot_down, "dp", axis=2, tiled=True),
    )
    w_gate = full_gate.reshape(width, keep * BLOCK)
    w_up = full_up.reshape(width, keep * BLOCK)
    w_down = full_down.reshape(keep * BLOCK, width)
    valid = jnp.repeat((jnp.arange(keep, dtype=jnp.int32) < count_mine).astype(jnp.float32), BLOCK)
    unit_gain = jnp.take(gain_blocks, kept_mine, axis=0).reshape(-1).astype(jnp.float32) * valid
    cot_full = lax.all_gather(cotangent, "tensor", axis=0, tiled=True)
    gate = jnp.dot(normed, w_gate, preferred_element_type=jnp.float32)
    up = jnp.dot(normed, w_up, preferred_element_type=jnp.float32)
    sigmoid_gate = jax.nn.sigmoid(gate)
    activated = gate * sigmoid_gate * up
    hidden_grad = lax.dot_general(
        cot_full, w_down, (((1,), (1,)), ((), ())), preferred_element_type=jnp.float32
    )
    scale = 1.0 / math.sqrt(tok_rows * lax.axis_size("dp"))
    unit_grad = jnp.sum(activated * hidden_grad, axis=0) * scale * valid
    masked_grad = hidden_grad * unit_gain
    gate_grad = (masked_grad * up * sigmoid_gate * (1.0 + gate * (1.0 - sigmoid_gate))).astype(
        jnp.bfloat16
    )
    up_grad = (masked_grad * gate * sigmoid_gate).astype(jnp.bfloat16)
    share = tok_rows // tensors
    term = lax.dot_general(
        gate_grad, w_gate, (((1,), (1,)), ((), ())), preferred_element_type=jnp.float32
    )
    dnormed = lax.psum_scatter(
        (
            term
            + lax.dot_general(
                up_grad, w_up, (((1,), (1,)), ((), ())), preferred_element_type=jnp.float32
            )
        ).astype(jnp.bfloat16),
        "tensor",
        scatter_dimension=0,
        tiled=True,
    ).astype(jnp.float32)
    norm_rows = lax.dynamic_slice_in_dim(normalized, mine * share, share, 0)
    inv_rows = lax.dynamic_slice_in_dim(inv_rms, mine * share, share, 0)
    scaled_grad = dnormed * gain_float
    input_grad = inv_rows * (
        scaled_grad - norm_rows * jnp.mean(scaled_grad * norm_rows, axis=-1, keepdims=True)
    )
    gain_grad = lax.psum_scatter(
        unit_grad.reshape(keep, BLOCK), "dp", scatter_dimension=1, tiled=True
    )
    return (input_grad.astype(jnp.bfloat16), gain_grad)


def solution(mesh):
    placed = (
        P("dp", None),
        P(),
        P("dp", "tensor"),
        P("dp", "tensor"),
        P("tensor", "dp"),
        P("tensor"),
        P(),
        P(),
        P(("dp", "tensor"), None),
    )
    return jax.shard_map(
        per_device,
        mesh=mesh,
        in_specs=placed,
        out_specs=(P(("dp", "tensor"), None), P("tensor", "dp")),
        check_vma=False,
    )
```

profile of v0, /device:TPU:6, one launch (start us, length us, event | category | flops | bytes accessed | tf_op | source)
XLA Modules:
  0.0 496.2 jit_solution(16025933105333028028)
XLA Ops:
  7.3 1.0 dynamic-slice_reduce_fusion
  8.3 1.3 copy.21
  9.9 1.3 copy.24
  11.2 1.0 copy.25
  12.1 0.6 gather_fusion.2
  12.7 1.6 gather_fusion.3
  14.3 0.6 gather_fusion
  14.9 0.7 broadcast_select_fusion
  15.7 0.7 all-gather.9.cloned.1.call-update
  16.4 0.7 all-gather.7.cloned.1.call-update
  17.8 0.6 gather_fusion.1
  18.4 0.6 dynamic_slice.13
  18.9 0.6 compare_convert_fusion
  20.2 87.2 %all-gather.11.cloned.1.call-done = bf16[8192,2,128]{2,0,1:T(8,128)(2,1)} async-done(((bf16[128,2,128]{2,0,1:T(8,128)(2,1)}), bf16[8192,2,128]{2,0,1:T(8,128)(2,1)}) %all-gather.11.cloned.1.call-update) | async-done | bytes 4194320 | tf_op jit(solution)/shard_map/all_gather | solution.py:35
  107.4 6.3 %copy.26 = bf16[8192,2,128]{0,2,1:T(8,128)(2,1)} copy(bf16[8192,2,128]{2,0,1:T(8,128)(2,1)} %all-gather.11.cloned.1.call-done) | data formatting | bytes 8388608 | tf_op jit(solution)/shard_map/all_gather | solution.py:35
  113.7 80.4 %all-gather.9.cloned.1.call-done = bf16[8192,2,128]{2,0,1:T(8,128)(2,1)} async-done(((bf16[128,2,128]{2,0,1:T(8,128)(2,1)}), bf16[8192,2,128]{2,0,1:T(8,128)(2,1)}) %all-gather.9.cloned.1.call-update) | async-done | bytes 4194320 | tf_op jit(solution)/shard_map/all_gather | solution.py:36
  194.1 6.4 %copy.23 = bf16[8192,2,128]{0,2,1:T(8,128)(2,1)} copy(bf16[8192,2,128]{2,0,1:T(8,128)(2,1)} %all-gather.9.cloned.1.call-done) | data formatting | bytes 8388608 | tf_op jit(solution)/shard_map/all_gather | solution.py:36
  200.5 3.9 fusion.2
  204.4 1.5 fusion.3
  206.0 31.3 %all-gather.7.cloned.1.call-done = bf16[128,8192]{1,0:T(8,128)(2,1)} async-done(((bf16[16,8192]{1,0:T(8,128)(2,1)}), bf16[128,8192]{1,0:T(8,128)(2,1)}) %all-gather.7.cloned.1.call-update) | async-done | bytes 2097168 | tf_op jit(solution)/shard_map/all_gather | solution.py:44
  237.2 93.2 %all-gather.5.cloned.1.call-done = bf16[2,128,8192]{2,1,0:T(8,128)(2,1)} async-done(((bf16[2,128,128]{2,1,0:T(8,128)(2,1)}), bf16[2,128,8192]{2,1,0:T(8,128)(2,1)}) %all-gather.5.cloned.1.call-update) | async-done | bytes 4194320 | tf_op jit(solution)/shard_map/all_gather | solution.py:37
  330.5 4.5 multiply_reduce_fusion.1
  335.0 0.8 fusion.4
  335.8 1.4 copy-done.3
  337.2 2.1 fusion
  339.4 1.3 dynamic-slice.4
  341.3 0.7 compare_select_fusion.2
  342.0 2.4 convert_multiply_fusion
  344.5 141.3 %all-reduce = f32[2,128]{1,0:T(2,128)S(1)} all-reduce(f32[2,128]{1,0:T(2,128)S(1)} %bitcast_multiply_fusion), channel_id=3, replica_groups=mesh['dp'=64,'tensor'=8] {'dp'}, use_global_device_ids=true, to_apply=%region_4.6.clone | all-reduce | flops 256 | bytes 2048
  485.8 0.6 constant_dynamic-slice_fusion
  486.4 1.3 multiply_reduce_fusion
  487.7 2.0 multiply_convert_fusion.3
  (37 shorter events, 1.8 us)
Async XLA Ops:
  7.2 7.1 %copy-start = (bf16[1792,128]{1,0:T(8,128)(2,1)S(1)}, bf16[1792,128]{1,0:T(8,128)(2,1)}, u32[]{:S(2)}) copy-start(bf16[1792,128]{1,0:T(8,128)(2,1)} %param.15) | copy-start | bytes 1376260
  7.2 10.6 %copy-start.5 = (bf16[8192]{0:T(1024)(128)(2,1)S(1)}, bf16[8192]{0:T(1024)(128)(2,1)}, u32[]{:S(2)}) copy-start(bf16[8192]{0:T(1024)(128)(2,1)} %param.12) | copy-start | bytes 49156
  7.2 10.6 %copy-start.6 = (bf16[1792]{0:T(1024)(128)(2,1)S(1)}, bf16[1792]{0:T(1024)(128)(2,1)}, u32[]{:S(2)}) copy-start(bf16[1792]{0:T(1024)(128)(2,1)} %param.16) | copy-start | bytes 10756
  7.2 11.2 %copy-start.7 = (s32[8]{0:T(128)S(1)}, s32[8]{0:T(128)}, u32[]{:S(2)}) copy-start(s32[8]{0:T(128)} %param.18) | copy-start | bytes 100
  7.2 12.4 %copy-start.4 = (bf16[128,8192]{1,0:T(8,128)(2,1)S(1)}, bf16[128,8192]{1,0:T(8,128)(2,1)}, u32[]{:S(2)}) copy-start(bf16[128,8192]{1,0:T(8,128)(2,1)} %param.11) | copy-start | bytes 6291460
  7.2 100.1 %all-gather.11.cloned.1.call-start = ((), (), s32[]{:S(2)}) async-start(), calls=%async_computation.4 | async-start | bytes 4259840 | tf_op jit(solution)/shard_map/all_gather | solution.py:35
  15.6 178.5 %all-gather.9.cloned.1.call-start = ((), (), s32[]{:S(2)}) async-start(), calls=%async_computation.3 | async-start | bytes 4259840 | tf_op jit(solution)/shard_map/all_gather | solution.py:36
  16.4 220.8 %all-gather.7.cloned.1.call-start = ((), (), s32[]{:S(2)}) async-start(), calls=%async_computation.2 | async-start | bytes 2359296 | tf_op jit(solution)/shard_map/all_gather | solution.py:44
  17.1 313.3 %all-gather.5.cloned.1.call-start = ((), (), s32[]{:S(2)}) async-start(), calls=%async_computation.1 | async-start | bytes 4259840 | tf_op jit(solution)/shard_map/all_gather | solution.py:37
  17.7 468.7 %reduce-scatter.3.cloned.1.call-start = ((), (), s32[]{:S(2)}) async-start(), calls=%async_computation.5 | async-start | bytes 2359296 | tf_op jit(solution)/shard_map/reduce_scatter | solution.py:63
  200.5 3.9 copy-start.2
  330.5 4.6 copy-start.1
  335.0 2.2 copy-start.3
Sparse Core Ops, SparseCore 0:
  15.8 91.5 all-gather.10
  110.8 83.3 all-gather.8
  196.2 40.9 all-gather.6
  240.9 89.5 all-gather.4
  339.4 40.2 reduce-scatter.2
where the time goes:
time: 497 us; the launch traced here: 496 us
  waiting for transfers between devices  294 us (59%)
  blocking collectives  141 us (28%)
  local copies, waits for them, and re-layouts  24.8 us (5%)
  between operations  14.6 us (3%)
  matrix products  12.8 us (3%)
  other arithmetic  8.41 us (2%)
    unnamed x1, blocking collectives  141 us
    all_gather x1, waiting for transfers between devices, per_device(): lax.all_gather(slot_down, 'dp', axis=2, tiled=True)  93.2 us
    all_gather x1, waiting for transfers between devices, per_device(): lax.all_gather(slot_gate, 'dp', axis=0, tiled=True)  87.2 us
    all_gather x1, waiting for transfers between devices, per_device(): lax.all_gather(slot_up, 'dp', axis=0, tiled=True)  80.4 us
    all_gather x1, waiting for transfers between devices, per_device(): cot_full = lax.all_gather(cotangent, 'tensor', axis=0, tiled=True)  31.3 us
  transfers between devices with their start and end apart: 5, of which 4 were waited for; matrix products, arithmetic and copies ran while one was open for 5% of the time, Pallas kernels for 0%

commit v1 on v0

v1 whole, which is shorter than its diff:
```python
import functools
import math

import jax
import jax.numpy as jnp
from jax import lax
from jax.experimental import pallas as pl
from jax.experimental.pallas import tpu as pltpu
from jax.sharding import Mesh
from jax.sharding import PartitionSpec as P

BLOCK = 128
Z, YH, CORE, YL, X = 8, 4, 2, 2, 4
DP = ("z", "yh", "core")
TENSOR = ("yl", "x")
SHARDS = YL * X
BF, F32 = jnp.bfloat16, jnp.float32
EXTRA = 16
NT = (((1,), (1,)), ((), ()))


def first_slot(counts_ref, shard):
    total = jnp.int32(0)
    for other in range(SHARDS):
        total += jnp.where(other < shard, counts_ref[other], 0)
    return total


def pack_kernel(place, kept, counts, g0, g1, u0, u1, d0, d1, m0, m1, out):
    first = first_slot(counts, place[0])
    slots = []
    for gate, up, down, gain in ((g0, u0, d0, m0), (g1, u1, d1, m1)):
        body = jnp.concatenate([gate[...], up[...], down[...].T], axis=1)
        row = jnp.broadcast_to(gain[0], (EXTRA, BLOCK))
        slots.append((body, jnp.concatenate([row] * 3, axis=1)))
    for dest in range(SHARDS):
        second = dest == first + 1
        out[dest, :BLOCK, :] = jnp.where(second, slots[1][0], slots[0][0])
        out[dest, BLOCK:, :] = jnp.where(second, slots[1][1], slots[0][1])


def pack(place, kept, counts, gate_w, up_w, down_w, mask_gain):
    rows, units = gate_w.shape
    blocks = units // BLOCK

    def pick(k, kept, place):
        return jnp.clip(kept[place[0], k], 0, blocks - 1)

    cols = [
        pl.BlockSpec((rows, BLOCK), lambda i, p, b, n, k=k: (0, pick(k, b, p)))
        for k in (0, 1)
    ]
    down = [
        pl.BlockSpec((BLOCK, rows), lambda i, p, b, n, k=k: (pick(k, b, p), 0))
        for k in (0, 1)
    ]
    gain = [
        pl.BlockSpec((1, 1, BLOCK), lambda i, p, b, n, k=k: (pick(k, b, p), 0, 0))
        for k in (0, 1)
    ]
    gains = mask_gain.reshape(blocks, 1, BLOCK)
    shape = (SHARDS, BLOCK + EXTRA, 3 * BLOCK)
    return pl.pallas_call(
        pack_kernel,
        out_shape=jax.ShapeDtypeStruct(shape, BF),
        grid_spec=pltpu.PrefetchScalarGridSpec(
            num_scalar_prefetch=3,
            grid=(1,),
            in_specs=cols + cols + down + gain,
            out_specs=pl.BlockSpec(shape, lambda i, *_: (0, 0, 0)),
        ),
        name="pack_slots",
    )(place, kept, counts, gate_w, gate_w, up_w, up_w, down_w, down_w, gains, gains)


def ffn_kernel(scale, place, normed, cot, gain, *refs):
    nchunk = (len(refs) - 1) // 2
    mine, theirs, out = refs[:nchunk], refs[nchunk : 2 * nchunk], refs[-1]
    z, core = place[1], place[2]
    pieces = [(z, 0)]
    for step in (1, 2, 3):
        pieces += [(lax.rem(z - step + Z, Z), 0), (lax.rem(z + step, Z), 0)]
    far = lax.rem(z + Z // 2, Z)
    pieces += [(far, 0), (far, YH // 2)]
    work = []
    for (zz, yh0), a, b in zip(pieces, mine, theirs):
        for k in range(a.shape[0] // BLOCK):
            at = (zz * YH + yh0 + k) * (CORE * BLOCK)
            near = pl.multiple_of(at + core * BLOCK, BLOCK)
            other = pl.multiple_of(at + (1 - core) * BLOCK, BLOCK)
            work.append((near, other, a, b, k * BLOCK))
    tokens = normed.shape[0]
    gate_up = jnp.zeros((tokens, 2 * BLOCK), F32)
    hidden = jnp.zeros((tokens, BLOCK), F32)
    for near, other, a, b, row in work:
        n2 = jnp.concatenate([normed[:, pl.ds(near, BLOCK)], normed[:, pl.ds(other, BLOCK)]], axis=1)
        c2 = jnp.concatenate([cot[:, pl.ds(near, BLOCK)], cot[:, pl.ds(other, BLOCK)]], axis=1)
        w2 = jnp.concatenate([a[row : row + BLOCK, :], b[row : row + BLOCK, :]], axis=0)
        gate_up += jnp.dot(n2, w2[:, : 2 * BLOCK], preferred_element_type=F32)
        hidden += jnp.dot(c2, w2[:, 2 * BLOCK :], preferred_element_type=F32)
    gate, up = gate_up[:, :BLOCK], gate_up[:, BLOCK:]
    sig = jax.nn.sigmoid(gate)
    unit = jnp.sum(gate * sig * up * hidden, axis=0, keepdims=True) * scale
    masked = hidden * gain[0:1, :].astype(F32)
    gate_grad = (masked * up * sig * (1.0 + gate * (1.0 - sig))).astype(BF)
    up_grad = (masked * gate * sig).astype(BF)
    grads = jnp.concatenate([gate_grad, up_grad], axis=1)
    share = tokens // SHARDS
    for near, other, a, b, row in work:
        for at, w in ((near, a), (other, b)):
            part = lax.dot_general(grads, w[row : row + BLOCK, : 2 * BLOCK], NT, preferred_element_type=F32)
            first = pl.multiple_of(at // BLOCK * share, share)
            out[:, pl.ds(first, share), :] = part.astype(BF).reshape(SHARDS, share, BLOCK)
    hi = unit.astype(BF)
    rest = unit - hi.astype(F32)
    mid = rest.astype(BF)
    lo = (rest - mid.astype(F32)).astype(BF)
    row = lax.broadcasted_iota(jnp.int32, (EXTRA, BLOCK), 0)
    split = jnp.where(
        row == 0, hi.astype(F32), jnp.where(row == 1, mid.astype(F32), jnp.where(row == 2, lo.astype(F32), 0.0))
    ).astype(BF)
    for dest in range(SHARDS):
        out[dest, -EXTRA:, :] = split


def ffn(place, normed, cot, gain, mine, theirs):
    tokens, width = normed.shape
    rows = width // BLOCK * (tokens // SHARDS) + EXTRA
    vmem = pl.BlockSpec(memory_space=pltpu.VMEM)
    scale = 1.0 / math.sqrt(tokens * Z * YH * CORE)
    return pl.pallas_call(
        functools.partial(ffn_kernel, scale),
        out_shape=jax.ShapeDtypeStruct((SHARDS, rows, BLOCK), BF),
        in_specs=[pl.BlockSpec(memory_space=pltpu.SMEM)] + [vmem] * (3 + len(mine) + len(theirs)),
        out_specs=vmem,
        compiler_params=pltpu.CompilerParams(vmem_limit_bytes=48 << 20),
        name="pruned_ffn",
    )(place, normed, cot, gain, *mine, *theirs)


def final_kernel(place, counts, act, gain, parts, grad, unit):
    share, width = act.shape
    x = act[...].astype(F32)
    inv = lax.rsqrt(jnp.mean(x * x, axis=-1, keepdims=True) + 1e-05)
    dnormed = []
    for j in range(width // BLOCK):
        total = parts[0, j * share : (j + 1) * share, :].astype(F32)
        for src in range(1, SHARDS):
            total += parts[src, j * share : (j + 1) * share, :].astype(F32)
        dnormed.append(total)
    scaled = jnp.concatenate(dnormed, axis=1) * gain[...].astype(F32)
    normalized = x * inv
    mean = jnp.mean(scaled * normalized, axis=-1, keepdims=True)
    grad[...] = (inv * (scaled - normalized * mean)).astype(BF)
    me = place[0]
    first, count = first_slot(counts, me), counts[me]
    for k in range(2):
        tail = parts[jnp.minimum(first + k, SHARDS - 1), -EXTRA:, :].astype(F32)
        value = jnp.sum(tail, axis=0, keepdims=True)
        unit[k : k + 1, :] = jnp.where(k < count, value, 0.0)


def final(place, counts, act, gain, parts):
    tokens, width = act.shape
    share = tokens // SHARDS
    return pl.pallas_call(
        final_kernel,
        out_shape=(
            jax.ShapeDtypeStruct((share, width), BF),
            jax.ShapeDtypeStruct((2, BLOCK), F32),
        ),
        grid_spec=pltpu.PrefetchScalarGridSpec(
            num_scalar_prefetch=2,
            grid=(1,),
            in_specs=[
                pl.BlockSpec((share, width), lambda i, p, n: (p[0], 0)),
                pl.BlockSpec((1, width), lambda i, p, n: (0, 0)),
                pl.BlockSpec(parts.shape, lambda i, p, n: (0, 0, 0)),
            ],
            out_specs=(
                pl.BlockSpec((share, width), lambda i, p, n: (0, 0)),
                pl.BlockSpec((2, BLOCK), lambda i, p, n: (0, 0)),
            ),
        ),
        compiler_params=pltpu.CompilerParams(vmem_limit_bytes=32 << 20),
        name="input_grad",
    )(place, counts, act, gain.reshape(1, -1), parts)


def ring(x):
    up = [(i, (i + 1) % Z) for i in range(Z)]
    down = [(i, (i - 1) % Z) for i in range(Z)]
    chunks, a, b = [x], x, x
    for _ in range(3):
        a, b = lax.ppermute(a, "z", up), lax.ppermute(b, "z", down)
        chunks += [a, b]
    half = x.shape[0] // 2
    chunks += [lax.ppermute(a[:half], "z", up), lax.ppermute(b[half:], "z", down)]
    return chunks


def per_device(
    activations, norm_gain, gate_w, up_w, down_w, mask_gain, kept_blocks, kept_counts, cotangent
):
    me = lax.axis_index(TENSOR)
    place = jnp.stack([me, lax.axis_index("z"), lax.axis_index("core")]).astype(jnp.int32)
    cot = lax.all_gather(cotangent, TENSOR, axis=0, tiled=True)

    sent = pack(place, kept_blocks, kept_counts, gate_w, up_w, down_w, mask_gain)
    got = lax.all_to_all(sent, TENSOR, split_axis=0, concat_axis=0, tiled=True)
    ends = jnp.cumsum(kept_counts)
    source = jnp.sum((ends <= me).astype(jnp.int32))
    slot = lax.dynamic_index_in_dim(got, source, 0, keepdims=False)
    unit_gain = slot[BLOCK:, :BLOCK]
    column = lax.all_gather(slot[:BLOCK], "yh", axis=0, tiled=True)
    mine = ring(column)
    swap = [(0, 1), (1, 0)]
    theirs = [lax.ppermute(chunk, "core", swap) for chunk in mine]

    act = activations.astype(F32)
    inv_rms = lax.rsqrt(jnp.mean(act * act, axis=-1, keepdims=True) + 1e-05)
    normed = (act * inv_rms * norm_gain.astype(F32)).astype(BF)

    parts = ffn(place, normed, cot, unit_gain, mine, theirs)
    got = lax.all_to_all(parts, TENSOR, split_axis=0, concat_axis=0, tiled=True)
    input_grad, unit = final(place, kept_counts, activations, norm_gain, got)
    copies = jnp.broadcast_to(unit[None], (Z * YH * CORE, 2, BLOCK))
    units = jnp.sum(lax.all_to_all(copies, DP, split_axis=0, concat_axis=0, tiled=True), axis=0)
    width = BLOCK // (Z * YH * CORE)
    gain_grad = lax.dynamic_slice_in_dim(units, lax.axis_index(DP) * width, width, 1)
    return input_grad, gain_grad


def solution(mesh):
    fine = Mesh(mesh.devices.reshape(Z, YH, CORE, YL, X), DP + TENSOR)
    placed = (
        P(DP, None),
        P(),
        P(DP, TENSOR),
        P(DP, TENSOR),
        P(TENSOR, DP),
        P(TENSOR),
        P(),
        P(),
        P(DP + TENSOR, None),
    )
    return jax.shard_map(
        per_device,
        mesh=fine,
        in_specs=placed,
        out_specs=(P(DP + TENSOR, None), P(TENSOR, DP)),
        check_vma=False,
    )
```

time: 497 us -> 208 us (0.42)
  waiting for transfers between devices: 294 us -> 51.5 us
  blocking collectives: 141 us -> 17.4 us
  starting transfers between devices: 0.19 us -> 77.5 us
  matrix products: 12.8 us -> 0 us
  Pallas kernels: 0 us -> 12.6 us
    all_gather x4 -> x1, waiting for transfers between devices: 292 us -> 0.01 us  [per_device(): cot = lax.all_gather(cotangent, TENSOR, axis=0, tiled=True)]
    unnamed x1 -> x0, blocking collectives: 141 us -> none
    ppermute x0 -> x17, starting transfers between devices: none -> 54 us  [the longest x6 27.8 us: ring(): a, b = (lax.ppermute(a, 'z', up), lax.ppermute(b, 'z', down))]
    all_to_all x0 -> x3, waiting for transfers between devices: none -> 42.8 us  [the longest x1 25.8 us: per_device(): got = lax.all_to_all(parts, TENSOR, split_axis=0, concat_axis=0, tiled=True)]
    all_to_all x0 -> x3, starting transfers between devices: none -> 23.5 us  [the longest x1 9.45 us: per_device(): got = lax.all_to_all(sent, TENSOR, split_axis=0, concat_axis=0, tiled=True)]
    all_gather x0 -> x1, blocking collectives: none -> 17.4 us  [per_device(): column = lax.all_gather(slot[:BLOCK], 'yh', axis=0, tiled=True)]
    unnamed x20 -> x65, local copies, waits for them, and re-layouts: 5.89 us -> 21.8 us
    dot_general x5 -> x0, matrix products: 12.8 us -> none  [the longest x1 4.55 us: per_device(): lax.dot_general(cot_full, w_down, (((1,), (1,)), ((), ())), preferred_ele...]
  transfers between devices with their start and end apart: 5 -> 21, of which waited for: 4 -> 5; matrix products, arithmetic and copies ran while one was open for 5% -> 2% of each run, Pallas kernels for 0% -> 0%
where the time goes in v1:
time: 208 us; the launch traced here: 205 us
  starting transfers between devices  77.5 us (37%)
  waiting for transfers between devices  51.5 us (25%)
  local copies, waits for them, and re-layouts  25.3 us (12%)
  blocking collectives  17.4 us (8%)
  between operations  16.4 us (8%)
  Pallas kernels  12.6 us (6%)
  other arithmetic  3.96 us (2%)
    ppermute x6, starting transfers between devices, ring(): a, b = (lax.ppermute(a, 'z', up), lax.ppermute(b, 'z', down))  27.8 us
    all_to_all x1, waiting for transfers between devices, per_device(): got = lax.all_to_all(parts, TENSOR, split_axis=0, concat_axis=0, tiled=True)  25.8 us
    unnamed x65, local copies, waits for them, and re-layouts  21.8 us
    ppermute x9, starting transfers between devices, per_device(): theirs = [lax.ppermute(chunk, 'core', swap) for chunk in mine]  19.2 us
    all_gather x1, blocking collectives, per_device(): column = lax.all_gather(slot[:BLOCK], 'yh', axis=0, tiled=True)  17.4 us
    all_to_all x1, waiting for transfers between devices, per_device(): lax.all_to_all(copies, DP, split_axis=0, concat_axis=0, tiled=True)  12.3 us
    all_to_all x1, starting transfers between devices, per_device(): got = lax.all_to_all(sent, TENSOR, split_axis=0, concat_axis=0, tiled=True)  9.45 us
    ppermute x6, waiting for transfers between devices, ring(): a, b = (lax.ppermute(a, 'z', up), lax.ppermute(b, 'z', down))  7.98 us
  transfers between devices with their start and end apart: 21, of which 5 were waited for; matrix products, arithmetic and copies ran while one was open for 2% of the time, Pallas kernels for 0%

profile of v1, /device:TPU:6, one launch (start us, length us, event | category | flops | bytes accessed | tf_op | source)
XLA Modules:
  0.0 204.8 jit_solution(5923018984248690203)
XLA Ops:
  7.2 1.3 copy.19.m0.m1
  8.5 1.3 copy.18.kept
  10.5 2.7 %pack_slots.1 = bf16[8,144,384]{2,1,0:T(8,128)(2,1)} custom-call(s32[3]{0:T(128)} %pad_add_fusion.place, s32[8,2]{1,0:T(8,128)} %copy.18.kept, s32[8]{0:T(128)} %counts.3, bf16[128,1792]{1,0:T(8,128)(2,1)} %g1.1, bf16[128,1792]{1,0:T(8,128)(2,1)} %g1.1, bf16[128,1792]{1,0:T(8,128)(2,1)} %u1_.1, bf16[128,1792]{1,0:T(8,128)(2,1)} %u1_.1, ...), custom_call_target="tpu_custom_call" | custom-call | tf_op jit(solution)/shard_map/pack_slots/pallas_call | solution.py:63
  13.2 9.4 %all-to-all-start = ((bf16[8,144,384]{2,1,0:T(8,128)(2,1)}), bf16[8,144,384]{2,1,0:T(8,128)(2,1)S(1)}, u32[]{:S(2)}, u32[]{:S(2)}) async-start(bf16[8,144,384]{2,1,0:T(8,128)(2,1)} %pack_slots.1), calls=%async_computation | async-start | bytes 1769472 | tf_op jit(solution)/shard_map/all_to_all | solution.py:210
  26.1 4.7 %all-to-all-done = bf16[8,144,384]{2,1,0:T(8,128)(2,1)S(1)} async-done(((bf16[8,144,384]{2,1,0:T(8,128)(2,1)}), bf16[8,144,384]{2,1,0:T(8,128)(2,1)S(1)}, u32[]{:S(2)}, u32[]{:S(2)}) %all-to-all-start) | async-done | bytes 884768 | tf_op jit(solution)/shard_map/all_to_all | solution.py:210
  31.9 17.4 %all-gather = bf16[1,512,384]{2,1,0:T(8,128)(2,1)S(1)} all-gather(bf16[1,128,384]{2,1,0:T(8,128)(2,1)S(1)} %constant_dynamic-slice_fusion), channel_id=2, replica_groups=mesh['z'=8,'yh'=4,'core'=2,'yl'=2,'x'=4] {'yh'}, dimensions={1}, use_global_device_ids=true | all-gather | bytes 491520 | tf_op jit(solution)/shard_map/all_gather | solution.py:215
  49.3 4.4 %collective-permute-start = (bf16[512,384]{1,0:T(8,128)(2,1)S(1)}, bf16[512,384]{1,0:T(8,128)(2,1)S(1)}, u32[]{:S(2)}, u32[]{:S(2)}) collective-permute-start(bf16[512,384]{1,0:T(8,128)(2,1)S(1)} %bitcast.8), channel_id=1, source_target_pairs={{0,64},{64,128},{128,192},{192,256},{256,320},{320,384},{384,448},... | collective-permute-start | bytes 1179656 | tf_op jit(solution)/shard_map/ppermute | solution.py:195
  53.7 9.3 %collective-permute-start.1 = (bf16[512,384]{1,0:T(8,128)(2,1)S(1)}, bf16[512,384]{1,0:T(8,128)(2,1)S(1)}, u32[]{:S(2)}, u32[]{:S(2)}) collective-permute-start(bf16[512,384]{1,0:T(8,128)(2,1)S(1)} %bitcast.9), channel_id=1, source_target_pairs={{0,448},{64,0},{128,64},{192,128},{256,192},{320,256},{384,320},{4... | collective-permute-start | bytes 1179656 | tf_op jit(solution)/shard_map/ppermute | solution.py:195
  63.0 4.2 %collective-permute-done.refs_1_ = bf16[512,384]{1,0:T(8,128)(2,1)S(1)} collective-permute-done((bf16[512,384]{1,0:T(8,128)(2,1)S(1)}, bf16[512,384]{1,0:T(8,128)(2,1)S(1)}, u32[]{:S(2)}, u32[]{:S(2)}) %collective-permute-start) | collective-permute-done | bytes 393248 | tf_op jit(solution)/shard_map/ppermute | solution.py:195
  67.2 1.9 collective-permute-start.2
  69.1 5.1 %collective-permute-start.3 = (bf16[512,384]{1,0:T(8,128)(2,1)S(1)}, bf16[512,384]{1,0:T(8,128)(2,1)S(1)}, u32[]{:S(2)}, u32[]{:S(2)}) collective-permute-start(bf16[512,384]{1,0:T(8,128)(2,1)S(1)} %collective-permute-done.1.refs_2_), channel_id=1, source_target_pairs={{0,448},{64,0},{128,64},{192,128},{256,192},{320,256},{384,320},{4... | collective-permute-start | bytes 1179656 | tf_op jit(solution)/shard_map/ppermute | solution.py:195
  74.3 3.8 %collective-permute-done.2.refs_3_ = bf16[512,384]{1,0:T(8,128)(2,1)S(1)} collective-permute-done((bf16[512,384]{1,0:T(8,128)(2,1)S(1)}, bf16[512,384]{1,0:T(8,128)(2,1)S(1)}, u32[]{:S(2)}, u32[]{:S(2)}) %collective-permute-start.2) | collective-permute-done | bytes 393248 | tf_op jit(solution)/shard_map/ppermute | solution.py:195
  78.1 1.9 collective-permute-start.4
  80.0 5.1 %collective-permute-start.5 = (bf16[512,384]{1,0:T(8,128)(2,1)S(1)}, bf16[512,384]{1,0:T(8,128)(2,1)S(1)}, u32[]{:S(2)}, u32[]{:S(2)}) collective-permute-start(bf16[512,384]{1,0:T(8,128)(2,1)S(1)} %collective-permute-done.3.refs_4_), channel_id=1, source_target_pairs={{0,448},{64,0},{128,64},{192,128},{256,192},{320,256},{384,320},{4... | collective-permute-start | bytes 1179656 | tf_op jit(solution)/shard_map/ppermute | solution.py:195
  85.2 1.9 collective-permute-start.8
  87.1 2.4 %collective-permute-start.10 = (bf16[512,384]{1,0:T(8,128)(2,1)S(1)}, bf16[512,384]{1,0:T(8,128)(2,1)S(1)}, u32[]{:S(2)}, u32[]{:S(2)}) collective-permute-start(bf16[512,384]{1,0:T(8,128)(2,1)S(1)} %collective-permute-done.1.refs_2_), channel_id=1, source_target_pairs={{0,8},{8,0},{1,9},{9,1},{2,10},{10,2},{3,11},{11,3},{4,12},{12,4},... | collective-permute-start | bytes 1179656 | tf_op jit(solution)/shard_map/ppermute | solution.py:218
  89.5 1.9 collective-permute-start.9
  91.5 2.4 %collective-permute-start.11 = (bf16[512,384]{1,0:T(8,128)(2,1)S(1)}, bf16[512,384]{1,0:T(8,128)(2,1)S(1)}, u32[]{:S(2)}, u32[]{:S(2)}) collective-permute-start(bf16[512,384]{1,0:T(8,128)(2,1)S(1)} %collective-permute-done.2.refs_3_), channel_id=1, source_target_pairs={{0,8},{8,0},{1,9},{9,1},{2,10},{10,2},{3,11},{11,3},{4,12},{12,4},... | collective-permute-start | bytes 1179656 | tf_op jit(solution)/shard_map/ppermute | solution.py:218
  94.4 1.9 collective-permute-start.6
  97.1 5.1 %collective-permute-start.7 = (bf16[256,384]{1,0:T(8,128)(2,1)S(1)}, bf16[256,384]{1,0:T(8,128)(2,1)S(1)}, u32[]{:S(2)}, u32[]{:S(2)}) collective-permute-start(bf16[256,384]{1,0:T(8,128)(2,1)S(1)} %slice.22), channel_id=1, source_target_pairs={{0,448},{64,0},{128,64},{192,128},{256,192},{320,256},{384,320},{4... | collective-permute-start | bytes 589832 | tf_op jit(solution)/shard_map/ppermute | solution.py:198
  103.0 1.9 collective-permute-start.12
  105.7 2.4 %collective-permute-start.13 = (bf16[512,384]{1,0:T(8,128)(2,1)S(1)}, bf16[512,384]{1,0:T(8,128)(2,1)S(1)}, u32[]{:S(2)}, u32[]{:S(2)}) collective-permute-start(bf16[512,384]{1,0:T(8,128)(2,1)S(1)} %collective-permute-done.4.refs_5_), channel_id=1, source_target_pairs={{0,8},{8,0},{1,9},{9,1},{2,10},{10,2},{3,11},{11,3},{4,12},{12,4},... | collective-permute-start | bytes 1179656 | tf_op jit(solution)/shard_map/ppermute | solution.py:218
  108.9 1.9 collective-permute-start.14
  110.9 2.4 %collective-permute-start.15 = (bf16[256,384]{1,0:T(8,128)(2,1)S(1)}, bf16[256,384]{1,0:T(8,128)(2,1)S(1)}, u32[]{:S(2)}, u32[]{:S(2)}) collective-permute-start(bf16[256,384]{1,0:T(8,128)(2,1)S(1)} %collective-permute-done.6.refs_7_), channel_id=1, source_target_pairs={{0,8},{8,0},{1,9},{9,1},{2,10},{10,2},{3,11},{11,3},{4,12},{12,4},... | collective-permute-start | bytes 589832 | tf_op jit(solution)/shard_map/ppermute | solution.py:218
  113.3 1.9 collective-permute-start.16
  115.2 1.9 fusion.2.normed
  134.5 6.5 %pruned_ffn.1 = bf16[8,1040,128]{2,1,0:T(8,128)(2,1)} custom-call(s32[3]{0:T(128)S(1)} %copy-done.27, bf16[128,8192]{1,0:T(8,128)(2,1)} %fusion.2.normed, bf16[128,8192]{1,0:T(8,128)(2,1)} %all-gather.3.cloned.1.call-done.cot, bf16[16,128]{1,0:T(8,128)(2,1)S(1)} %slice.20.gain, bf16[512,384]{1,0:T(8,128)(2,1)S(1)} %bitcast.11, ...), custom_call_target="tpu_custom_call" | custom-call | tf_op jit(solution)/shard_map/pruned_ffn/pallas_call | solution.py:131
  141.0 6.9 %all-to-all-start.1 = ((bf16[8,1040,128]{2,1,0:T(8,128)(2,1)}), bf16[8,1040,128]{2,1,0:T(8,128)(2,1)}, u32[]{:S(2)}, u32[]{:S(2)}) async-start(bf16[8,1040,128]{2,1,0:T(8,128)(2,1)} %pruned_ffn.1), calls=%async_computation.1 | async-start | bytes 4259840 | tf_op jit(solution)/shard_map/all_to_all | solution.py:225
  147.9 25.8 %all-to-all-done.1.parts = bf16[8,1040,128]{2,1,0:T(8,128)(2,1)} async-done(((bf16[8,1040,128]{2,1,0:T(8,128)(2,1)}), bf16[8,1040,128]{2,1,0:T(8,128)(2,1)}, u32[]{:S(2)}, u32[]{:S(2)}) %all-to-all-start.1) | async-done | bytes 2129952 | tf_op jit(solution)/shard_map/all_to_all | solution.py:225
  173.7 3.4 %input_grad.1 = (bf16[16,8192]{1,0:T(8,128)(2,1)}, f32[2,128]{1,0:T(2,128)S(1)}) custom-call(s32[3]{0:T(128)S(1)} %copy-done.27, s32[8]{0:T(128)S(1)} %copy-done.28, bf16[128,8192]{1,0:T(8,128)(2,1)S(1)} %copy-done, bf16[1,8192]{1,0:T(2,128)(2,1)S(1)} %reshape.48.gain, bf16[8,1040,128]{2,1,0:T(8,128)(2,1)} %all-to-all-done.1.parts), custom_call_target="tpu_custom_call" | custom-call | tf_op jit(solution)/shard_map/input_grad/pallas_call | solution.py:166
  177.8 7.2 %all-to-all-start.2 = ((f32[64,2,128]{2,1,0:T(2,128)}), f32[64,2,128]{2,1,0:T(2,128)S(1)}, u32[]{:S(2)}, u32[]{:S(2)}) async-start(f32[64,2,128]{2,1,0:T(2,128)} %broadcast_in_dim.2), calls=%async_computation.2 | async-start | bytes 131072 | tf_op jit(solution)/shard_map/all_to_all | solution.py:228
  185.0 12.3 %all-to-all-done.2 = f32[64,2,128]{2,1,0:T(2,128)S(1)} async-done(((f32[64,2,128]{2,1,0:T(2,128)}), f32[64,2,128]{2,1,0:T(2,128)S(1)}, u32[]{:S(2)}, u32[]{:S(2)}) %all-to-all-start.2) | async-done | bytes 65568 | tf_op jit(solution)/shard_map/all_to_all | solution.py:228
  (97 shorter events, 25.5 us)
Async XLA Ops:
  10.4 12.9 %copy-start.28 = (s32[8]{0:T(128)S(1)}, s32[8]{0:T(128)}, u32[]{:S(2)}) copy-start(s32[8]{0:T(128)} %counts.3) | copy-start | bytes 100
  13.2 73.9 %copy-start.31 = (bf16[8192]{0:T(1024)(128)(2,1)S(1)}, bf16[8192]{0:T(1024)(128)(2,1)}, u32[]{:S(2)}) copy-start(bf16[8192]{0:T(1024)(128)(2,1)} %param.10) | copy-start | bytes 49156
  13.2 80.7 %copy-start = (bf16[128,8192]{1,0:T(8,128)(2,1)S(1)}, bf16[128,8192]{1,0:T(8,128)(2,1)}, u32[]{:S(2)}) copy-start(bf16[128,8192]{1,0:T(8,128)(2,1)} %act.1) | copy-start | bytes 6291460
  13.2 17.7 %all-to-all-start = ((bf16[8,144,384]{2,1,0:T(8,128)(2,1)}), bf16[8,144,384]{2,1,0:T(8,128)(2,1)S(1)}, u32[]{:S(2)}, u32[]{:S(2)}) async-start(bf16[8,144,384]{2,1,0:T(8,128)(2,1)} %pack_slots.1), calls=%async_computation | async-start | bytes 1769472 | tf_op jit(solution)/shard_map/all_to_all | solution.py:210
  22.6 99.1 %all-gather.3.cloned.1.call-start = ((), (), s32[]{:S(2)}) async-start(), calls=%async_computation.3 | async-start | bytes 2359296 | tf_op jit(solution)/shard_map/all_gather | solution.py:207
  30.9 1.0 copy-start.29
  49.3 17.9 %collective-permute-start = (bf16[512,384]{1,0:T(8,128)(2,1)S(1)}, bf16[512,384]{1,0:T(8,128)(2,1)S(1)}, u32[]{:S(2)}, u32[]{:S(2)}) collective-permute-start(bf16[512,384]{1,0:T(8,128)(2,1)S(1)} %bitcast.8), channel_id=1, source_target_pairs={{0,64},{64,128},{128,192},{192,256},{256,320},{320,384},{384,448},... | collective-permute-start | bytes 1179656 | tf_op jit(solution)/shard_map/ppermute | solution.py:195
  53.7 15.4 %collective-permute-start.1 = (bf16[512,384]{1,0:T(8,128)(2,1)S(1)}, bf16[512,384]{1,0:T(8,128)(2,1)S(1)}, u32[]{:S(2)}, u32[]{:S(2)}) collective-permute-start(bf16[512,384]{1,0:T(8,128)(2,1)S(1)} %bitcast.9), channel_id=1, source_target_pairs={{0,448},{64,0},{128,64},{192,128},{256,192},{320,256},{384,320},{4... | collective-permute-start | bytes 1179656 | tf_op jit(solution)/shard_map/ppermute | solution.py:195
  67.2 40.9 %copy-start.1 = (bf16[512,384]{1,0:T(8,128)(2,1)}, bf16[512,384]{1,0:T(8,128)(2,1)S(1)}, u32[]{:S(2)}) copy-start(bf16[512,384]{1,0:T(8,128)(2,1)S(1)} %collective-permute-done.refs_1_) | copy-start | bytes 1179652
  67.2 10.9 %collective-permute-start.2 = (bf16[512,384]{1,0:T(8,128)(2,1)S(1)}, bf16[512,384]{1,0:T(8,128)(2,1)S(1)}, u32[]{:S(2)}, u32[]{:S(2)}) collective-permute-start(bf16[512,384]{1,0:T(8,128)(2,1)S(1)} %collective-permute-done.refs_1_), channel_id=1, source_target_pairs={{0,64},{64,128},{128,192},{192,256},{256,320},{320,384},{384,448},... | collective-permute-start | bytes 1179656 | tf_op jit(solution)/shard_map/ppermute | solution.py:195
  69.1 39.0 %copy-start.3 = (bf16[512,384]{1,0:T(8,128)(2,1)}, bf16[512,384]{1,0:T(8,128)(2,1)S(1)}, u32[]{:S(2)}) copy-start(bf16[512,384]{1,0:T(8,128)(2,1)S(1)} %collective-permute-done.1.refs_2_) | copy-start | bytes 1179652
  69.1 10.9 %collective-permute-start.3 = (bf16[512,384]{1,0:T(8,128)(2,1)S(1)}, bf16[512,384]{1,0:T(8,128)(2,1)S(1)}, u32[]{:S(2)}, u32[]{:S(2)}) collective-permute-start(bf16[512,384]{1,0:T(8,128)(2,1)S(1)} %collective-permute-done.1.refs_2_), channel_id=1, source_target_pairs={{0,448},{64,0},{128,64},{192,128},{256,192},{320,256},{384,320},{4... | collective-permute-start | bytes 1179656 | tf_op jit(solution)/shard_map/ppermute | solution.py:195
  78.1 32.8 %copy-start.5 = (bf16[512,384]{1,0:T(8,128)(2,1)}, bf16[512,384]{1,0:T(8,128)(2,1)S(1)}, u32[]{:S(2)}) copy-start(bf16[512,384]{1,0:T(8,128)(2,1)S(1)} %collective-permute-done.2.refs_3_) | copy-start | bytes 1179652
  78.1 13.4 %collective-permute-start.4 = (bf16[512,384]{1,0:T(8,128)(2,1)S(1)}, bf16[512,384]{1,0:T(8,128)(2,1)S(1)}, u32[]{:S(2)}, u32[]{:S(2)}) collective-permute-start(bf16[512,384]{1,0:T(8,128)(2,1)S(1)} %collective-permute-done.2.refs_3_), channel_id=1, source_target_pairs={{0,64},{64,128},{128,192},{192,256},{256,320},{320,384},{384,448},... | collective-permute-start | bytes 1179656 | tf_op jit(solution)/shard_map/ppermute | solution.py:195
  80.0 37.2 %copy-start.7 = (bf16[512,384]{1,0:T(8,128)(2,1)}, bf16[512,384]{1,0:T(8,128)(2,1)S(1)}, u32[]{:S(2)}) copy-start(bf16[512,384]{1,0:T(8,128)(2,1)S(1)} %collective-permute-done.3.refs_4_) | copy-start | bytes 1179652
  80.0 14.4 %collective-permute-start.5 = (bf16[512,384]{1,0:T(8,128)(2,1)S(1)}, bf16[512,384]{1,0:T(8,128)(2,1)S(1)}, u32[]{:S(2)}, u32[]{:S(2)}) collective-permute-start(bf16[512,384]{1,0:T(8,128)(2,1)S(1)} %collective-permute-done.3.refs_4_), channel_id=1, source_target_pairs={{0,448},{64,0},{128,64},{192,128},{256,192},{320,256},{384,320},{4... | collective-permute-start | bytes 1179656 | tf_op jit(solution)/shard_map/ppermute | solution.py:195
  85.2 11.2 %collective-permute-start.8 = (bf16[512,384]{1,0:T(8,128)(2,1)S(1)}, bf16[512,384]{1,0:T(8,128)(2,1)S(1)}, u32[]{:S(2)}, u32[]{:S(2)}) collective-permute-start(bf16[512,384]{1,0:T(8,128)(2,1)S(1)} %bitcast.10), channel_id=1, source_target_pairs={{0,8},{8,0},{1,9},{9,1},{2,10},{10,2},{3,11},{11,3},{4,12},{12,4},... | collective-permute-start | bytes 1179656 | tf_op jit(solution)/shard_map/ppermute | solution.py:218
  87.1 15.2 %collective-permute-start.10 = (bf16[512,384]{1,0:T(8,128)(2,1)S(1)}, bf16[512,384]{1,0:T(8,128)(2,1)S(1)}, u32[]{:S(2)}, u32[]{:S(2)}) collective-permute-start(bf16[512,384]{1,0:T(8,128)(2,1)S(1)} %collective-permute-done.1.refs_2_), channel_id=1, source_target_pairs={{0,8},{8,0},{1,9},{9,1},{2,10},{10,2},{3,11},{11,3},{4,12},{12,4},... | collective-permute-start | bytes 1179656 | tf_op jit(solution)/shard_map/ppermute | solution.py:218
  89.5 15.4 %collective-permute-start.9 = (bf16[512,384]{1,0:T(8,128)(2,1)S(1)}, bf16[512,384]{1,0:T(8,128)(2,1)S(1)}, u32[]{:S(2)}, u32[]{:S(2)}) collective-permute-start(bf16[512,384]{1,0:T(8,128)(2,1)S(1)} %collective-permute-done.refs_1_), channel_id=1, source_target_pairs={{0,8},{8,0},{1,9},{9,1},{2,10},{10,2},{3,11},{11,3},{4,12},{12,4},... | collective-permute-start | bytes 1179656 | tf_op jit(solution)/shard_map/ppermute | solution.py:218
  91.5 16.7 %collective-permute-start.11 = (bf16[512,384]{1,0:T(8,128)(2,1)S(1)}, bf16[512,384]{1,0:T(8,128)(2,1)S(1)}, u32[]{:S(2)}, u32[]{:S(2)}) collective-permute-start(bf16[512,384]{1,0:T(8,128)(2,1)S(1)} %collective-permute-done.2.refs_3_), channel_id=1, source_target_pairs={{0,8},{8,0},{1,9},{9,1},{2,10},{10,2},{3,11},{11,3},{4,12},{12,4},... | collective-permute-start | bytes 1179656 | tf_op jit(solution)/shard_map/ppermute | solution.py:218
  94.4 16.5 %collective-permute-start.6 = (bf16[256,384]{1,0:T(8,128)(2,1)S(1)}, bf16[256,384]{1,0:T(8,128)(2,1)S(1)}, u32[]{:S(2)}, u32[]{:S(2)}) collective-permute-start(bf16[256,384]{1,0:T(8,128)(2,1)S(1)} %slice.21), channel_id=1, source_target_pairs={{0,64},{64,128},{128,192},{192,256},{256,320},{320,384},{384,448},... | collective-permute-start | bytes 589832 | tf_op jit(solution)/shard_map/ppermute | solution.py:198
  97.1 16.2 %collective-permute-start.7 = (bf16[256,384]{1,0:T(8,128)(2,1)S(1)}, bf16[256,384]{1,0:T(8,128)(2,1)S(1)}, u32[]{:S(2)}, u32[]{:S(2)}) collective-permute-start(bf16[256,384]{1,0:T(8,128)(2,1)S(1)} %slice.22), channel_id=1, source_target_pairs={{0,448},{64,0},{128,64},{192,128},{256,192},{320,256},{384,320},{4... | collective-permute-start | bytes 589832 | tf_op jit(solution)/shard_map/ppermute | solution.py:198
  102.3 19.5 %copy-start.27 = (s32[3]{0:T(128)S(1)}, s32[3]{0:T(128)}, u32[]{:S(2)}) copy-start(s32[3]{0:T(128)} %pad_add_fusion.place) | copy-start | bytes 40
  103.0 15.1 %collective-permute-start.12 = (bf16[512,384]{1,0:T(8,128)(2,1)S(1)}, bf16[512,384]{1,0:T(8,128)(2,1)S(1)}, u32[]{:S(2)}, u32[]{:S(2)}) collective-permute-start(bf16[512,384]{1,0:T(8,128)(2,1)S(1)} %collective-permute-done.3.refs_4_), channel_id=1, source_target_pairs={{0,8},{8,0},{1,9},{9,1},{2,10},{10,2},{3,11},{11,3},{4,12},{12,4},... | collective-permute-start | bytes 1179656 | tf_op jit(solution)/shard_map/ppermute | solution.py:218
  105.7 13.2 %collective-permute-start.13 = (bf16[512,384]{1,0:T(8,128)(2,1)S(1)}, bf16[512,384]{1,0:T(8,128)(2,1)S(1)}, u32[]{:S(2)}, u32[]{:S(2)}) collective-permute-start(bf16[512,384]{1,0:T(8,128)(2,1)S(1)} %collective-permute-done.4.refs_5_), channel_id=1, source_target_pairs={{0,8},{8,0},{1,9},{9,1},{2,10},{10,2},{3,11},{11,3},{4,12},{12,4},... | collective-permute-start | bytes 1179656 | tf_op jit(solution)/shard_map/ppermute | solution.py:218
  108.9 10.8 %collective-permute-start.14 = (bf16[512,384]{1,0:T(8,128)(2,1)S(1)}, bf16[512,384]{1,0:T(8,128)(2,1)S(1)}, u32[]{:S(2)}, u32[]{:S(2)}) collective-permute-start(bf16[512,384]{1,0:T(8,128)(2,1)S(1)} %collective-permute-done.5.refs_6_), channel_id=1, source_target_pairs={{0,8},{8,0},{1,9},{9,1},{2,10},{10,2},{3,11},{11,3},{4,12},{12,4},... | collective-permute-start | bytes 1179656 | tf_op jit(solution)/shard_map/ppermute | solution.py:218
  110.9 8.8 %collective-permute-start.15 = (bf16[256,384]{1,0:T(8,128)(2,1)S(1)}, bf16[256,384]{1,0:T(8,128)(2,1)S(1)}, u32[]{:S(2)}, u32[]{:S(2)}) collective-permute-start(bf16[256,384]{1,0:T(8,128)(2,1)S(1)} %collective-permute-done.6.refs_7_), channel_id=1, source_target_pairs={{0,8},{8,0},{1,9},{9,1},{2,10},{10,2},{3,11},{11,3},{4,12},{12,4},... | collective-permute-start | bytes 589832 | tf_op jit(solution)/shard_map/ppermute | solution.py:218
  113.3 4.8 %copy-start.21 = (bf16[256,384]{1,0:T(8,128)(2,1)}, bf16[256,384]{1,0:T(8,128)(2,1)S(1)}, u32[]{:S(2)}) copy-start(bf16[256,384]{1,0:T(8,128)(2,1)S(1)} %collective-permute-done.7.refs_8_) | copy-start | bytes 589828
  113.3 7.8 %collective-permute-start.16 = (bf16[256,384]{1,0:T(8,128)(2,1)S(1)}, bf16[256,384]{1,0:T(8,128)(2,1)S(1)}, u32[]{:S(2)}, u32[]{:S(2)}) collective-permute-start(bf16[256,384]{1,0:T(8,128)(2,1)S(1)} %collective-permute-done.7.refs_8_), channel_id=1, source_target_pairs={{0,8},{8,0},{1,9},{9,1},{2,10},{10,2},{3,11},{11,3},{4,12},{12,4},... | collective-permute-start | bytes 589832 | tf_op jit(solution)/shard_map/ppermute | solution.py:218
  121.8 1.0 copy-start.2
  141.0 32.7 %all-to-all-start.1 = ((bf16[8,1040,128]{2,1,0:T(8,128)(2,1)}), bf16[8,1040,128]{2,1,0:T(8,128)(2,1)}, u32[]{:S(2)}, u32[]{:S(2)}) async-start(bf16[8,1040,128]{2,1,0:T(8,128)(2,1)} %pruned_ffn.1), calls=%async_computation.1 | async-start | bytes 4259840 | tf_op jit(solution)/shard_map/all_to_all | solution.py:225
  177.8 19.4 %all-to-all-start.2 = ((f32[64,2,128]{2,1,0:T(2,128)}), f32[64,2,128]{2,1,0:T(2,128)S(1)}, u32[]{:S(2)}, u32[]{:S(2)}) async-start(f32[64,2,128]{2,1,0:T(2,128)} %broadcast_in_dim.2), calls=%async_computation.2 | async-start | bytes 131072 | tf_op jit(solution)/shard_map/all_to_all | solution.py:228
  (21 other events, 18.5 us)
Sparse Core Ops, SparseCore 0:
  25.5 47.7 all-gather.2

commit v2 on v1

v2 whole, which is shorter than its diff:
```python
import functools
import math

import jax
import jax.numpy as jnp
from jax import lax
from jax.experimental import pallas as pl
from jax.experimental.pallas import tpu as pltpu
from jax.sharding import Mesh
from jax.sharding import PartitionSpec as P

BLOCK = 128
Z, YH, CORE, YL, X = 8, 4, 2, 2, 4
DP = ("z", "yh", "core")
TENSOR = ("yl", "x")
SHARDS = YL * X
BF, F32 = jnp.bfloat16, jnp.float32
EXTRA = 16
UNITS = (8,)
NT = (((1,), (1,)), ((), ()))


def first_slot(counts_ref, shard):
    total = jnp.int32(0)
    for other in range(SHARDS):
        total += jnp.where(other < shard, counts_ref[other], 0)
    return total


def pack_kernel(place, kept, counts, g0, g1, u0, u1, d0, d1, m0, m1, out):
    first = first_slot(counts, place[0])
    slots = []
    for gate, up, down, gain in ((g0, u0, d0, m0), (g1, u1, d1, m1)):
        body = jnp.concatenate([gate[...], up[...], down[...].T], axis=1)
        row = jnp.broadcast_to(gain[0], (EXTRA, BLOCK))
        slots.append((body, jnp.concatenate([row] * 3, axis=1)))
    for dest in range(SHARDS):
        second = dest == first + 1
        out[dest, :BLOCK, :] = jnp.where(second, slots[1][0], slots[0][0])
        out[dest, BLOCK:, :] = jnp.where(second, slots[1][1], slots[0][1])


def pack(place, kept, counts, gate_w, up_w, down_w, mask_gain):
    rows, units = gate_w.shape
    blocks = units // BLOCK

    def pick(k, kept, place):
        return jnp.clip(kept[place[0], k], 0, blocks - 1)

    cols = [
        pl.BlockSpec((rows, BLOCK), lambda i, p, b, n, k=k: (0, pick(k, b, p)))
        for k in (0, 1)
    ]
    down = [
        pl.BlockSpec((BLOCK, rows), lambda i, p, b, n, k=k: (pick(k, b, p), 0))
        for k in (0, 1)
    ]
    gain = [
        pl.BlockSpec((1, 1, BLOCK), lambda i, p, b, n, k=k: (pick(k, b, p), 0, 0))
        for k in (0, 1)
    ]
    gains = mask_gain.reshape(blocks, 1, BLOCK)
    shape = (SHARDS, BLOCK + EXTRA, 3 * BLOCK)
    return pl.pallas_call(
        pack_kernel,
        out_shape=jax.ShapeDtypeStruct(shape, BF),
        grid_spec=pltpu.PrefetchScalarGridSpec(
            num_scalar_prefetch=3,
            grid=(1,),
            in_specs=cols + cols + down + gain,
            out_specs=pl.BlockSpec(shape, lambda i, *_: (0, 0, 0)),
        ),
        name="pack_slots",
    )(place, kept, counts, gate_w, gate_w, up_w, up_w, down_w, down_w, gains, gains)


def ffn_kernel(scale, layout, place, normed, cot, gain, *refs):
    count = len(layout)
    mine, theirs = refs[:count], refs[count : 2 * count]
    out, unit_out = refs[2 * count : 2 * count + 2]
    n_buf, c_buf = refs[2 * count + 2 : 2 * count + 4]
    a_buf, b_buf = refs[2 * count + 4 : 3 * count + 4], refs[3 * count + 4 : 4 * count + 4]
    sems = refs[-1]
    z, core = place[1], place[2]
    copies, work = [], []

    def copy(source, target):
        one = pltpu.make_async_copy(source, target, sems.at[len(copies)])
        one.start()
        copies.append(one)
        return one

    half = normed.shape[1] // 2
    acts = []
    for source, target in ((normed, n_buf), (cot, c_buf)):
        for k in range(2):
            cols = pl.ds(k * half, half)
            acts.append(copy(source.at[:, cols], target.at[:, cols]))
    for i, pieces in enumerate(layout):
        row = 0
        for shift, yh0, length in pieces:
            rows = pl.ds(row, length * BLOCK)
            both = [
                copy(mine[i].at[rows, :], a_buf[i].at[rows, :]),
                copy(theirs[i].at[rows, :], b_buf[i].at[rows, :]),
            ]
            zz = shift[0] if isinstance(shift, tuple) else lax.rem(z + shift + Z, Z)
            for k in range(length):
                at = (zz * YH + yh0 + k) * (CORE * BLOCK)
                near = pl.multiple_of(at + core * BLOCK, BLOCK)
                other = pl.multiple_of(at + (1 - core) * BLOCK, BLOCK)
                work.append((both if k == 0 else [], near, other, a_buf[i], b_buf[i], row))
                row += BLOCK
    for one in acts:
        one.wait()
    tokens = normed.shape[0]
    gate_up = jnp.zeros((tokens, 2 * BLOCK), F32)
    hidden = jnp.zeros((tokens, BLOCK), F32)
    for waits, near, other, a, b, row in work:
        for one in waits:
            one.wait()
        n2 = jnp.concatenate([n_buf[:, pl.ds(near, BLOCK)], n_buf[:, pl.ds(other, BLOCK)]], axis=1)
        c2 = jnp.concatenate([c_buf[:, pl.ds(near, BLOCK)], c_buf[:, pl.ds(other, BLOCK)]], axis=1)
        w2 = jnp.concatenate([a[row : row + BLOCK, :], b[row : row + BLOCK, :]], axis=0)
        gate_up += jnp.dot(n2, w2[:, : 2 * BLOCK], preferred_element_type=F32)
        hidden += jnp.dot(c2, w2[:, 2 * BLOCK :], preferred_element_type=F32)
    gate, up = gate_up[:, :BLOCK], gate_up[:, BLOCK:]
    sig = jax.nn.sigmoid(gate)
    unit = jnp.sum(gate * sig * up * hidden, axis=0, keepdims=True) * scale
    unit_out[...] = jnp.broadcast_to(unit, unit_out.shape)
    masked = hidden * gain[0:1, :].astype(F32)
    gate_grad = (masked * up * sig * (1.0 + gate * (1.0 - sig))).astype(BF)
    up_grad = (masked * gate * sig).astype(BF)
    grads = jnp.concatenate([gate_grad, up_grad], axis=1)
    share = tokens // SHARDS
    for _, near, other, a, b, row in work:
        for at, w in ((near, a), (other, b)):
            part = lax.dot_general(grads, w[row : row + BLOCK, : 2 * BLOCK], NT, preferred_element_type=F32)
            first = pl.multiple_of(at // BLOCK * share, share)
            out[:, pl.ds(first, share), :] = part.astype(BF).reshape(SHARDS, share, BLOCK)


def ffn(place, normed, cot, gain, layout, mine, theirs):
    tokens, width = normed.shape
    rows = width // BLOCK * (tokens // SHARDS)
    vmem = pl.BlockSpec(memory_space=pltpu.VMEM)
    anyw = pl.BlockSpec(memory_space=pl.ANY)
    scale = 1.0 / math.sqrt(tokens * Z * YH * CORE)
    buffers = [pltpu.VMEM(x.shape, BF) for x in (normed, cot, *mine, *theirs)]
    copies = 4 + 2 * sum(len(pieces) for pieces in layout)
    return pl.pallas_call(
        functools.partial(ffn_kernel, scale, layout),
        out_shape=(
            jax.ShapeDtypeStruct((SHARDS, rows, BLOCK), BF),
            jax.ShapeDtypeStruct(UNITS + (BLOCK,), F32),
        ),
        in_specs=[pl.BlockSpec(memory_space=pltpu.SMEM), anyw, anyw, vmem] + [anyw] * (2 * len(mine)),
        out_specs=(vmem, vmem),
        scratch_shapes=buffers + [pltpu.SemaphoreType.DMA((copies,))],
        compiler_params=pltpu.CompilerParams(vmem_limit_bytes=56 << 20),
        name="pruned_ffn",
    )(place, normed, cot, gain, *mine, *theirs)


def final_kernel(place, act, gain, parts, grad):
    share, width = act.shape
    x = act[...].astype(F32)
    inv = lax.rsqrt(jnp.mean(x * x, axis=-1, keepdims=True) + 1e-05)
    dnormed = []
    for j in range(width // BLOCK):
        total = parts[0, j * share : (j + 1) * share, :].astype(F32)
        for src in range(1, SHARDS):
            total += parts[src, j * share : (j + 1) * share, :].astype(F32)
        dnormed.append(total)
    scaled = jnp.concatenate(dnormed, axis=1) * gain[...].astype(F32)
    normalized = x * inv
    mean = jnp.mean(scaled * normalized, axis=-1, keepdims=True)
    grad[...] = (inv * (scaled - normalized * mean)).astype(BF)


def final(place, act, gain, parts):
    tokens, width = act.shape
    share = tokens // SHARDS
    return pl.pallas_call(
        final_kernel,
        out_shape=jax.ShapeDtypeStruct((share, width), BF),
        grid_spec=pltpu.PrefetchScalarGridSpec(
            num_scalar_prefetch=1,
            grid=(1,),
            in_specs=[
                pl.BlockSpec((share, width), lambda i, p: (p[0], 0)),
                pl.BlockSpec((1, width), lambda i, p: (0, 0)),
                pl.BlockSpec(parts.shape, lambda i, p: (0, 0, 0)),
            ],
            out_specs=pl.BlockSpec((share, width), lambda i, p: (0, 0)),
        ),
        compiler_params=pltpu.CompilerParams(vmem_limit_bytes=12 << 20),
        name="input_grad",
    )(place, act, gain.reshape(1, -1), parts)


def whole(x, yh0):
    length = x.shape[0] // BLOCK
    return lax.all_gather(x, "z", axis=0, tiled=True), tuple(((i,), yh0, length) for i in range(Z))


def swapped(x, axis, size, distance):
    return lax.ppermute(x, axis, [(i, i ^ distance) for i in range(size)])


def summed_over_dp(x):
    for axis, size in (("core", CORE), ("yh", YH), ("z", Z)):
        distance = 1
        while distance < size:
            x = x + swapped(x, axis, size, distance)
            distance *= 2
    return x


def per_device(
    activations, norm_gain, gate_w, up_w, down_w, mask_gain, kept_blocks, kept_counts, cotangent
):
    me = lax.axis_index(TENSOR)
    place = jnp.stack([me, lax.axis_index("z"), lax.axis_index("core")]).astype(jnp.int32)

    sent = pack(place, kept_blocks, kept_counts, gate_w, up_w, down_w, mask_gain)
    got = lax.all_to_all(sent, TENSOR, split_axis=0, concat_axis=0, tiled=True)
    ends = jnp.cumsum(kept_counts)
    source = jnp.sum((ends <= me).astype(jnp.int32))
    slot = lax.dynamic_index_in_dim(got, source, 0, keepdims=False)
    column = lax.all_gather(slot[:BLOCK], "yh", axis=0, tiled=True)
    weights, order = whole(column, 0)

    cotangent, activations_late, slot, _ = lax.optimization_barrier((cotangent, activations, slot, column))
    unit_gain = slot[BLOCK:, :BLOCK]
    wide = jnp.broadcast_to(cotangent[None], (SHARDS,) + cotangent.shape)
    cot = lax.all_to_all(wide, TENSOR, split_axis=0, concat_axis=0, tiled=True).reshape(-1, cotangent.shape[1])
    act = activations_late.astype(F32)
    inv_rms = lax.rsqrt(jnp.mean(act * act, axis=-1, keepdims=True) + 1e-05)
    normed = (act * inv_rms * norm_gain.astype(F32)).astype(BF)

    other = lax.ppermute(weights, "core", [(0, 1), (1, 0)])
    parts, unit = ffn(place, normed, cot, unit_gain, (order,), [weights], [other])
    got = lax.all_to_all(parts, TENSOR, split_axis=0, concat_axis=0, tiled=True)
    input_grad = final(place, activations, norm_gain, got)

    units = lax.all_gather(summed_over_dp(unit)[:1], TENSOR, axis=0, tiled=True)
    width = BLOCK // (Z * YH * CORE)
    count = kept_counts[me]
    slots = ends[me] - count + jnp.arange(2)
    mine_units = lax.dynamic_slice_in_dim(units, lax.axis_index(DP) * width, width, 1)
    picked = jnp.take(mine_units, jnp.minimum(slots, SHARDS - 1), axis=0)
    gain_grad = jnp.where((jnp.arange(2) < count)[:, None], picked, 0.0)
    return input_grad, gain_grad


def solution(mesh):
    fine = Mesh(mesh.devices.reshape(Z, YH, CORE, YL, X), DP + TENSOR)
    placed = (
        P(DP, None),
        P(),
        P(DP, TENSOR),
        P(DP, TENSOR),
        P(TENSOR, DP),
        P(TENSOR),
        P(),
        P(),
        P(DP + TENSOR, None),
    )
    return jax.shard_map(
        per_device,
        mesh=fine,
        in_specs=placed,
        out_specs=(P(DP + TENSOR, None), P(TENSOR, DP)),
        check_vma=False,
    )
```

time: 208 us -> 207 us (level)
  starting transfers between devices: 77.5 us -> 46.6 us
  waiting for transfers between devices: 51.5 us -> 78.8 us
  local copies, waits for them, and re-layouts: 25.3 us -> 6.65 us
  blocking collectives: 17.4 us -> 34.3 us
    all_gather x1, waiting for transfers between devices: 0.01 us -> 43.6 us  [whole(): lax.all_gather(x, 'z', axis=0, tiled=True)]
    ppermute x17 -> x7, starting transfers between devices: 54 us -> 26 us  [the longest x6 24 us: swapped(): return lax.ppermute(x, axis, [(i, i ^ distance) for i in range(size)])]
    all_to_all x1, waiting for transfers between devices: 25.8 us -> 0.01 us  [per_device(): got = lax.all_to_all(parts, TENSOR, split_axis=0, concat_axis=0, tiled=True)]
    ppermute x17 -> x7, waiting for transfers between devices: 8.01 us -> 29.7 us  [the longest x6 26.8 us: swapped(): return lax.ppermute(x, axis, [(i, i ^ distance) for i in range(size)])]
    unnamed x65 -> x14, local copies, waits for them, and re-layouts: 21.8 us -> 1.38 us
    all_gather x0 -> x1, blocking collectives: none -> 16.8 us  [per_device(): units = lax.all_gather(summed_over_dp(unit)[:1], TENSOR, axis=0, tiled=True)]
    all_to_all x1, waiting for transfers between devices: 12.3 us -> 0.01 us  [per_device(): lax.all_to_all(wide, TENSOR, split_axis=0, concat_axis=0, tiled=True)]
  transfers between devices with their start and end apart: 21 -> 11, of which waited for: 5 -> 9; matrix products, arithmetic and copies ran while one was open for 2% -> 4% of each run, Pallas kernels for 0% -> 0%
where the time goes in v2:
time: 207 us; the launch traced here: 203 us
  waiting for transfers between devices  78.8 us (38%)
  starting transfers between devices  46.6 us (23%)
  blocking collectives  34.3 us (17%)
  between operations  17.4 us (8%)
  Pallas kernels  14.3 us (7%)
  local copies, waits for them, and re-layouts  6.65 us (3%)
  other arithmetic  5.14 us (2%)
    all_gather x1, waiting for transfers between devices, whole(): lax.all_gather(x, 'z', axis=0, tiled=True)  43.6 us
    ppermute x6, waiting for transfers between devices, swapped(): return lax.ppermute(x, axis, [(i, i ^ distance) for i in range(size)])  26.8 us
    ppermute x6, starting transfers between devices, swapped(): return lax.ppermute(x, axis, [(i, i ^ distance) for i in range(size)])  24 us
    all_gather x1, blocking collectives, per_device(): column = lax.all_gather(slot[:BLOCK], 'yh', axis=0, tiled=True)  17.6 us
    all_gather x1, blocking collectives, per_device(): units = lax.all_gather(summed_over_dp(unit)[:1], TENSOR, axis=0, tiled=True)  16.8 us
    all_to_all x1, starting transfers between devices, per_device(): got = lax.all_to_all(sent, TENSOR, split_axis=0, concat_axis=0, tiled=True)  9.32 us
    pallas_call x1, Pallas kernels, ffn(): pl.pallas_call(functools.partial(ffn_kernel, scale, layout), out_shape=(j...  8.12 us
    all_to_all x1, starting transfers between devices, per_device(): got = lax.all_to_all(parts, TENSOR, split_axis=0, concat_axis=0, tiled=True)  5.73 us
  transfers between devices with their start and end apart: 11, of which 9 were waited for; matrix products, arithmetic and copies ran while one was open for 4% of the time, Pallas kernels for 0%

profile of v2, /device:TPU:6, one launch (start us, length us, event | category | flops | bytes accessed | tf_op | source)
XLA Modules:
  0.0 203.2 jit_solution(4465101424619035157)
XLA Ops:
  7.2 1.3 copy.20.m0.m1
  8.5 1.3 copy.19.kept
  9.8 0.7 pad_add_fusion.place
  10.5 2.7 %pack_slots.1 = bf16[8,144,384]{2,1,0:T(8,128)(2,1)} custom-call(s32[3]{0:T(128)} %pad_add_fusion.place, s32[8,2]{1,0:T(8,128)} %copy.19.kept, s32[8]{0:T(128)} %counts.1, bf16[128,1792]{1,0:T(8,128)(2,1)} %g1.1, bf16[128,1792]{1,0:T(8,128)(2,1)} %g1.1, bf16[128,1792]{1,0:T(8,128)(2,1)} %u1_.1, bf16[128,1792]{1,0:T(8,128)(2,1)} %u1_.1, ...), custom_call_target="tpu_custom_call" | custom-call | tf_op jit(solution)/shard_map/pack_slots/pallas_call | solution.py:64
  13.2 9.3 %all-to-all-start = ((bf16[8,144,384]{2,1,0:T(8,128)(2,1)}), bf16[8,144,384]{2,1,0:T(8,128)(2,1)S(1)}, u32[]{:S(2)}, u32[]{:S(2)}) async-start(bf16[8,144,384]{2,1,0:T(8,128)(2,1)} %pack_slots.1), calls=%async_computation | async-start | bytes 1769472 | tf_op jit(solution)/shard_map/all_to_all | solution.py:227
  22.7 0.6 fusion.3
  25.3 5.5 %all-to-all-done = bf16[8,144,384]{2,1,0:T(8,128)(2,1)S(1)} async-done(((bf16[8,144,384]{2,1,0:T(8,128)(2,1)}), bf16[8,144,384]{2,1,0:T(8,128)(2,1)S(1)}, u32[]{:S(2)}, u32[]{:S(2)}) %all-to-all-start) | async-done | bytes 884768 | tf_op jit(solution)/shard_map/all_to_all | solution.py:227
  30.8 17.6 %all-gather = bf16[1,512,384]{2,1,0:T(8,128)(2,1)} all-gather(bf16[1,128,384]{2,1,0:T(8,128)(2,1)S(1)} %constant_dynamic-slice_fusion), channel_id=2, replica_groups=mesh['z'=8,'yh'=4,'core'=2,'yl'=2,'x'=4] {'yh'}, dimensions={1}, use_global_device_ids=true | all-gather | bytes 491520 | tf_op jit(solution)/shard_map/all_gather | solution.py:231
  48.4 1.5 broadcast_in_dim.27
  50.0 5.6 %all-to-all-start.1 = ((bf16[8,16,8192]{2,1,0:T(8,128)(2,1)}), bf16[8,16,8192]{2,1,0:T(8,128)(2,1)}, u32[]{:S(2)}, u32[]{:S(2)}) async-start(bf16[8,16,8192]{2,1,0:T(8,128)(2,1)} %broadcast_in_dim.27), calls=%async_computation.1 | async-start | bytes 4194304 | tf_op jit(solution)/shard_map/all_to_all | solution.py:237
  55.5 43.6 %all-gather.5.cloned.1.call-done = bf16[1,4096,384]{2,1,0:T(8,128)(2,1)} async-done(((bf16[1,512,384]{2,1,0:T(8,128)(2,1)}), bf16[1,4096,384]{2,1,0:T(8,128)(2,1)}) %all-gather.5.cloned.1.call-update) | async-done | bytes 3145744 | tf_op jit(solution)/shard_map/all_gather | solution.py:204
  99.2 1.9 collective-permute-start
  101.1 0.6 slice.14.gain
  102.2 1.9 fusion.2.normed
  104.1 2.9 %collective-permute-done.refs_1_ = bf16[4096,384]{1,0:T(8,128)(2,1)} collective-permute-done((bf16[4096,384]{1,0:T(8,128)(2,1)}, bf16[4096,384]{1,0:T(8,128)(2,1)}, u32[]{:S(2)}, u32[]{:S(2)}) %collective-permute-start) | collective-permute-done | bytes 3145760 | tf_op jit(solution)/shard_map/ppermute | solution.py:242
  107.1 8.1 %pruned_ffn.1 = (bf16[8,1024,128]{2,1,0:T(8,128)(2,1)}, f32[8,128]{1,0:T(8,128)}) custom-call(s32[3]{0:T(128)} %pad_add_fusion.place, bf16[128,8192]{1,0:T(8,128)(2,1)} %fusion.2.normed, bf16[128,8192]{1,0:T(8,128)(2,1)} %bitcast.6.cot, bf16[16,128]{1,0:T(8,128)(2,1)} %slice.14.gain, bf16[4096,384]{1,0:T(8,128)(2,1)} %bitcast.17, ...), custom_call_target="tpu_custom_call" | custom-call | tf_op jit(solution)/shard_map/pruned_ffn/pallas_call | solution.py:151
  115.2 5.7 %all-to-all-start.2 = ((bf16[8,1024,128]{2,1,0:T(8,128)(2,1)}), bf16[8,1024,128]{2,1,0:T(8,128)(2,1)}, u32[]{:S(2)}, u32[]{:S(2)}) async-start(bf16[8,1024,128]{2,1,0:T(8,128)(2,1)} %get-tuple-element.10), calls=%async_computation.2 | async-start | bytes 4194304 | tf_op jit(solution)/shard_map/all_to_all | solution.py:244
  120.9 1.9 collective-permute-start.1
  122.9 1.1 collective-permute-done.1
  124.0 4.3 %collective-permute-start.2 = (f32[8,128]{1,0:T(8,128)S(1)}, f32[8,128]{1,0:T(8,128)S(1)}, u32[]{:S(2)}, u32[]{:S(2)}) collective-permute-start(f32[8,128]{1,0:T(8,128)S(1)} %add.91), channel_id=1, source_target_pairs={{0,16},{16,0},{32,48},{48,32},{1,17},{17,1},{33,49},{49,33},{2,18}... | collective-permute-start | bytes 12296 | tf_op jit(solution)/shard_map/ppermute | solution.py:208
  128.3 15.9 %collective-permute-done.2 = f32[8,128]{1,0:T(8,128)S(1)} collective-permute-done((f32[8,128]{1,0:T(8,128)S(1)}, f32[8,128]{1,0:T(8,128)S(1)}, u32[]{:S(2)}, u32[]{:S(2)}) %collective-permute-start.2) | collective-permute-done | bytes 4128 | tf_op jit(solution)/shard_map/ppermute | solution.py:208
  144.2 6.7 %collective-permute-start.3 = (f32[8,128]{1,0:T(8,128)S(1)}, f32[8,128]{1,0:T(8,128)S(1)}, u32[]{:S(2)}, u32[]{:S(2)}) collective-permute-start(f32[8,128]{1,0:T(8,128)S(1)} %add.92), channel_id=1, source_target_pairs={{0,32},{16,48},{32,0},{48,16},{1,33},{17,49},{33,1},{49,17},{2,34}... | collective-permute-start | bytes 12296 | tf_op jit(solution)/shard_map/ppermute | solution.py:208
  150.9 0.6 constant_dynamic-slice_fusion.2
  153.6 2.8 %collective-permute-start.4 = (f32[8,128]{1,0:T(8,128)S(1)}, f32[8,128]{1,0:T(8,128)S(1)}, u32[]{:S(2)}, u32[]{:S(2)}) collective-permute-start(f32[8,128]{1,0:T(8,128)S(1)} %add.93), channel_id=1, source_target_pairs={{0,64},{64,0},{128,192},{192,128},{256,320},{320,256},{384,448},{4... | collective-permute-start | bytes 12296 | tf_op jit(solution)/shard_map/ppermute | solution.py:208
  156.4 2.6 %collective-permute-done.4 = f32[8,128]{1,0:T(8,128)S(1)} collective-permute-done((f32[8,128]{1,0:T(8,128)S(1)}, f32[8,128]{1,0:T(8,128)S(1)}, u32[]{:S(2)}, u32[]{:S(2)}) %collective-permute-start.4) | collective-permute-done | bytes 4128 | tf_op jit(solution)/shard_map/ppermute | solution.py:208
  159.1 3.5 %collective-permute-start.5 = (f32[8,128]{1,0:T(8,128)S(1)}, f32[8,128]{1,0:T(8,128)S(1)}, u32[]{:S(2)}, u32[]{:S(2)}) collective-permute-start(f32[8,128]{1,0:T(8,128)S(1)} %add.94), channel_id=1, source_target_pairs={{0,128},{64,192},{128,0},{192,64},{256,384},{320,448},{384,256},{4... | collective-permute-start | bytes 12296 | tf_op jit(solution)/shard_map/ppermute | solution.py:208
  162.6 2.8 %collective-permute-done.5 = f32[8,128]{1,0:T(8,128)S(1)} collective-permute-done((f32[8,128]{1,0:T(8,128)S(1)}, f32[8,128]{1,0:T(8,128)S(1)}, u32[]{:S(2)}, u32[]{:S(2)}) %collective-permute-start.5) | collective-permute-done | bytes 4128 | tf_op jit(solution)/shard_map/ppermute | solution.py:208
  165.5 4.8 %collective-permute-start.6 = (f32[8,128]{1,0:T(8,128)S(1)}, f32[8,128]{1,0:T(8,128)S(1)}, u32[]{:S(2)}, u32[]{:S(2)}) collective-permute-start(f32[8,128]{1,0:T(8,128)S(1)} %add.95), channel_id=1, source_target_pairs={{0,256},{64,320},{128,384},{192,448},{256,0},{320,64},{384,128},{4... | collective-permute-start | bytes 12296 | tf_op jit(solution)/shard_map/ppermute | solution.py:208
  170.9 4.0 %collective-permute-done.6 = f32[8,128]{1,0:T(8,128)S(1)} collective-permute-done((f32[8,128]{1,0:T(8,128)S(1)}, f32[8,128]{1,0:T(8,128)S(1)}, u32[]{:S(2)}, u32[]{:S(2)}) %collective-permute-start.6) | collective-permute-done | bytes 4128 | tf_op jit(solution)/shard_map/ppermute | solution.py:208
  174.9 16.8 %all-gather.2 = f32[8,1,128]{2,1,0:T(1,128)S(1)} all-gather(f32[1,1,128]{2,1,0:T(1,128)S(1)} %slice_bitcast_fusion), channel_id=1, replica_groups=mesh['z'=8,'yh'=4,'core'=2,'yl'=2,'x'=4] {'yl','x'}, dimensions={0}, use_global_device_ids=true | all-gather | bytes 4608 | tf_op jit(solution)/shard_map/all_gather | solution.py:247
  192.3 0.6 select_select_fusion
  192.9 3.4 %input_grad.1 = bf16[16,8192]{1,0:T(8,128)(2,1)} custom-call(s32[3]{0:T(128)S(1)} %copy-done.1, bf16[128,8192]{1,0:T(8,128)(2,1)S(1)} %copy-done, bf16[1,8192]{1,0:T(2,128)(2,1)S(1)} %reshape.61.gain, bf16[8,1024,128]{2,1,0:T(8,128)(2,1)} %all-to-all-done.2.parts), custom_call_target="tpu_custom_call" | custom-call | tf_op jit(solution)/shard_map/input_grad/pallas_call | solution.py:184
  (37 shorter events, 2.9 us)
Async XLA Ops:
  7.2 15.4 %copy-start.5 = (s32[8]{0:T(128)S(1)}, s32[8]{0:T(128)}, u32[]{:S(2)}) copy-start(s32[8]{0:T(128)} %counts.1) | copy-start | bytes 100
  10.5 37.9 %copy-start.2 = (bf16[16,8192]{1,0:T(8,128)(2,1)S(1)}, bf16[16,8192]{1,0:T(8,128)(2,1)}, u32[]{:S(2)}) copy-start(bf16[16,8192]{1,0:T(8,128)(2,1)} %param.17) | copy-start | bytes 786436
  13.2 17.6 %all-to-all-start = ((bf16[8,144,384]{2,1,0:T(8,128)(2,1)}), bf16[8,144,384]{2,1,0:T(8,128)(2,1)S(1)}, u32[]{:S(2)}, u32[]{:S(2)}) async-start(bf16[8,144,384]{2,1,0:T(8,128)(2,1)} %pack_slots.1), calls=%async_computation | async-start | bytes 1769472 | tf_op jit(solution)/shard_map/all_to_all | solution.py:227
  22.5 76.6 %all-gather.5.cloned.1.call-start = ((), (), s32[]{:S(2)}) async-start(), calls=%async_computation.3 | async-start | bytes 3538944 | tf_op jit(solution)/shard_map/all_gather | solution.py:204
  48.4 52.7 %copy-start.3 = (bf16[8192]{0:T(1024)(128)(2,1)S(1)}, bf16[8192]{0:T(1024)(128)(2,1)}, u32[]{:S(2)}) copy-start(bf16[8192]{0:T(1024)(128)(2,1)} %param.10) | copy-start | bytes 49156
  48.4 53.3 %copy-start = (bf16[128,8192]{1,0:T(8,128)(2,1)S(1)}, bf16[128,8192]{1,0:T(8,128)(2,1)}, u32[]{:S(2)}) copy-start(bf16[128,8192]{1,0:T(8,128)(2,1)} %act.1) | copy-start | bytes 6291460
  50.0 54.2 %all-to-all-start.1 = ((bf16[8,16,8192]{2,1,0:T(8,128)(2,1)}), bf16[8,16,8192]{2,1,0:T(8,128)(2,1)}, u32[]{:S(2)}, u32[]{:S(2)}) async-start(bf16[8,16,8192]{2,1,0:T(8,128)(2,1)} %broadcast_in_dim.27), calls=%async_computation.1 | async-start | bytes 4194304 | tf_op jit(solution)/shard_map/all_to_all | solution.py:237
  99.2 7.9 %collective-permute-start = (bf16[4096,384]{1,0:T(8,128)(2,1)}, bf16[4096,384]{1,0:T(8,128)(2,1)}, u32[]{:S(2)}, u32[]{:S(2)}) collective-permute-start(bf16[4096,384]{1,0:T(8,128)(2,1)} %bitcast.16), channel_id=1, source_target_pairs={{0,8},{8,0},{1,9},{9,1},{2,10},{10,2},{3,11},{11,3},{4,12},{12,4},... | collective-permute-start | bytes 9437192 | tf_op jit(solution)/shard_map/ppermute | solution.py:242
  115.2 5.8 %copy-start.4 = (f32[8,128]{1,0:T(8,128)S(1)}, f32[8,128]{1,0:T(8,128)}, u32[]{:S(2)}) copy-start(f32[8,128]{1,0:T(8,128)} %get-tuple-element.11) | copy-start | bytes 12292
  115.2 77.7 %copy-start.1 = (s32[3]{0:T(128)S(1)}, s32[3]{0:T(128)}, u32[]{:S(2)}) copy-start(s32[3]{0:T(128)} %pad_add_fusion.place) | copy-start | bytes 40
  115.2 77.7 %all-to-all-start.2 = ((bf16[8,1024,128]{2,1,0:T(8,128)(2,1)}), bf16[8,1024,128]{2,1,0:T(8,128)(2,1)}, u32[]{:S(2)}, u32[]{:S(2)}) async-start(bf16[8,1024,128]{2,1,0:T(8,128)(2,1)} %get-tuple-element.10), calls=%async_computation.2 | async-start | bytes 4194304 | tf_op jit(solution)/shard_map/all_to_all | solution.py:244
  120.9 3.0 %collective-permute-start.1 = (f32[8,128]{1,0:T(8,128)S(1)}, f32[8,128]{1,0:T(8,128)S(1)}, u32[]{:S(2)}, u32[]{:S(2)}) collective-permute-start(f32[8,128]{1,0:T(8,128)S(1)} %copy-done.4), channel_id=1, source_target_pairs={{0,8},{8,0},{1,9},{9,1},{2,10},{10,2},{3,11},{11,3},{4,12},{12,4},... | collective-permute-start | bytes 12296 | tf_op jit(solution)/shard_map/ppermute | solution.py:208
  124.0 20.2 %collective-permute-start.2 = (f32[8,128]{1,0:T(8,128)S(1)}, f32[8,128]{1,0:T(8,128)S(1)}, u32[]{:S(2)}, u32[]{:S(2)}) collective-permute-start(f32[8,128]{1,0:T(8,128)S(1)} %add.91), channel_id=1, source_target_pairs={{0,16},{16,0},{32,48},{48,32},{1,17},{17,1},{33,49},{49,33},{2,18}... | collective-permute-start | bytes 12296 | tf_op jit(solution)/shard_map/ppermute | solution.py:208
  144.2 9.4 %collective-permute-start.3 = (f32[8,128]{1,0:T(8,128)S(1)}, f32[8,128]{1,0:T(8,128)S(1)}, u32[]{:S(2)}, u32[]{:S(2)}) collective-permute-start(f32[8,128]{1,0:T(8,128)S(1)} %add.92), channel_id=1, source_target_pairs={{0,32},{16,48},{32,0},{48,16},{1,33},{17,49},{33,1},{49,17},{2,34}... | collective-permute-start | bytes 12296 | tf_op jit(solution)/shard_map/ppermute | solution.py:208
  153.6 5.5 %collective-permute-start.4 = (f32[8,128]{1,0:T(8,128)S(1)}, f32[8,128]{1,0:T(8,128)S(1)}, u32[]{:S(2)}, u32[]{:S(2)}) collective-permute-start(f32[8,128]{1,0:T(8,128)S(1)} %add.93), channel_id=1, source_target_pairs={{0,64},{64,0},{128,192},{192,128},{256,320},{320,256},{384,448},{4... | collective-permute-start | bytes 12296 | tf_op jit(solution)/shard_map/ppermute | solution.py:208
  159.1 6.4 %collective-permute-start.5 = (f32[8,128]{1,0:T(8,128)S(1)}, f32[8,128]{1,0:T(8,128)S(1)}, u32[]{:S(2)}, u32[]{:S(2)}) collective-permute-start(f32[8,128]{1,0:T(8,128)S(1)} %add.94), channel_id=1, source_target_pairs={{0,128},{64,192},{128,0},{192,64},{256,384},{320,448},{384,256},{4... | collective-permute-start | bytes 12296 | tf_op jit(solution)/shard_map/ppermute | solution.py:208
  165.5 9.4 %collective-permute-start.6 = (f32[8,128]{1,0:T(8,128)S(1)}, f32[8,128]{1,0:T(8,128)S(1)}, u32[]{:S(2)}, u32[]{:S(2)}) collective-permute-start(f32[8,128]{1,0:T(8,128)S(1)} %add.95), channel_id=1, source_target_pairs={{0,256},{64,320},{128,384},{192,448},{256,0},{320,64},{384,128},{4... | collective-permute-start | bytes 12296 | tf_op jit(solution)/shard_map/ppermute | solution.py:208
Sparse Core Ops, SparseCore 0:
  48.5 50.6 all-gather.4

commit v3 on v2

--- a/solution.py
+++ b/solution.py
@@ -17,6 +17,7 @@
 BF, F32 = jnp.bfloat16, jnp.float32
 EXTRA = 16
 UNITS = (8,)
+PARTS = 2
 NT = (((1,), (1,)), ((), ()))
 
 
@@ -106,7 +107,7 @@
             ]
             zz = shift[0] if isinstance(shift, tuple) else lax.rem(z + shift + Z, Z)
             for k in range(length):
-                at = (zz * YH + yh0 + k) * (CORE * BLOCK)
+                at = (zz * YH + lax.rem(place[3] - yh0 - k + YH, YH)) * (CORE * BLOCK)
                 near = pl.multiple_of(at + core * BLOCK, BLOCK)
                 other = pl.multiple_of(at + (1 - core) * BLOCK, BLOCK)
                 work.append((both if k == 0 else [], near, other, a_buf[i], b_buf[i], row))
@@ -208,8 +209,8 @@
     return lax.ppermute(x, axis, [(i, i ^ distance) for i in range(size)])
 
 
-def summed_over_dp(x):
-    for axis, size in (("core", CORE), ("yh", YH), ("z", Z)):
+def summed(x, *axes):
+    for axis, size in axes:
         distance = 1
         while distance < size:
             x = x + swapped(x, axis, size, distance)
@@ -217,19 +218,25 @@
     return x
 
 
+def along_y(x):
+    shifted = [lax.ppermute(x, "yh", [(i, (i + k) % YH) for i in range(YH)]) for k in range(1, YH)]
+    return jnp.concatenate([x] + shifted, axis=0)
+
+
 def per_device(
     activations, norm_gain, gate_w, up_w, down_w, mask_gain, kept_blocks, kept_counts, cotangent
 ):
     me = lax.axis_index(TENSOR)
-    place = jnp.stack([me, lax.axis_index("z"), lax.axis_index("core")]).astype(jnp.int32)
+    place = jnp.stack([me, lax.axis_index("z"), lax.axis_index("core"), lax.axis_index("yh")]).astype(jnp.int32)
 
     sent = pack(place, kept_blocks, kept_counts, gate_w, up_w, down_w, mask_gain)
     got = lax.all_to_all(sent, TENSOR, split_axis=0, concat_axis=0, tiled=True)
     ends = jnp.cumsum(kept_counts)
     source = jnp.sum((ends <= me).astype(jnp.int32))
     slot = lax.dynamic_index_in_dim(got, source, 0, keepdims=False)
-    column = lax.all_gather(slot[:BLOCK], "yh", axis=0, tiled=True)
-    weights, order = whole(column, 0)
+    column = along_y(slot[:BLOCK])
+    halves = [whole(part, i * YH // PARTS) for i, part in enumerate(jnp.split(column, PARTS))]
+    weights, order = [one for one, _ in halves], tuple(one for _, one in halves)
 
     cotangent, activations_late, slot, _ = lax.optimization_barrier((cotangent, activations, slot, column))
     unit_gain = slot[BLOCK:, :BLOCK]
@@ -239,18 +246,20 @@
     inv_rms = lax.rsqrt(jnp.mean(act * act, axis=-1, keepdims=True) + 1e-05)
     normed = (act * inv_rms * norm_gain.astype(F32)).astype(BF)
 
-    other = lax.ppermute(weights, "core", [(0, 1), (1, 0)])
-    parts, unit = ffn(place, normed, cot, unit_gain, (order,), [weights], [other])
+    other = [lax.ppermute(one, "core", [(0, 1), (1, 0)]) for one in weights]
+    parts, unit = ffn(place, normed, cot, unit_gain, order, weights, other)
     got = lax.all_to_all(parts, TENSOR, split_axis=0, concat_axis=0, tiled=True)
+    unit = summed(unit, ("core", CORE), ("z", Z))
+    unit, got = lax.optimization_barrier((unit, got))
+    copies = jnp.broadcast_to(unit[None, :1], (YH * SHARDS, 1, BLOCK))
+    units = lax.all_to_all(copies, ("yh",) + TENSOR, split_axis=0, concat_axis=0, tiled=True)
     input_grad = final(place, activations, norm_gain, got)
-
-    units = lax.all_gather(summed_over_dp(unit)[:1], TENSOR, axis=0, tiled=True)
     width = BLOCK // (Z * YH * CORE)
-    count = kept_counts[me]
-    slots = ends[me] - count + jnp.arange(2)
-    mine_units = lax.dynamic_slice_in_dim(units, lax.axis_index(DP) * width, width, 1)
-    picked = jnp.take(mine_units, jnp.minimum(slots, SHARDS - 1), axis=0)
-    gain_grad = jnp.where((jnp.arange(2) < count)[:, None], picked, 0.0)
+    units = lax.dynamic_slice_in_dim(units.reshape(YH * SHARDS, BLOCK), lax.axis_index(DP) * width, width, 1)
+    count, k = kept_counts[me], jnp.arange(2)
+    source = jnp.tile(jnp.arange(SHARDS), YH)
+    wanted = (source[None] == ends[me] - count + k[:, None]) & (k < count)[:, None]
+    gain_grad = jnp.sum(jnp.where(wanted[:, :, None], units[None], 0.0), axis=1)
     return input_grad, gain_grad
 
 

time: 207 us -> 205 us (level)
  blocking collectives: 34.3 us -> 0 us
  waiting for transfers between devices: 78.8 us -> 94.7 us
  starting transfers between devices: 46.6 us -> 61.8 us
    all_gather x2 -> x0, blocking collectives: 34.3 us -> none  [the longest x1 17.6 us: per_device(): column = lax.all_gather(slot[:BLOCK], 'yh', axis=0, tiled=True)]
    all_gather x1 -> x2, waiting for transfers between devices: 43.6 us -> 64.1 us  [whole(): lax.all_gather(x, 'z', axis=0, tiled=True)]
    ppermute x6 -> x4, waiting for transfers between devices: 26.8 us -> 8.34 us  [swapped(): return lax.ppermute(x, axis, [(i, i ^ distance) for i in range(size)])]
    ppermute x1 -> x5, starting transfers between devices: 1.91 us -> 16.9 us  [the longest x3 13.1 us: along_y(): lax.ppermute(x, 'yh', [(i, (i + k) % YH) for i in range(YH)])]
    ppermute x6 -> x4, starting transfers between devices: 24 us -> 12.7 us  [swapped(): return lax.ppermute(x, axis, [(i, i ^ distance) for i in range(size)])]
    all_to_all x0 -> x1, starting transfers between devices: none -> 8.92 us  [per_device(): lax.all_to_all(copies, ('yh',) + TENSOR, split_axis=0, concat_axis=0, til...]
    ppermute x1 -> x5, waiting for transfers between devices: 2.93 us -> 11.5 us  [the longest x3 9.78 us: along_y(): lax.ppermute(x, 'yh', [(i, (i + k) % YH) for i in range(YH)])]
    all_to_all x0 -> x1, waiting for transfers between devices: none -> 4.43 us  [per_device(): lax.all_to_all(copies, ('yh',) + TENSOR, split_axis=0, concat_axis=0, til...]
  transfers between devices with their start and end apart: 11 -> 15, of which waited for: 9 -> 12; matrix products, arithmetic and copies ran while one was open for 4% -> 4% of each run, Pallas kernels for 0% -> 2%
where the time goes in v3:
time: 205 us; the launch traced here: 203 us
  waiting for transfers between devices  94.7 us (46%)
  starting transfers between devices  61.8 us (30%)
  between operations  17.5 us (9%)
  Pallas kernels  15.4 us (8%)
  local copies, waits for them, and re-layouts  6.9 us (3%)
  other arithmetic  6.67 us (3%)
    all_gather x2, waiting for transfers between devices, whole(): lax.all_gather(x, 'z', axis=0, tiled=True)  64.1 us
    ppermute x3, starting transfers between devices, along_y(): lax.ppermute(x, 'yh', [(i, (i + k) % YH) for i in range(YH)])  13.1 us
    ppermute x4, starting transfers between devices, swapped(): return lax.ppermute(x, axis, [(i, i ^ distance) for i in range(size)])  12.7 us
    ppermute x3, waiting for transfers between devices, along_y(): lax.ppermute(x, 'yh', [(i, (i + k) % YH) for i in range(YH)])  9.78 us
    all_to_all x1, starting transfers between devices, per_device(): got = lax.all_to_all(sent, TENSOR, split_axis=0, concat_axis=0, tiled=True)  9.45 us
    pallas_call x1, Pallas kernels, ffn(): pl.pallas_call(functools.partial(ffn_kernel, scale, layout), out_shape=(j...  9.23 us
    all_to_all x1, starting transfers between devices, per_device(): lax.all_to_all(copies, ('yh',) + TENSOR, split_axis=0, concat_axis=0, til...  8.92 us
    ppermute x4, waiting for transfers between devices, swapped(): return lax.ppermute(x, axis, [(i, i ^ distance) for i in range(size)])  8.34 us
  transfers between devices with their start and end apart: 15, of which 12 were waited for; matrix products, arithmetic and copies ran while one was open for 4% of the time, Pallas kernels for 2%

profile of v3, /device:TPU:6, one launch (start us, length us, event | category | flops | bytes accessed | tf_op | source)
XLA Modules:
  0.0 203.0 jit_solution(2679195230591387965)
XLA Ops:
  7.2 1.3 copy.22.kept
  8.5 1.3 copy.23.m0.m1
  10.4 2.7 %pack_slots.1 = bf16[8,144,384]{2,1,0:T(8,128)(2,1)} custom-call(s32[4]{0:T(128)} %pad_add_fusion.place, s32[8,2]{1,0:T(8,128)} %copy.22.kept, s32[8]{0:T(128)} %counts.1, bf16[128,1792]{1,0:T(8,128)(2,1)} %g1.1, bf16[128,1792]{1,0:T(8,128)(2,1)} %g1.1, bf16[128,1792]{1,0:T(8,128)(2,1)} %u1_.1, bf16[128,1792]{1,0:T(8,128)(2,1)} %u1_.1, ...), custom_call_target="tpu_custom_call" | custom-call | tf_op jit(solution)/shard_map/pack_slots/pallas_call | solution.py:65
  13.1 9.4 %all-to-all-start = ((bf16[8,144,384]{2,1,0:T(8,128)(2,1)}), bf16[8,144,384]{2,1,0:T(8,128)(2,1)S(1)}, u32[]{:S(2)}, u32[]{:S(2)}) async-start(bf16[8,144,384]{2,1,0:T(8,128)(2,1)} %pack_slots.1), calls=%async_computation | async-start | bytes 1769472 | tf_op jit(solution)/shard_map/all_to_all | solution.py:233
  25.4 5.5 %all-to-all-done = bf16[8,144,384]{2,1,0:T(8,128)(2,1)S(1)} async-done(((bf16[8,144,384]{2,1,0:T(8,128)(2,1)}), bf16[8,144,384]{2,1,0:T(8,128)(2,1)S(1)}, u32[]{:S(2)}, u32[]{:S(2)}) %all-to-all-start) | async-done | bytes 884768 | tf_op jit(solution)/shard_map/all_to_all | solution.py:233
  30.8 4.1 %collective-permute-start = (bf16[128,384]{1,0:T(8,128)(2,1)S(1)}, bf16[128,384]{1,0:T(8,128)(2,1)S(1)}, u32[]{:S(2)}, u32[]{:S(2)}) collective-permute-start(bf16[128,384]{1,0:T(8,128)(2,1)S(1)} %dynamic-slice_bitcast_fusion.1), channel_id=1, source_target_pairs={{0,16},{16,32},{32,48},{48,0},{1,17},{17,33},{33,49},{49,1},{2,18}... | collective-permute-start | bytes 294920 | tf_op jit(solution)/shard_map/ppermute | solution.py:222
  34.9 5.6 %collective-permute-done = bf16[128,384]{1,0:T(8,128)(2,1)S(1)} collective-permute-done((bf16[128,384]{1,0:T(8,128)(2,1)S(1)}, bf16[128,384]{1,0:T(8,128)(2,1)S(1)}, u32[]{:S(2)}, u32[]{:S(2)}) %collective-permute-start) | collective-permute-done | bytes 98336 | tf_op jit(solution)/shard_map/ppermute | solution.py:222
  41.2 2.7 %collective-permute-start.2 = (bf16[128,384]{1,0:T(8,128)(2,1)S(1)}, bf16[128,384]{1,0:T(8,128)(2,1)S(1)}, u32[]{:S(2)}, u32[]{:S(2)}) collective-permute-start(bf16[128,384]{1,0:T(8,128)(2,1)S(1)} %dynamic-slice_bitcast_fusion.1), channel_id=1, source_target_pairs={{0,48},{16,0},{32,16},{48,32},{1,49},{17,1},{33,17},{49,33},{2,50}... | collective-permute-start | bytes 294920 | tf_op jit(solution)/shard_map/ppermute | solution.py:222
  44.0 6.3 %collective-permute-start.1 = (bf16[128,384]{1,0:T(8,128)(2,1)S(1)}, bf16[128,384]{1,0:T(8,128)(2,1)S(1)}, u32[]{:S(2)}, u32[]{:S(2)}) collective-permute-start(bf16[128,384]{1,0:T(8,128)(2,1)S(1)} %dynamic-slice_bitcast_fusion.1), channel_id=1, source_target_pairs={{0,32},{16,48},{32,0},{48,16},{1,33},{17,49},{33,1},{49,17},{2,34}... | collective-permute-start | bytes 294920 | tf_op jit(solution)/shard_map/ppermute | solution.py:222
  50.3 4.2 %collective-permute-done.1 = bf16[128,384]{1,0:T(8,128)(2,1)S(1)} collective-permute-done((bf16[128,384]{1,0:T(8,128)(2,1)S(1)}, bf16[128,384]{1,0:T(8,128)(2,1)S(1)}, u32[]{:S(2)}, u32[]{:S(2)}) %collective-permute-start.1) | collective-permute-done | bytes 98336 | tf_op jit(solution)/shard_map/ppermute | solution.py:222
  54.5 0.7 pad_maximum_fusion.1
  55.2 1.5 broadcast_in_dim.42
  56.8 8.1 %all-to-all-start.1 = ((bf16[8,16,8192]{2,1,0:T(8,128)(2,1)}), bf16[8,16,8192]{2,1,0:T(8,128)(2,1)}, u32[]{:S(2)}, u32[]{:S(2)}) async-start(bf16[8,16,8192]{2,1,0:T(8,128)(2,1)} %broadcast_in_dim.42), calls=%async_computation.1 | async-start | bytes 4194304 | tf_op jit(solution)/shard_map/all_to_all | solution.py:244
  66.0 22.4 %all-gather.3.cloned.1.call-done.refs_0_ = bf16[2048,384]{1,0:T(8,128)(2,1)} async-done(((bf16[256,384]{1,0:T(8,128)(2,1)}), bf16[2048,384]{1,0:T(8,128)(2,1)}) %all-gather.3.cloned.1.call-update) | async-done | bytes 1572880 | tf_op jit(solution)/shard_map/all_gather | solution.py:205
  88.3 1.9 collective-permute-start.3
  90.3 41.8 %all-gather.5.cloned.1.call-done.refs_1_ = bf16[2048,384]{1,0:T(8,128)(2,1)} async-done(((bf16[256,384]{1,0:T(8,128)(2,1)}), bf16[2048,384]{1,0:T(8,128)(2,1)}) %all-gather.5.cloned.1.call-update) | async-done | bytes 1572880 | tf_op jit(solution)/shard_map/all_gather | solution.py:205
  132.0 1.9 collective-permute-start.4
  134.0 1.9 fusion.2.normed
  135.9 1.8 collective-permute-done.4.refs_3_
  137.7 9.2 %pruned_ffn.1 = (bf16[8,1024,128]{2,1,0:T(8,128)(2,1)}, f32[8,128]{1,0:T(8,128)}) custom-call(s32[4]{0:T(128)} %pad_add_fusion.place, bf16[128,8192]{1,0:T(8,128)(2,1)} %fusion.2.normed, bf16[128,8192]{1,0:T(8,128)(2,1)} %bitcast.7.cot, bf16[16,128]{1,0:T(8,128)(2,1)} %slice.14.gain, bf16[2048,384]{1,0:T(8,128)(2,1)} %all-gather.3.cloned.1.call-done.refs_0_, ...), custom_call_target="tpu_custom_call" | custom-call | tf_op jit(solution)/shard_map/pruned_ffn/pallas_call | solution.py:152
  146.9 5.7 %all-to-all-start.2 = ((bf16[8,1024,128]{2,1,0:T(8,128)(2,1)}), bf16[8,1024,128]{2,1,0:T(8,128)(2,1)}, u32[]{:S(2)}, u32[]{:S(2)}) async-start(bf16[8,1024,128]{2,1,0:T(8,128)(2,1)} %get-tuple-element.13), calls=%async_computation.2 | async-start | bytes 4194304 | tf_op jit(solution)/shard_map/all_to_all | solution.py:251
  152.7 1.9 collective-permute-start.5
  154.6 1.1 collective-permute-done.5
  155.7 2.8 %collective-permute-start.6 = (f32[8,128]{1,0:T(8,128)S(1)}, f32[8,128]{1,0:T(8,128)S(1)}, u32[]{:S(2)}, u32[]{:S(2)}) collective-permute-start(f32[8,128]{1,0:T(8,128)S(1)} %add.58), channel_id=1, source_target_pairs={{0,64},{64,0},{128,192},{192,128},{256,320},{320,256},{384,448},{4... | collective-permute-start | bytes 12296 | tf_op jit(solution)/shard_map/ppermute | solution.py:209
  159.1 2.1 %collective-permute-done.6 = f32[8,128]{1,0:T(8,128)S(1)} collective-permute-done((f32[8,128]{1,0:T(8,128)S(1)}, f32[8,128]{1,0:T(8,128)S(1)}, u32[]{:S(2)}, u32[]{:S(2)}) %collective-permute-start.6) | collective-permute-done | bytes 4128 | tf_op jit(solution)/shard_map/ppermute | solution.py:209
  161.2 3.2 %collective-permute-start.7 = (f32[8,128]{1,0:T(8,128)S(1)}, f32[8,128]{1,0:T(8,128)S(1)}, u32[]{:S(2)}, u32[]{:S(2)}) collective-permute-start(f32[8,128]{1,0:T(8,128)S(1)} %add.59), channel_id=1, source_target_pairs={{0,128},{64,192},{128,0},{192,64},{256,384},{320,448},{384,256},{4... | collective-permute-start | bytes 12296 | tf_op jit(solution)/shard_map/ppermute | solution.py:209
  167.6 4.8 %collective-permute-start.8 = (f32[8,128]{1,0:T(8,128)S(1)}, f32[8,128]{1,0:T(8,128)S(1)}, u32[]{:S(2)}, u32[]{:S(2)}) collective-permute-start(f32[8,128]{1,0:T(8,128)S(1)} %add.60), channel_id=1, source_target_pairs={{0,256},{64,320},{128,384},{192,448},{256,0},{320,64},{384,128},{4... | collective-permute-start | bytes 12296 | tf_op jit(solution)/shard_map/ppermute | solution.py:209
  172.5 4.5 %collective-permute-done.8 = f32[8,128]{1,0:T(8,128)S(1)} collective-permute-done((f32[8,128]{1,0:T(8,128)S(1)}, f32[8,128]{1,0:T(8,128)S(1)}, u32[]{:S(2)}, u32[]{:S(2)}) %collective-permute-start.8) | collective-permute-done | bytes 4128 | tf_op jit(solution)/shard_map/ppermute | solution.py:209
  177.0 0.8 all-to-all-done.2.parts
  178.4 8.9 %all-to-all-start.3 = ((f32[32,1,128]{2,1,0:T(1,128)}), f32[32,1,128]{2,1,0:T(1,128)S(1)}, u32[]{:S(2)}, u32[]{:S(2)}) async-start(f32[32,1,128]{2,1,0:T(1,128)} %broadcast_in_dim.45), calls=%async_computation.3 | async-start | bytes 32768 | tf_op jit(solution)/shard_map/all_to_all | solution.py:255
  187.4 3.4 %input_grad.1 = bf16[16,8192]{1,0:T(8,128)(2,1)} custom-call(s32[4]{0:T(128)S(1)} %copy-done.1, bf16[128,8192]{1,0:T(8,128)(2,1)S(1)} %copy-done, bf16[1,8192]{1,0:T(2,128)(2,1)S(1)} %reshape.93.gain, bf16[8,1024,128]{2,1,0:T(8,128)(2,1)} %all-to-all-done.2.parts), custom_call_target="tpu_custom_call" | custom-call | tf_op jit(solution)/shard_map/input_grad/pallas_call | solution.py:185
  190.8 4.4 %all-to-all-done.3 = f32[32,1,128]{2,1,0:T(1,128)S(1)} async-done(((f32[32,1,128]{2,1,0:T(1,128)}), f32[32,1,128]{2,1,0:T(1,128)S(1)}, u32[]{:S(2)}, u32[]{:S(2)}) %all-to-all-start.3) | async-done | bytes 16416 | tf_op jit(solution)/shard_map/all_to_all | solution.py:255
  (47 shorter events, 7.5 us)
Async XLA Ops:
  10.4 12.2 %copy-start.5 = (s32[8]{0:T(128)S(1)}, s32[8]{0:T(128)}, u32[]{:S(2)}) copy-start(s32[8]{0:T(128)} %counts.1) | copy-start | bytes 100
  13.1 42.1 %copy-start.2 = (bf16[16,8192]{1,0:T(8,128)(2,1)S(1)}, bf16[16,8192]{1,0:T(8,128)(2,1)}, u32[]{:S(2)}) copy-start(bf16[16,8192]{1,0:T(8,128)(2,1)} %param.17) | copy-start | bytes 786436
  13.1 17.7 %all-to-all-start = ((bf16[8,144,384]{2,1,0:T(8,128)(2,1)}), bf16[8,144,384]{2,1,0:T(8,128)(2,1)S(1)}, u32[]{:S(2)}, u32[]{:S(2)}) async-start(bf16[8,144,384]{2,1,0:T(8,128)(2,1)} %pack_slots.1), calls=%async_computation | async-start | bytes 1769472 | tf_op jit(solution)/shard_map/all_to_all | solution.py:233
  22.6 65.8 %all-gather.3.cloned.1.call-start = ((), (), s32[]{:S(2)}) async-start(), calls=%async_computation.4 | async-start | bytes 1769472 | tf_op jit(solution)/shard_map/all_gather | solution.py:205
  30.8 9.6 %collective-permute-start = (bf16[128,384]{1,0:T(8,128)(2,1)S(1)}, bf16[128,384]{1,0:T(8,128)(2,1)S(1)}, u32[]{:S(2)}, u32[]{:S(2)}) collective-permute-start(bf16[128,384]{1,0:T(8,128)(2,1)S(1)} %dynamic-slice_bitcast_fusion.1), channel_id=1, source_target_pairs={{0,16},{16,32},{32,48},{48,0},{1,17},{17,33},{33,49},{49,1},{2,18}... | collective-permute-start | bytes 294920 | tf_op jit(solution)/shard_map/ppermute | solution.py:222
  41.2 90.8 %all-gather.5.cloned.1.call-start = ((), (), s32[]{:S(2)}) async-start(), calls=%async_computation.5 | async-start | bytes 1769472 | tf_op jit(solution)/shard_map/all_gather | solution.py:205
  41.2 9.0 %collective-permute-start.2 = (bf16[128,384]{1,0:T(8,128)(2,1)S(1)}, bf16[128,384]{1,0:T(8,128)(2,1)S(1)}, u32[]{:S(2)}, u32[]{:S(2)}) collective-permute-start(bf16[128,384]{1,0:T(8,128)(2,1)S(1)} %dynamic-slice_bitcast_fusion.1), channel_id=1, source_target_pairs={{0,48},{16,0},{32,16},{48,32},{1,49},{17,1},{33,17},{49,33},{2,50}... | collective-permute-start | bytes 294920 | tf_op jit(solution)/shard_map/ppermute | solution.py:222
  44.0 10.5 %collective-permute-start.1 = (bf16[128,384]{1,0:T(8,128)(2,1)S(1)}, bf16[128,384]{1,0:T(8,128)(2,1)S(1)}, u32[]{:S(2)}, u32[]{:S(2)}) collective-permute-start(bf16[128,384]{1,0:T(8,128)(2,1)S(1)} %dynamic-slice_bitcast_fusion.1), channel_id=1, source_target_pairs={{0,32},{16,48},{32,0},{48,16},{1,33},{17,49},{33,1},{49,17},{2,34}... | collective-permute-start | bytes 294920 | tf_op jit(solution)/shard_map/ppermute | solution.py:222
  56.8 8.1 %copy-start.3 = (bf16[8192]{0:T(1024)(128)(2,1)S(1)}, bf16[8192]{0:T(1024)(128)(2,1)}, u32[]{:S(2)}) copy-start(bf16[8192]{0:T(1024)(128)(2,1)} %param.10) | copy-start | bytes 49156
  56.8 8.7 %copy-start = (bf16[128,8192]{1,0:T(8,128)(2,1)S(1)}, bf16[128,8192]{1,0:T(8,128)(2,1)}, u32[]{:S(2)}) copy-start(bf16[128,8192]{1,0:T(8,128)(2,1)} %act.1) | copy-start | bytes 6291460
  56.8 79.1 %all-to-all-start.1 = ((bf16[8,16,8192]{2,1,0:T(8,128)(2,1)}), bf16[8,16,8192]{2,1,0:T(8,128)(2,1)}, u32[]{:S(2)}, u32[]{:S(2)}) async-start(bf16[8,16,8192]{2,1,0:T(8,128)(2,1)} %broadcast_in_dim.42), calls=%async_computation.1 | async-start | bytes 4194304 | tf_op jit(solution)/shard_map/all_to_all | solution.py:244
  88.3 47.6 %collective-permute-start.3 = (bf16[2048,384]{1,0:T(8,128)(2,1)}, bf16[2048,384]{1,0:T(8,128)(2,1)}, u32[]{:S(2)}, u32[]{:S(2)}) collective-permute-start(bf16[2048,384]{1,0:T(8,128)(2,1)} %all-gather.3.cloned.1.call-done.refs_0_), channel_id=1, source_target_pairs={{0,8},{8,0},{1,9},{9,1},{2,10},{10,2},{3,11},{11,3},{4,12},{12,4},... | collective-permute-start | bytes 4718600 | tf_op jit(solution)/shard_map/ppermute | solution.py:249
  132.0 5.6 %collective-permute-start.4 = (bf16[2048,384]{1,0:T(8,128)(2,1)}, bf16[2048,384]{1,0:T(8,128)(2,1)}, u32[]{:S(2)}, u32[]{:S(2)}) collective-permute-start(bf16[2048,384]{1,0:T(8,128)(2,1)} %all-gather.5.cloned.1.call-done.refs_1_), channel_id=1, source_target_pairs={{0,8},{8,0},{1,9},{9,1},{2,10},{10,2},{3,11},{11,3},{4,12},{12,4},... | collective-permute-start | bytes 4718600 | tf_op jit(solution)/shard_map/ppermute | solution.py:249
  146.9 5.8 %copy-start.4 = (f32[8,128]{1,0:T(8,128)S(1)}, f32[8,128]{1,0:T(8,128)}, u32[]{:S(2)}) copy-start(f32[8,128]{1,0:T(8,128)} %get-tuple-element.12) | copy-start | bytes 12292
  146.9 40.5 %copy-start.1 = (s32[4]{0:T(128)S(1)}, s32[4]{0:T(128)}, u32[]{:S(2)}) copy-start(s32[4]{0:T(128)} %pad_add_fusion.place) | copy-start | bytes 52
  146.9 30.8 %all-to-all-start.2 = ((bf16[8,1024,128]{2,1,0:T(8,128)(2,1)}), bf16[8,1024,128]{2,1,0:T(8,128)(2,1)}, u32[]{:S(2)}, u32[]{:S(2)}) async-start(bf16[8,1024,128]{2,1,0:T(8,128)(2,1)} %get-tuple-element.13), calls=%async_computation.2 | async-start | bytes 4194304 | tf_op jit(solution)/shard_map/all_to_all | solution.py:251
  152.7 3.0 %collective-permute-start.5 = (f32[8,128]{1,0:T(8,128)S(1)}, f32[8,128]{1,0:T(8,128)S(1)}, u32[]{:S(2)}, u32[]{:S(2)}) collective-permute-start(f32[8,128]{1,0:T(8,128)S(1)} %copy-done.4), channel_id=1, source_target_pairs={{0,8},{8,0},{1,9},{9,1},{2,10},{10,2},{3,11},{11,3},{4,12},{12,4},... | collective-permute-start | bytes 12296 | tf_op jit(solution)/shard_map/ppermute | solution.py:209
  155.7 5.5 %collective-permute-start.6 = (f32[8,128]{1,0:T(8,128)S(1)}, f32[8,128]{1,0:T(8,128)S(1)}, u32[]{:S(2)}, u32[]{:S(2)}) collective-permute-start(f32[8,128]{1,0:T(8,128)S(1)} %add.58), channel_id=1, source_target_pairs={{0,64},{64,0},{128,192},{192,128},{256,320},{320,256},{384,448},{4... | collective-permute-start | bytes 12296 | tf_op jit(solution)/shard_map/ppermute | solution.py:209
  161.2 6.4 %collective-permute-start.7 = (f32[8,128]{1,0:T(8,128)S(1)}, f32[8,128]{1,0:T(8,128)S(1)}, u32[]{:S(2)}, u32[]{:S(2)}) collective-permute-start(f32[8,128]{1,0:T(8,128)S(1)} %add.59), channel_id=1, source_target_pairs={{0,128},{64,192},{128,0},{192,64},{256,384},{320,448},{384,256},{4... | collective-permute-start | bytes 12296 | tf_op jit(solution)/shard_map/ppermute | solution.py:209
  167.6 9.4 %collective-permute-start.8 = (f32[8,128]{1,0:T(8,128)S(1)}, f32[8,128]{1,0:T(8,128)S(1)}, u32[]{:S(2)}, u32[]{:S(2)}) collective-permute-start(f32[8,128]{1,0:T(8,128)S(1)} %add.60), channel_id=1, source_target_pairs={{0,256},{64,320},{128,384},{192,448},{256,0},{320,64},{384,128},{4... | collective-permute-start | bytes 12296 | tf_op jit(solution)/shard_map/ppermute | solution.py:209
  178.4 16.9 %all-to-all-start.3 = ((f32[32,1,128]{2,1,0:T(1,128)}), f32[32,1,128]{2,1,0:T(1,128)S(1)}, u32[]{:S(2)}, u32[]{:S(2)}) async-start(f32[32,1,128]{2,1,0:T(1,128)} %broadcast_in_dim.45), calls=%async_computation.3 | async-start | bytes 32768 | tf_op jit(solution)/shard_map/all_to_all | solution.py:255
Sparse Core Ops, SparseCore 0:
  41.3 46.9 all-gather.2
  90.4 41.5 all-gather.4

commit v4 on v3

--- a/solution.py
+++ b/solution.py
@@ -17,7 +17,6 @@
 BF, F32 = jnp.bfloat16, jnp.float32
 EXTRA = 16
 UNITS = (8,)
-PARTS = 2
 NT = (((1,), (1,)), ((), ()))
 
 
@@ -107,7 +106,7 @@
             ]
             zz = shift[0] if isinstance(shift, tuple) else lax.rem(z + shift + Z, Z)
             for k in range(length):
-                at = (zz * YH + lax.rem(place[3] - yh0 - k + YH, YH)) * (CORE * BLOCK)
+                at = (zz * YH + yh0 + k) * (CORE * BLOCK)
                 near = pl.multiple_of(at + core * BLOCK, BLOCK)
                 other = pl.multiple_of(at + (1 - core) * BLOCK, BLOCK)
                 work.append((both if k == 0 else [], near, other, a_buf[i], b_buf[i], row))
@@ -218,25 +217,20 @@
     return x
 
 
-def along_y(x):
-    shifted = [lax.ppermute(x, "yh", [(i, (i + k) % YH) for i in range(YH)]) for k in range(1, YH)]
-    return jnp.concatenate([x] + shifted, axis=0)
-
-
 def per_device(
     activations, norm_gain, gate_w, up_w, down_w, mask_gain, kept_blocks, kept_counts, cotangent
 ):
     me = lax.axis_index(TENSOR)
-    place = jnp.stack([me, lax.axis_index("z"), lax.axis_index("core"), lax.axis_index("yh")]).astype(jnp.int32)
+    place = jnp.stack([me, lax.axis_index("z"), lax.axis_index("core")]).astype(jnp.int32)
 
     sent = pack(place, kept_blocks, kept_counts, gate_w, up_w, down_w, mask_gain)
     got = lax.all_to_all(sent, TENSOR, split_axis=0, concat_axis=0, tiled=True)
     ends = jnp.cumsum(kept_counts)
     source = jnp.sum((ends <= me).astype(jnp.int32))
     slot = lax.dynamic_index_in_dim(got, source, 0, keepdims=False)
-    column = along_y(slot[:BLOCK])
-    halves = [whole(part, i * YH // PARTS) for i, part in enumerate(jnp.split(column, PARTS))]
-    weights, order = [one for one, _ in halves], tuple(one for _, one in halves)
+    column = lax.all_gather(slot[:BLOCK], "yh", axis=0, tiled=True)
+    gathered, order = whole(column, 0)
+    weights, order = [gathered], (order,)
 
     cotangent, activations_late, slot, _ = lax.optimization_barrier((cotangent, activations, slot, column))
     unit_gain = slot[BLOCK:, :BLOCK]

time: 205 us -> 173 us (0.84)
  waiting for transfers between devices: 94.7 us -> 65.2 us
  blocking collectives: 0 us -> 17.6 us
  starting transfers between devices: 61.8 us -> 44.5 us
    all_gather x2 -> x1, waiting for transfers between devices: 64.1 us -> 43.6 us  [whole(): lax.all_gather(x, 'z', axis=0, tiled=True)]
    all_gather x0 -> x1, blocking collectives: none -> 17.6 us  [per_device(): column = lax.all_gather(slot[:BLOCK], 'yh', axis=0, tiled=True)]
    ppermute x3 -> x0, starting transfers between devices: 13.1 us -> none  [along_y(): lax.ppermute(x, 'yh', [(i, (i + k) % YH) for i in range(YH)])]
    ppermute x3 -> x0, waiting for transfers between devices: 9.78 us -> none  [along_y(): lax.ppermute(x, 'yh', [(i, (i + k) % YH) for i in range(YH)])]
    all_to_all x1, starting transfers between devices: 8.1 us -> 5.57 us  [per_device(): lax.all_to_all(wide, TENSOR, split_axis=0, concat_axis=0, tiled=True)]
  transfers between devices with their start and end apart: 15 -> 10, of which waited for: 12 -> 9; matrix products, arithmetic and copies ran while one was open for 4% -> 4% of each run, Pallas kernels for 2% -> 2%
where the time goes in v4:
time: 173 us; the launch traced here: 171 us
  waiting for transfers between devices  65.2 us (38%)
  starting transfers between devices  44.5 us (26%)
  blocking collectives  17.6 us (10%)
  between operations  17.5 us (10%)
  Pallas kernels  14.3 us (8%)
  local copies, waits for them, and re-layouts  6.96 us (4%)
  other arithmetic  5.24 us (3%)
    all_gather x1, waiting for transfers between devices, whole(): lax.all_gather(x, 'z', axis=0, tiled=True)  43.6 us
    all_gather x1, blocking collectives, per_device(): column = lax.all_gather(slot[:BLOCK], 'yh', axis=0, tiled=True)  17.6 us
    ppermute x4, starting transfers between devices, swapped(): return lax.ppermute(x, axis, [(i, i ^ distance) for i in range(size)])  13.1 us
    all_to_all x1, starting transfers between devices, per_device(): got = lax.all_to_all(sent, TENSOR, split_axis=0, concat_axis=0, tiled=True)  9.32 us
    all_to_all x1, starting transfers between devices, per_device(): lax.all_to_all(copies, ('yh',) + TENSOR, split_axis=0, concat_axis=0, til...  8.92 us
    pallas_call x1, Pallas kernels, ffn(): pl.pallas_call(functools.partial(ffn_kernel, scale, layout), out_shape=(j...  8.12 us
    ppermute x4, waiting for transfers between devices, swapped(): return lax.ppermute(x, axis, [(i, i ^ distance) for i in range(size)])  7.88 us
    all_to_all x1, starting transfers between devices, per_device(): got = lax.all_to_all(parts, TENSOR, split_axis=0, concat_axis=0, tiled=True)  5.73 us
  transfers between devices with their start and end apart: 10, of which 9 were waited for; matrix products, arithmetic and copies ran while one was open for 4% of the time, Pallas kernels for 2%

profile of v4, /device:TPU:6, one launch (start us, length us, event | category | flops | bytes accessed | tf_op | source)
XLA Modules:
  0.0 171.2 jit_solution(941834909248170112)
XLA Ops:
  7.2 1.3 copy.23.m0.m1
  8.5 1.3 copy.22.kept
  9.8 0.6 pad_add_fusion.place
  10.4 2.8 %pack_slots.1 = bf16[8,144,384]{2,1,0:T(8,128)(2,1)} custom-call(s32[3]{0:T(128)} %pad_add_fusion.place, s32[8,2]{1,0:T(8,128)} %copy.22.kept, s32[8]{0:T(128)} %counts.1, bf16[128,1792]{1,0:T(8,128)(2,1)} %g1.1, bf16[128,1792]{1,0:T(8,128)(2,1)} %g1.1, bf16[128,1792]{1,0:T(8,128)(2,1)} %u1_.1, bf16[128,1792]{1,0:T(8,128)(2,1)} %u1_.1, ...), custom_call_target="tpu_custom_call" | custom-call | tf_op jit(solution)/shard_map/pack_slots/pallas_call | solution.py:64
  13.2 9.3 %all-to-all-start = ((bf16[8,144,384]{2,1,0:T(8,128)(2,1)}), bf16[8,144,384]{2,1,0:T(8,128)(2,1)S(1)}, u32[]{:S(2)}, u32[]{:S(2)}) async-start(bf16[8,144,384]{2,1,0:T(8,128)(2,1)} %pack_slots.1), calls=%async_computation | async-start | bytes 1769472 | tf_op jit(solution)/shard_map/all_to_all | solution.py:227
  22.7 0.6 fusion.3
  25.2 5.5 %all-to-all-done = bf16[8,144,384]{2,1,0:T(8,128)(2,1)S(1)} async-done(((bf16[8,144,384]{2,1,0:T(8,128)(2,1)}), bf16[8,144,384]{2,1,0:T(8,128)(2,1)S(1)}, u32[]{:S(2)}, u32[]{:S(2)}) %all-to-all-start) | async-done | bytes 884768 | tf_op jit(solution)/shard_map/all_to_all | solution.py:227
  30.7 17.6 %all-gather = bf16[1,512,384]{2,1,0:T(8,128)(2,1)} all-gather(bf16[1,128,384]{2,1,0:T(8,128)(2,1)S(1)} %constant_dynamic-slice_fusion), channel_id=2, replica_groups=mesh['z'=8,'yh'=4,'core'=2,'yl'=2,'x'=4] {'yh'}, dimensions={1}, use_global_device_ids=true | all-gather | bytes 491520 | tf_op jit(solution)/shard_map/all_gather | solution.py:231
  48.4 1.5 broadcast_in_dim.42
  49.9 5.6 %all-to-all-start.1 = ((bf16[8,16,8192]{2,1,0:T(8,128)(2,1)}), bf16[8,16,8192]{2,1,0:T(8,128)(2,1)}, u32[]{:S(2)}, u32[]{:S(2)}) async-start(bf16[8,16,8192]{2,1,0:T(8,128)(2,1)} %broadcast_in_dim.42), calls=%async_computation.1 | async-start | bytes 4194304 | tf_op jit(solution)/shard_map/all_to_all | solution.py:238
  55.5 43.6 %all-gather.4.cloned.1.call-done = bf16[1,4096,384]{2,1,0:T(8,128)(2,1)} async-done(((bf16[1,512,384]{2,1,0:T(8,128)(2,1)}), bf16[1,4096,384]{2,1,0:T(8,128)(2,1)}) %all-gather.4.cloned.1.call-update) | async-done | bytes 3145744 | tf_op jit(solution)/shard_map/all_gather | solution.py:204
  99.1 1.9 %collective-permute-start = (bf16[4096,384]{1,0:T(8,128)(2,1)}, bf16[4096,384]{1,0:T(8,128)(2,1)}, u32[]{:S(2)}, u32[]{:S(2)}) collective-permute-start(bf16[4096,384]{1,0:T(8,128)(2,1)} %bitcast.14), channel_id=1, source_target_pairs={{0,8},{8,0},{1,9},{9,1},{2,10},{10,2},{3,11},{11,3},{4,12},{12,4},... | collective-permute-start | bytes 9437192 | tf_op jit(solution)/shard_map/ppermute | solution.py:243
  101.1 0.6 slice.14.gain
  102.2 1.9 %fusion.2.normed = bf16[128,8192]{1,0:T(8,128)(2,1)} fusion(bf16[128,8192]{1,0:T(8,128)(2,1)S(1)} %copy-done, f32[8192]{0:T(1024)S(1)} %convert_element_type.15, f32[128]{0:T(128)S(1)} %add_rsqrt_fusion), kind=kLoop, calls=%fused_computation.4 | loop fusion | flops 4194304 | bytes 4227584 | tf_op jit(solution)/shard_map/convert_element_type | solution.py:241
  104.1 2.9 %collective-permute-done.refs_1_ = bf16[4096,384]{1,0:T(8,128)(2,1)} collective-permute-done((bf16[4096,384]{1,0:T(8,128)(2,1)}, bf16[4096,384]{1,0:T(8,128)(2,1)}, u32[]{:S(2)}, u32[]{:S(2)}) %collective-permute-start) | collective-permute-done | bytes 3145760 | tf_op jit(solution)/shard_map/ppermute | solution.py:243
  107.0 8.1 %pruned_ffn.1 = (bf16[8,1024,128]{2,1,0:T(8,128)(2,1)}, f32[8,128]{1,0:T(8,128)}) custom-call(s32[3]{0:T(128)} %pad_add_fusion.place, bf16[128,8192]{1,0:T(8,128)(2,1)} %fusion.2.normed, bf16[128,8192]{1,0:T(8,128)(2,1)} %bitcast.6.cot, bf16[16,128]{1,0:T(8,128)(2,1)} %slice.14.gain, bf16[4096,384]{1,0:T(8,128)(2,1)} %bitcast.15, ...), custom_call_target="tpu_custom_call" | custom-call | tf_op jit(solution)/shard_map/pruned_ffn/pallas_call | solution.py:151
  115.2 5.7 %all-to-all-start.2 = ((bf16[8,1024,128]{2,1,0:T(8,128)(2,1)}), bf16[8,1024,128]{2,1,0:T(8,128)(2,1)}, u32[]{:S(2)}, u32[]{:S(2)}) async-start(bf16[8,1024,128]{2,1,0:T(8,128)(2,1)} %get-tuple-element.13), calls=%async_computation.2 | async-start | bytes 4194304 | tf_op jit(solution)/shard_map/all_to_all | solution.py:245
  120.9 1.9 %collective-permute-start.1 = (f32[8,128]{1,0:T(8,128)S(1)}, f32[8,128]{1,0:T(8,128)S(1)}, u32[]{:S(2)}, u32[]{:S(2)}) collective-permute-start(f32[8,128]{1,0:T(8,128)S(1)} %copy-done.4), channel_id=1, source_target_pairs={{0,8},{8,0},{1,9},{9,1},{2,10},{10,2},{3,11},{11,3},{4,12},{12,4},... | collective-permute-start | bytes 12296 | tf_op jit(solution)/shard_map/ppermute | solution.py:208
  122.8 1.1 collective-permute-done.1
  123.9 2.8 %collective-permute-start.2 = (f32[8,128]{1,0:T(8,128)S(1)}, f32[8,128]{1,0:T(8,128)S(1)}, u32[]{:S(2)}, u32[]{:S(2)}) collective-permute-start(f32[8,128]{1,0:T(8,128)S(1)} %add.58), channel_id=1, source_target_pairs={{0,64},{64,0},{128,192},{192,128},{256,320},{320,256},{384,448},{4... | collective-permute-start | bytes 12296 | tf_op jit(solution)/shard_map/ppermute | solution.py:208
  127.4 2.1 %collective-permute-done.2 = f32[8,128]{1,0:T(8,128)S(1)} collective-permute-done((f32[8,128]{1,0:T(8,128)S(1)}, f32[8,128]{1,0:T(8,128)S(1)}, u32[]{:S(2)}, u32[]{:S(2)}) %collective-permute-start.2) | collective-permute-done | bytes 4128 | tf_op jit(solution)/shard_map/ppermute | solution.py:208
  129.4 3.6 %collective-permute-start.3 = (f32[8,128]{1,0:T(8,128)S(1)}, f32[8,128]{1,0:T(8,128)S(1)}, u32[]{:S(2)}, u32[]{:S(2)}) collective-permute-start(f32[8,128]{1,0:T(8,128)S(1)} %add.59), channel_id=1, source_target_pairs={{0,128},{64,192},{128,0},{192,64},{256,384},{320,448},{384,256},{4... | collective-permute-start | bytes 12296 | tf_op jit(solution)/shard_map/ppermute | solution.py:208
  133.0 0.7 iota_compare_fusion
  133.7 0.7 constant_dynamic-slice_fusion.2
  135.8 4.8 %collective-permute-start.4 = (f32[8,128]{1,0:T(8,128)S(1)}, f32[8,128]{1,0:T(8,128)S(1)}, u32[]{:S(2)}, u32[]{:S(2)}) collective-permute-start(f32[8,128]{1,0:T(8,128)S(1)} %add.60), channel_id=1, source_target_pairs={{0,256},{64,320},{128,384},{192,448},{256,0},{320,64},{384,128},{4... | collective-permute-start | bytes 12296 | tf_op jit(solution)/shard_map/ppermute | solution.py:208
  140.7 4.5 %collective-permute-done.4 = f32[8,128]{1,0:T(8,128)S(1)} collective-permute-done((f32[8,128]{1,0:T(8,128)S(1)}, f32[8,128]{1,0:T(8,128)S(1)}, u32[]{:S(2)}, u32[]{:S(2)}) %collective-permute-start.4) | collective-permute-done | bytes 4128 | tf_op jit(solution)/shard_map/ppermute | solution.py:208
  145.2 0.8 all-to-all-done.2.parts
  146.0 0.6 broadcast_in_dim.45
  146.6 8.9 %all-to-all-start.3 = ((f32[32,1,128]{2,1,0:T(1,128)}), f32[32,1,128]{2,1,0:T(1,128)S(1)}, u32[]{:S(2)}, u32[]{:S(2)}) async-start(f32[32,1,128]{2,1,0:T(1,128)} %broadcast_in_dim.45), calls=%async_computation.3 | async-start | bytes 32768 | tf_op jit(solution)/shard_map/all_to_all | solution.py:249
  155.7 3.4 %input_grad.1 = bf16[16,8192]{1,0:T(8,128)(2,1)} custom-call(s32[3]{0:T(128)S(1)} %copy-done.1, bf16[128,8192]{1,0:T(8,128)(2,1)S(1)} %copy-done, bf16[1,8192]{1,0:T(2,128)(2,1)S(1)} %reshape.93.gain, bf16[8,1024,128]{2,1,0:T(8,128)(2,1)} %all-to-all-done.2.parts), custom_call_target="tpu_custom_call" | custom-call | tf_op jit(solution)/shard_map/input_grad/pallas_call | solution.py:184
  159.1 4.5 %all-to-all-done.3 = f32[32,1,128]{2,1,0:T(1,128)S(1)} async-done(((f32[32,1,128]{2,1,0:T(1,128)}), f32[32,1,128]{2,1,0:T(1,128)S(1)}, u32[]{:S(2)}, u32[]{:S(2)}) %all-to-all-start.3) | async-done | bytes 16416 | tf_op jit(solution)/shard_map/all_to_all | solution.py:249
  163.7 0.7 select_reduce_fusion
  (35 shorter events, 1.9 us)
Async XLA Ops:
  7.2 15.3 %copy-start.5 = (s32[8]{0:T(128)S(1)}, s32[8]{0:T(128)}, u32[]{:S(2)}) copy-start(s32[8]{0:T(128)} %counts.1) | copy-start | bytes 100
  10.4 37.9 %copy-start.2 = (bf16[16,8192]{1,0:T(8,128)(2,1)S(1)}, bf16[16,8192]{1,0:T(8,128)(2,1)}, u32[]{:S(2)}) copy-start(bf16[16,8192]{1,0:T(8,128)(2,1)} %param.17) | copy-start | bytes 786436
  13.2 17.6 %all-to-all-start = ((bf16[8,144,384]{2,1,0:T(8,128)(2,1)}), bf16[8,144,384]{2,1,0:T(8,128)(2,1)S(1)}, u32[]{:S(2)}, u32[]{:S(2)}) async-start(bf16[8,144,384]{2,1,0:T(8,128)(2,1)} %pack_slots.1), calls=%async_computation | async-start | bytes 1769472 | tf_op jit(solution)/shard_map/all_to_all | solution.py:227
  22.5 76.6 %all-gather.4.cloned.1.call-start = ((), (), s32[]{:S(2)}) async-start(), calls=%async_computation.4 | async-start | bytes 3538944 | tf_op jit(solution)/shard_map/all_gather | solution.py:204
  48.4 52.7 %copy-start.3 = (bf16[8192]{0:T(1024)(128)(2,1)S(1)}, bf16[8192]{0:T(1024)(128)(2,1)}, u32[]{:S(2)}) copy-start(bf16[8192]{0:T(1024)(128)(2,1)} %param.10) | copy-start | bytes 49156
  48.4 53.3 %copy-start = (bf16[128,8192]{1,0:T(8,128)(2,1)S(1)}, bf16[128,8192]{1,0:T(8,128)(2,1)}, u32[]{:S(2)}) copy-start(bf16[128,8192]{1,0:T(8,128)(2,1)} %act.1) | copy-start | bytes 6291460
  49.9 54.2 %all-to-all-start.1 = ((bf16[8,16,8192]{2,1,0:T(8,128)(2,1)}), bf16[8,16,8192]{2,1,0:T(8,128)(2,1)}, u32[]{:S(2)}, u32[]{:S(2)}) async-start(bf16[8,16,8192]{2,1,0:T(8,128)(2,1)} %broadcast_in_dim.42), calls=%async_computation.1 | async-start | bytes 4194304 | tf_op jit(solution)/shard_map/all_to_all | solution.py:238
  99.1 7.9 %collective-permute-start = (bf16[4096,384]{1,0:T(8,128)(2,1)}, bf16[4096,384]{1,0:T(8,128)(2,1)}, u32[]{:S(2)}, u32[]{:S(2)}) collective-permute-start(bf16[4096,384]{1,0:T(8,128)(2,1)} %bitcast.14), channel_id=1, source_target_pairs={{0,8},{8,0},{1,9},{9,1},{2,10},{10,2},{3,11},{11,3},{4,12},{12,4},... | collective-permute-start | bytes 9437192 | tf_op jit(solution)/shard_map/ppermute | solution.py:243
  115.1 5.8 %copy-start.4 = (f32[8,128]{1,0:T(8,128)S(1)}, f32[8,128]{1,0:T(8,128)}, u32[]{:S(2)}) copy-start(f32[8,128]{1,0:T(8,128)} %get-tuple-element.12) | copy-start | bytes 12292
  115.2 40.5 %copy-start.1 = (s32[3]{0:T(128)S(1)}, s32[3]{0:T(128)}, u32[]{:S(2)}) copy-start(s32[3]{0:T(128)} %pad_add_fusion.place) | copy-start | bytes 40
  115.2 30.8 %all-to-all-start.2 = ((bf16[8,1024,128]{2,1,0:T(8,128)(2,1)}), bf16[8,1024,128]{2,1,0:T(8,128)(2,1)}, u32[]{:S(2)}, u32[]{:S(2)}) async-start(bf16[8,1024,128]{2,1,0:T(8,128)(2,1)} %get-tuple-element.13), calls=%async_computation.2 | async-start | bytes 4194304 | tf_op jit(solution)/shard_map/all_to_all | solution.py:245
  120.9 3.0 %collective-permute-start.1 = (f32[8,128]{1,0:T(8,128)S(1)}, f32[8,128]{1,0:T(8,128)S(1)}, u32[]{:S(2)}, u32[]{:S(2)}) collective-permute-start(f32[8,128]{1,0:T(8,128)S(1)} %copy-done.4), channel_id=1, source_target_pairs={{0,8},{8,0},{1,9},{9,1},{2,10},{10,2},{3,11},{11,3},{4,12},{12,4},... | collective-permute-start | bytes 12296 | tf_op jit(solution)/shard_map/ppermute | solution.py:208
  123.9 5.5 %collective-permute-start.2 = (f32[8,128]{1,0:T(8,128)S(1)}, f32[8,128]{1,0:T(8,128)S(1)}, u32[]{:S(2)}, u32[]{:S(2)}) collective-permute-start(f32[8,128]{1,0:T(8,128)S(1)} %add.58), channel_id=1, source_target_pairs={{0,64},{64,0},{128,192},{192,128},{256,320},{320,256},{384,448},{4... | collective-permute-start | bytes 12296 | tf_op jit(solution)/shard_map/ppermute | solution.py:208
  129.4 6.4 %collective-permute-start.3 = (f32[8,128]{1,0:T(8,128)S(1)}, f32[8,128]{1,0:T(8,128)S(1)}, u32[]{:S(2)}, u32[]{:S(2)}) collective-permute-start(f32[8,128]{1,0:T(8,128)S(1)} %add.59), channel_id=1, source_target_pairs={{0,128},{64,192},{128,0},{192,64},{256,384},{320,448},{384,256},{4... | collective-permute-start | bytes 12296 | tf_op jit(solution)/shard_map/ppermute | solution.py:208
  135.8 9.4 %collective-permute-start.4 = (f32[8,128]{1,0:T(8,128)S(1)}, f32[8,128]{1,0:T(8,128)S(1)}, u32[]{:S(2)}, u32[]{:S(2)}) collective-permute-start(f32[8,128]{1,0:T(8,128)S(1)} %add.60), channel_id=1, source_target_pairs={{0,256},{64,320},{128,384},{192,448},{256,0},{320,64},{384,128},{4... | collective-permute-start | bytes 12296 | tf_op jit(solution)/shard_map/ppermute | solution.py:208
  146.6 16.9 %all-to-all-start.3 = ((f32[32,1,128]{2,1,0:T(1,128)}), f32[32,1,128]{2,1,0:T(1,128)S(1)}, u32[]{:S(2)}, u32[]{:S(2)}) async-start(f32[32,1,128]{2,1,0:T(1,128)} %broadcast_in_dim.45), calls=%async_computation.3 | async-start | bytes 32768 | tf_op jit(solution)/shard_map/all_to_all | solution.py:249
Sparse Core Ops, SparseCore 0:
  48.4 50.6 all-gather.3

commit v5 on v4

v5 whole, which is shorter than its diff:
```python
import functools
import math

import jax
import jax.numpy as jnp
from jax import lax
from jax.experimental import pallas as pl
from jax.experimental.pallas import tpu as pltpu
from jax.sharding import Mesh
from jax.sharding import PartitionSpec as P

BLOCK = 128
Z, YH, CORE, YL, X = 8, 4, 2, 2, 4
DP = ("z", "yh", "core")
TENSOR = ("yl", "x")
SHARDS = YL * X
BF, F32 = jnp.bfloat16, jnp.float32
NT = (((1,), (1,)), ((), ()))


def pack_kernel(me, kept, counts, g0, g1, u0, u1, d0, d1, out):
    first = jnp.int32(0)
    for shard in range(SHARDS):
        first += jnp.where(shard < me[0], counts[shard], 0)
    slots = [
        jnp.concatenate([gate[...], up[...], down[...].T], axis=1)
        for gate, up, down in ((g0, u0, d0), (g1, u1, d1))
    ]
    for dest in range(SHARDS):
        out[dest] = jnp.where(dest == first + 1, slots[1], slots[0])


def pack(me, kept, counts, gate_w, up_w, down_w):
    rows, units = gate_w.shape

    def block(kept, me, k):
        return jnp.clip(kept[me[0], k], 0, units // BLOCK - 1)

    cols = [pl.BlockSpec((rows, BLOCK), lambda i, m, b, n, k=k: (0, block(b, m, k))) for k in (0, 1)]
    down = [pl.BlockSpec((BLOCK, rows), lambda i, m, b, n, k=k: (block(b, m, k), 0)) for k in (0, 1)]
    shape = (SHARDS, BLOCK, 3 * BLOCK)
    return pl.pallas_call(
        pack_kernel,
        out_shape=jax.ShapeDtypeStruct(shape, BF),
        grid_spec=pltpu.PrefetchScalarGridSpec(
            num_scalar_prefetch=3,
            grid=(1,),
            in_specs=cols + cols + down,
            out_specs=pl.BlockSpec(shape, lambda i, *_: (0, 0, 0)),
        ),
        name="pack_slots",
    )(me, kept, counts, gate_w, gate_w, up_w, up_w, down_w, down_w)


def ffn_kernel(scale, normed, cot, gain, weights, out, unit_out, n_buf, c_buf, w_buf, sems):
    chunk = normed.shape[1] // Z
    copies = []
    for i in range(Z):
        part = pl.ds(i * chunk, chunk)
        views = ((normed, n_buf, (slice(None), part)), (cot, c_buf, (slice(None), part)), (weights, w_buf, (part, slice(None))))
        for j, (source, target, at) in enumerate(views):
            one = pltpu.make_async_copy(source.at[at], target.at[at], sems.at[3 * i + j])
            one.start()
            copies.append(one)
    tokens = normed.shape[0]
    gate_up = jnp.zeros((tokens, 2 * BLOCK), F32)
    hidden = jnp.zeros((tokens, BLOCK), F32)
    rows = [
        [((z * CORE + core) * YH + yh) * BLOCK for core in range(CORE)]
        for z in range(Z) for yh in range(YH)
    ]
    wide = CORE * BLOCK
    for i, pair in enumerate(rows):
        if i % YH == 0:
            for one in copies[3 * (i // YH) : 3 * (i // YH) + 3]:
                one.wait()
        w2 = jnp.concatenate([w_buf[row : row + BLOCK, :] for row in pair], axis=0)
        gate_up += jnp.dot(n_buf[:, i * wide : (i + 1) * wide], w2[:, : 2 * BLOCK], preferred_element_type=F32)
        hidden += jnp.dot(c_buf[:, i * wide : (i + 1) * wide], w2[:, 2 * BLOCK :], preferred_element_type=F32)
    gate, up = gate_up[:, :BLOCK], gate_up[:, BLOCK:]
    sig = jax.nn.sigmoid(gate)
    unit = jnp.sum(gate * sig * up * hidden, axis=0, keepdims=True) * scale
    unit_out[...] = jnp.broadcast_to(unit, unit_out.shape)
    masked = hidden * gain[0:1, :].astype(F32)
    gate_grad = (masked * up * sig * (1.0 + gate * (1.0 - sig))).astype(BF)
    up_grad = (masked * gate * sig).astype(BF)
    grads = jnp.concatenate([gate_grad, up_grad], axis=1)
    share = tokens // SHARDS
    for i, pair in enumerate(rows):
        w2 = jnp.concatenate([w_buf[row : row + BLOCK, : 2 * BLOCK] for row in pair], axis=0)
        part = lax.dot_general(grads, w2, NT, preferred_element_type=F32).astype(BF)
        for core in range(CORE):
            block = part[:, core * BLOCK : (core + 1) * BLOCK].reshape(SHARDS, share, BLOCK)
            first = (i * CORE + core) * share
            out[:, first : first + share, :] = block


def ffn(normed, cot, gain, weights):
    tokens, width = normed.shape
    rows = width // BLOCK * (tokens // SHARDS)
    vmem = pl.BlockSpec(memory_space=pltpu.VMEM)
    anyw = pl.BlockSpec(memory_space=pl.ANY)
    scale = 1.0 / math.sqrt(tokens * Z * YH * CORE)
    buffers = [pltpu.VMEM(x.shape, BF) for x in (normed, cot, weights)]
    return pl.pallas_call(
        functools.partial(ffn_kernel, scale),
        out_shape=(
            jax.ShapeDtypeStruct((SHARDS, rows, BLOCK), BF),
            jax.ShapeDtypeStruct((8, BLOCK), F32),
        ),
        in_specs=[anyw, anyw, vmem, anyw],
        out_specs=(vmem, vmem),
        scratch_shapes=buffers + [pltpu.SemaphoreType.DMA((3 * Z,))],
        compiler_params=pltpu.CompilerParams(vmem_limit_bytes=56 << 20),
        name="pruned_ffn",
    )(normed, cot, gain, weights)


def final_kernel(place, act, gain, parts, grad):
    share, width = act.shape
    x = act[...].astype(F32)
    inv = lax.rsqrt(jnp.mean(x * x, axis=-1, keepdims=True) + 1e-05)
    dnormed = []
    for j in range(width // BLOCK):
        total = parts[0, j * share : (j + 1) * share, :].astype(F32)
        for src in range(1, SHARDS):
            total += parts[src, j * share : (j + 1) * share, :].astype(F32)
        dnormed.append(total)
    scaled = jnp.concatenate(dnormed, axis=1) * gain[...].astype(F32)
    normalized = x * inv
    mean = jnp.mean(scaled * normalized, axis=-1, keepdims=True)
    grad[...] = (inv * (scaled - normalized * mean)).astype(BF)


def final(place, act, gain, parts):
    tokens, width = act.shape
    share = tokens // SHARDS
    return pl.pallas_call(
        final_kernel,
        out_shape=jax.ShapeDtypeStruct((share, width), BF),
        grid_spec=pltpu.PrefetchScalarGridSpec(
            num_scalar_prefetch=1,
            grid=(1,),
            in_specs=[
                pl.BlockSpec((share, width), lambda i, p: (p[0], 0)),
                pl.BlockSpec((1, width), lambda i, p: (0, 0)),
                pl.BlockSpec(parts.shape, lambda i, p: (0, 0, 0)),
            ],
            out_specs=pl.BlockSpec((share, width), lambda i, p: (0, 0)),
        ),
        compiler_params=pltpu.CompilerParams(vmem_limit_bytes=12 << 20),
        name="input_grad",
    )(place, act, gain.reshape(1, -1), parts)


def per_device(
    activations, norm_gain, gate_w, up_w, down_w, mask_gain, kept_blocks, kept_counts, cotangent
):
    me = lax.axis_index(TENSOR)
    shards, k = jnp.arange(SHARDS), jnp.arange(2)
    blocks = mask_gain.shape[0] // BLOCK
    sent = pack(me.reshape(1), kept_blocks, kept_counts, gate_w, up_w, down_w)
    got = lax.all_to_all(sent, TENSOR, split_axis=0, concat_axis=0, tiled=True)
    ends = jnp.cumsum(kept_counts)
    source = jnp.minimum(jnp.sum((ends <= me).astype(jnp.int32)), SHARDS - 1)
    slot = lax.dynamic_index_in_dim(got, source, 0, keepdims=False)
    column = lax.all_gather(slot, "yh", axis=0, tiled=True)
    weights = lax.all_gather(column, ("z", "core"), axis=0, tiled=True)

    late, _ = lax.optimization_barrier(((cotangent, activations, mask_gain, kept_blocks, kept_counts), column))
    cotangent, act, mask_gain, kept_blocks, kept_counts = late
    kept = jnp.clip(kept_blocks[me], 0, blocks - 1)
    first = jnp.sum(jnp.where(shards < me, kept_counts, 0))
    copies = jnp.broadcast_to(cotangent[None], (SHARDS,) + cotangent.shape)
    cot = lax.all_to_all(copies, TENSOR, split_axis=0, concat_axis=0, tiled=True)
    cot = cot.reshape(-1, cotangent.shape[1])
    act = act.astype(F32)
    inv_rms = lax.rsqrt(jnp.mean(act * act, axis=-1, keepdims=True) + 1e-05)
    normed = (act * inv_rms * norm_gain.astype(F32)).astype(BF)
    gains = jnp.take(mask_gain.reshape(blocks, BLOCK), kept, axis=0)
    gains = lax.all_gather(gains, TENSOR, axis=0, tiled=True)
    which = me - jnp.sum(jnp.where(shards == source, ends - kept_counts, 0))
    unit_gain = lax.dynamic_slice_in_dim(gains, source * 2 + jnp.clip(which, 0, 1), 1, 0)

    parts, unit = ffn(normed, cot, unit_gain, weights)
    got = lax.all_to_all(parts, TENSOR, split_axis=0, concat_axis=0, tiled=True)
    unit = unit + lax.ppermute(unit, "core", [(0, 1), (1, 0)])
    unit = jnp.sum(lax.all_gather(unit[:1], "z", axis=0, tiled=True), axis=0)
    unit, got = lax.optimization_barrier((unit, got))
    copies = jnp.broadcast_to(unit[None, None], (YH * SHARDS, 1, BLOCK))
    units = lax.all_to_all(copies, ("yh",) + TENSOR, split_axis=0, concat_axis=0, tiled=True)
    input_grad = final(me.reshape(1), activations, norm_gain, got)
    width = BLOCK // (Z * YH * CORE)
    units = lax.dynamic_slice_in_dim(units.reshape(YH * SHARDS, BLOCK), lax.axis_index(DP) * width, width, 1)
    count = kept_counts[me]
    owner = jnp.tile(shards, YH)
    wanted = (owner[None] == first + k[:, None]) & (k < count)[:, None]
    gain_grad = jnp.sum(jnp.where(wanted[:, :, None], units[None], 0.0), axis=1)
    return input_grad, gain_grad


def solution(mesh):
    fine = Mesh(mesh.devices.reshape(Z, YH, CORE, YL, X), DP + TENSOR)
    placed = (
        P(DP, None),
        P(),
        P(DP, TENSOR),
        P(DP, TENSOR),
        P(TENSOR, DP),
        P(TENSOR),
        P(),
        P(),
        P(DP + TENSOR, None),
    )
    return jax.shard_map(
        per_device,
        mesh=fine,
        in_specs=placed,
        out_specs=(P(DP + TENSOR, None), P(TENSOR, DP)),
        check_vma=False,
    )
```

time: 173 us -> 162 us (0.936)
  blocking collectives: 17.6 us -> 59.7 us
  waiting for transfers between devices: 65.2 us -> 29 us
  starting transfers between devices: 44.5 us -> 31.8 us
  between operations: 17.5 us -> 15.5 us
    all_gather x1 -> x3, blocking collectives: 17.6 us -> 59.7 us  [the longest x1 27.8 us: per_device(): gains = lax.all_gather(gains, TENSOR, axis=0, tiled=True)]
    all_gather x1, waiting for transfers between devices: 43.6 us -> 11.5 us  [per_device(): weights = lax.all_gather(column, ('z', 'core'), axis=0, tiled=True)]
    ppermute x5 -> x1, starting transfers between devices: 15 us -> 1.92 us  [per_device(): unit = unit + lax.ppermute(unit, 'core', [(0, 1), (1, 0)])]
    ppermute x5 -> x1, waiting for transfers between devices: 10.8 us -> 0.36 us  [per_device(): unit = unit + lax.ppermute(unit, 'core', [(0, 1), (1, 0)])]
    all_to_all x1, waiting for transfers between devices: 0.77 us -> 6.1 us  [per_device(): got = lax.all_to_all(parts, TENSOR, split_axis=0, concat_axis=0, tiled=True)]
  transfers between devices with their start and end apart: 10 -> 6, of which waited for: 9 -> 5; matrix products, arithmetic and copies ran while one was open for 4% -> 6% of each run, Pallas kernels for 2% -> 2%
where the time goes in v5:
time: 162 us; the launch traced here: 161 us
  blocking collectives  59.7 us (37%)
  starting transfers between devices  31.8 us (20%)
  waiting for transfers between devices  29 us (18%)
  between operations  15.5 us (10%)
  Pallas kernels  13.4 us (8%)
  other arithmetic  6.24 us (4%)
  local copies, waits for them, and re-layouts  5.52 us (3%)
    all_gather x1, blocking collectives, per_device(): gains = lax.all_gather(gains, TENSOR, axis=0, tiled=True)  27.8 us
    all_gather x1, blocking collectives, per_device(): column = lax.all_gather(slot, 'yh', axis=0, tiled=True)  17.1 us
    all_gather x1, blocking collectives, per_device(): unit = jnp.sum(lax.all_gather(unit[:1], 'z', axis=0, tiled=True), axis=0)  14.8 us
    all_gather x1, waiting for transfers between devices, per_device(): weights = lax.all_gather(column, ('z', 'core'), axis=0, tiled=True)  11.5 us
    all_to_all x1, starting transfers between devices, per_device(): got = lax.all_to_all(sent, TENSOR, split_axis=0, concat_axis=0, tiled=True)  9.44 us
    all_to_all x1, starting transfers between devices, per_device(): lax.all_to_all(copies, ('yh',) + TENSOR, split_axis=0, concat_axis=0, til...  8.92 us
    pallas_call x1, Pallas kernels, ffn(): pl.pallas_call(functools.partial(ffn_kernel, scale), out_shape=(jax.Shape...  7.9 us
    all_to_all x1, waiting for transfers between devices, per_device(): got = lax.all_to_all(parts, TENSOR, split_axis=0, concat_axis=0, tiled=True)  6.1 us
  transfers between devices with their start and end apart: 6, of which 5 were waited for; matrix products, arithmetic and copies ran while one was open for 6% of the time, Pallas kernels for 2%

profile of v5, /device:TPU:6, one launch (start us, length us, event | category | flops | bytes accessed | tf_op | source)
XLA Modules:
  0.0 161.2 jit_solution(2608141032569284248)
XLA Ops:
  7.2 1.3 copy.16.kept
  8.5 2.7 %pack_slots.1 = bf16[8,128,384]{2,1,0:T(8,128)(2,1)} custom-call(s32[1]{0:T(128)} %bitcast.me.place, s32[8,2]{1,0:T(8,128)} %copy.16.kept, s32[8]{0:T(128)} %counts.1, bf16[128,1792]{1,0:T(8,128)(2,1)} %g1.1, bf16[128,1792]{1,0:T(8,128)(2,1)} %g1.1, bf16[128,1792]{1,0:T(8,128)(2,1)} %u1_.1, bf16[128,1792]{1,0:T(8,128)(2,1)} %u1_.1, bf16[1792,128]{1,0:T(8,128)(2,1)} %d1.1, ...), custom_call_target="tpu_custom_call" | custom-call | tf_op jit(solution)/shard_map/pack_slots/pallas_call | solution.py:42
  11.2 9.4 %all-to-all-start = ((bf16[8,128,384]{2,1,0:T(8,128)(2,1)}), bf16[8,128,384]{2,1,0:T(8,128)(2,1)S(1)}, u32[]{:S(2)}, u32[]{:S(2)}) async-start(bf16[8,128,384]{2,1,0:T(8,128)(2,1)} %pack_slots.1), calls=%async_computation | async-start | bytes 1572864 | tf_op jit(solution)/shard_map/all_to_all | solution.py:163
  20.7 0.2 reduce-window.9
  20.9 0.6 fusion.3
  22.1 6.1 %all-to-all-done = bf16[8,128,384]{2,1,0:T(8,128)(2,1)S(1)} async-done(((bf16[8,128,384]{2,1,0:T(8,128)(2,1)}), bf16[8,128,384]{2,1,0:T(8,128)(2,1)S(1)}, u32[]{:S(2)}, u32[]{:S(2)}) %all-to-all-start) | async-done | bytes 786464 | tf_op jit(solution)/shard_map/all_to_all | solution.py:163
  28.3 17.1 %all-gather = bf16[1,512,384]{2,1,0:T(8,128)(2,1)} all-gather(bf16[1,128,384]{2,1,0:T(8,128)(2,1)S(1)} %constant_dynamic-slice_fusion.2), channel_id=2, replica_groups=mesh['z'=8,'yh'=4,'core'=2,'yl'=2,'x'=4] {'yh'}, dimensions={1}, use_global_device_ids=true | all-gather | bytes 491520 | tf_op jit(solution)/shard_map/all_gather | solution.py:167
  45.4 1.5 broadcast_in_dim.55
  46.9 5.8 %all-to-all-start.1 = ((bf16[8,16,8192]{2,1,0:T(8,128)(2,1)}), bf16[8,16,8192]{2,1,0:T(8,128)(2,1)}, u32[]{:S(2)}, u32[]{:S(2)}) async-start(bf16[8,16,8192]{2,1,0:T(8,128)(2,1)} %broadcast_in_dim.55), calls=%async_computation.1 | async-start | bytes 4194304 | tf_op jit(solution)/shard_map/all_to_all | solution.py:175
  52.7 0.7 fusion.5
  54.1 0.2 clamp_reduce_fusion
  54.3 0.6 gather_fusion
  54.9 27.8 %all-gather.2 = bf16[8,2,128]{2,1,0:T(2,128)(2,1)S(1)} all-gather(bf16[1,2,128]{2,1,0:T(2,128)(2,1)S(1)} %fusion.7), channel_id=1, replica_groups=mesh['z'=8,'yh'=4,'core'=2,'yl'=2,'x'=4] {'yl','x'}, dimensions={0}, use_global_device_ids=true | all-gather | bytes 4608 | tf_op jit(solution)/shard_map/all_gather | solution.py:181
  82.8 0.5 constant_dynamic-slice_fusion.1.gain
  83.3 0.5 fusion
  83.8 1.9 %fusion.2.normed = bf16[128,8192]{1,0:T(8,128)(2,1)} fusion(bf16[128,8192]{1,0:T(8,128)(2,1)S(1)} %copy-done.1, f32[8192]{0:T(1024)S(1)} %convert_element_type.14, f32[128]{0:T(128)S(1)} %add_rsqrt_fusion), kind=kLoop, calls=%fused_computation.5 | loop fusion | flops 4194304 | bytes 4227584 | tf_op jit(solution)/shard_map/convert_element_type | solution.py:179
  85.7 11.5 %all-gather.6.cloned.1.call-done = bf16[1,8192,384]{2,1,0:T(8,128)(2,1)} async-done(((bf16[1,512,384]{2,1,0:T(8,128)(2,1)}), bf16[1,8192,384]{2,1,0:T(8,128)(2,1)}) %all-gather.6.cloned.1.call-update) | async-done | bytes 6291472 | tf_op jit(solution)/shard_map/all_gather | solution.py:168
  97.2 7.9 %pruned_ffn.1 = (bf16[8,1024,128]{2,1,0:T(8,128)(2,1)}, f32[8,128]{1,0:T(8,128)}) custom-call(bf16[128,8192]{1,0:T(8,128)(2,1)} %fusion.2.normed, bf16[128,8192]{1,0:T(8,128)(2,1)} %bitcast.1.cot, bf16[1,128]{1,0:T(2,128)(2,1)} %constant_dynamic-slice_fusion.1.gain, bf16[8192,384]{1,0:T(8,128)(2,1)} %bitcast.22), custom_call_target="tpu_custom_call" | custom-call | tf_op jit(solution)/shard_map/pruned_ffn/pallas_call | solution.py:105
  105.1 5.7 %all-to-all-start.2 = ((bf16[8,1024,128]{2,1,0:T(8,128)(2,1)}), bf16[8,1024,128]{2,1,0:T(8,128)(2,1)}, u32[]{:S(2)}, u32[]{:S(2)}) async-start(bf16[8,1024,128]{2,1,0:T(8,128)(2,1)} %get-tuple-element.17), calls=%async_computation.2 | async-start | bytes 4194304 | tf_op jit(solution)/shard_map/all_to_all | solution.py:186
  110.8 0.6 dynamic_slice.19
  111.4 0.6 iota_compare_fusion
  112.0 1.9 %collective-permute-start = (f32[8,128]{1,0:T(8,128)S(1)}, f32[8,128]{1,0:T(8,128)S(1)}, u32[]{:S(2)}, u32[]{:S(2)}) collective-permute-start(f32[8,128]{1,0:T(8,128)S(1)} %copy-done.4), channel_id=1, source_target_pairs={{0,8},{8,0},{1,9},{9,1},{2,10},{10,2},{3,11},{11,3},{4,12},{12,4},... | collective-permute-start | bytes 12296 | tf_op jit(solution)/shard_map/ppermute | solution.py:187
  114.0 0.7 iota_add_fusion
  114.7 0.4 collective-permute-done
  115.1 14.8 %all-gather.3 = f32[8,1,128]{2,1,0:T(1,128)S(1)} all-gather(f32[1,1,128]{2,1,0:T(1,128)S(1)} %slice_bitcast_fusion), channel_id=1, replica_groups=mesh['z'=8,'yh'=4,'core'=2,'yl'=2,'x'=4] {'z'}, dimensions={0}, use_global_device_ids=true | all-gather | bytes 4608 | tf_op jit(solution)/shard_map/all_gather | solution.py:188
  129.9 6.1 %all-to-all-done.2.parts = bf16[8,1024,128]{2,1,0:T(8,128)(2,1)} async-done(((bf16[8,1024,128]{2,1,0:T(8,128)(2,1)}), bf16[8,1024,128]{2,1,0:T(8,128)(2,1)}, u32[]{:S(2)}, u32[]{:S(2)}) %all-to-all-start.2) | async-done | bytes 2097184 | tf_op jit(solution)/shard_map/all_to_all | solution.py:186
  136.0 0.6 broadcast_in_dim.60
  136.6 8.9 %all-to-all-start.3 = ((f32[32,1,128]{2,1,0:T(1,128)}), f32[32,1,128]{2,1,0:T(1,128)S(1)}, u32[]{:S(2)}, u32[]{:S(2)}) async-start(f32[32,1,128]{2,1,0:T(1,128)} %broadcast_in_dim.60), calls=%async_computation.3 | async-start | bytes 32768 | tf_op jit(solution)/shard_map/all_to_all | solution.py:191
  145.7 2.9 %input_grad.1 = bf16[16,8192]{1,0:T(8,128)(2,1)} custom-call(s32[1]{0:T(128)} %bitcast.me.place, bf16[128,8192]{1,0:T(8,128)(2,1)S(1)} %copy-done.1, bf16[1,8192]{1,0:T(2,128)(2,1)S(1)} %reshape.145.gain, bf16[8,1024,128]{2,1,0:T(8,128)(2,1)} %all-to-all-done.2.parts), custom_call_target="tpu_custom_call" | custom-call | tf_op jit(solution)/shard_map/input_grad/pallas_call | solution.py:138
  148.5 5.0 %all-to-all-done.3 = f32[32,1,128]{2,1,0:T(1,128)S(1)} async-done(((f32[32,1,128]{2,1,0:T(1,128)}), f32[32,1,128]{2,1,0:T(1,128)S(1)}, u32[]{:S(2)}, u32[]{:S(2)}) %all-to-all-start.3) | async-done | bytes 16416 | tf_op jit(solution)/shard_map/all_to_all | solution.py:191
  153.5 0.1 constant_dynamic-slice_fusion
  153.7 0.7 select_reduce_fusion
  (32 shorter events, 0.5 us)
Async XLA Ops:
  7.2 47.1 %copy-start = (bf16[1792]{0:T(1024)(128)(2,1)S(1)}, bf16[1792]{0:T(1024)(128)(2,1)}, u32[]{:S(2)}) copy-start(bf16[1792]{0:T(1024)(128)(2,1)} %param.14) | copy-start | bytes 10756
  8.5 12.1 %copy-start.6 = (s32[8]{0:T(128)S(1)}, s32[8]{0:T(128)}, u32[]{:S(2)}) copy-start(s32[8]{0:T(128)} %counts.1) | copy-start | bytes 100
  11.2 34.1 %copy-start.2 = (bf16[16,8192]{1,0:T(8,128)(2,1)S(1)}, bf16[16,8192]{1,0:T(8,128)(2,1)}, u32[]{:S(2)}) copy-start(bf16[16,8192]{1,0:T(8,128)(2,1)} %param.17) | copy-start | bytes 786436
  11.2 17.0 %all-to-all-start = ((bf16[8,128,384]{2,1,0:T(8,128)(2,1)}), bf16[8,128,384]{2,1,0:T(8,128)(2,1)S(1)}, u32[]{:S(2)}, u32[]{:S(2)}) async-start(bf16[8,128,384]{2,1,0:T(8,128)(2,1)} %pack_slots.1), calls=%async_computation | async-start | bytes 1572864 | tf_op jit(solution)/shard_map/all_to_all | solution.py:163
  20.7 76.5 %all-gather.6.cloned.1.call-start = ((), (), s32[]{:S(2)}) async-start(), calls=%async_computation.4 | async-start | bytes 6684672 | tf_op jit(solution)/shard_map/all_gather | solution.py:168
  46.9 7.1 %copy-start.3 = (bf16[8192]{0:T(1024)(128)(2,1)S(1)}, bf16[8192]{0:T(1024)(128)(2,1)}, u32[]{:S(2)}) copy-start(bf16[8192]{0:T(1024)(128)(2,1)} %param.10) | copy-start | bytes 49156
  46.9 7.1 %copy-start.5 = (s32[8,2]{0,1:T(2,128)S(1)}, s32[8,2]{0,1:T(2,128)}, u32[]{:S(2)}) copy-start(s32[8,2]{0,1:T(2,128)} %param.15) | copy-start | bytes 196
  46.9 36.4 %copy-start.1 = (bf16[128,8192]{1,0:T(8,128)(2,1)S(1)}, bf16[128,8192]{1,0:T(8,128)(2,1)}, u32[]{:S(2)}) copy-start(bf16[128,8192]{1,0:T(8,128)(2,1)} %act.1) | copy-start | bytes 6291460
  46.9 38.8 %all-to-all-start.1 = ((bf16[8,16,8192]{2,1,0:T(8,128)(2,1)}), bf16[8,16,8192]{2,1,0:T(8,128)(2,1)}, u32[]{:S(2)}, u32[]{:S(2)}) async-start(bf16[8,16,8192]{2,1,0:T(8,128)(2,1)} %broadcast_in_dim.55), calls=%async_computation.1 | async-start | bytes 4194304 | tf_op jit(solution)/shard_map/all_to_all | solution.py:175
  105.1 6.9 %copy-start.4 = (f32[8,128]{1,0:T(8,128)S(1)}, f32[8,128]{1,0:T(8,128)}, u32[]{:S(2)}) copy-start(f32[8,128]{1,0:T(8,128)} %get-tuple-element.16) | copy-start | bytes 12292
  105.1 30.9 %all-to-all-start.2 = ((bf16[8,1024,128]{2,1,0:T(8,128)(2,1)}), bf16[8,1024,128]{2,1,0:T(8,128)(2,1)}, u32[]{:S(2)}, u32[]{:S(2)}) async-start(bf16[8,1024,128]{2,1,0:T(8,128)(2,1)} %get-tuple-element.17), calls=%async_computation.2 | async-start | bytes 4194304 | tf_op jit(solution)/shard_map/all_to_all | solution.py:186
  112.0 3.1 %collective-permute-start = (f32[8,128]{1,0:T(8,128)S(1)}, f32[8,128]{1,0:T(8,128)S(1)}, u32[]{:S(2)}, u32[]{:S(2)}) collective-permute-start(f32[8,128]{1,0:T(8,128)S(1)} %copy-done.4), channel_id=1, source_target_pairs={{0,8},{8,0},{1,9},{9,1},{2,10},{10,2},{3,11},{11,3},{4,12},{12,4},... | collective-permute-start | bytes 12296 | tf_op jit(solution)/shard_map/ppermute | solution.py:187
  136.6 16.9 %all-to-all-start.3 = ((f32[32,1,128]{2,1,0:T(1,128)}), f32[32,1,128]{2,1,0:T(1,128)S(1)}, u32[]{:S(2)}, u32[]{:S(2)}) async-start(f32[32,1,128]{2,1,0:T(1,128)} %broadcast_in_dim.60), calls=%async_computation.3 | async-start | bytes 32768 | tf_op jit(solution)/shard_map/all_to_all | solution.py:191
Sparse Core Ops, SparseCore 0:
  45.5 51.6 all-gather.5

commit v6 on v2

--- a/solution.py
+++ b/solution.py
@@ -16,19 +16,13 @@
 SHARDS = YL * X
 BF, F32 = jnp.bfloat16, jnp.float32
 EXTRA = 16
-UNITS = (8,)
 NT = (((1,), (1,)), ((), ()))
 
 
-def first_slot(counts_ref, shard):
-    total = jnp.int32(0)
-    for other in range(SHARDS):
-        total += jnp.where(other < shard, counts_ref[other], 0)
-    return total
-
-
-def pack_kernel(place, kept, counts, g0, g1, u0, u1, d0, d1, m0, m1, out):
-    first = first_slot(counts, place[0])
+def pack_kernel(me, kept, counts, g0, g1, u0, u1, d0, d1, m0, m1, out):
+    first = jnp.int32(0)
+    for shard in range(SHARDS):
+        first += jnp.where(shard < me[0], counts[shard], 0)
     slots = []
     for gate, up, down, gain in ((g0, u0, d0, m0), (g1, u1, d1, m1)):
         body = jnp.concatenate([gate[...], up[...], down[...].T], axis=1)
@@ -40,26 +34,16 @@
         out[dest, BLOCK:, :] = jnp.where(second, slots[1][1], slots[0][1])
 
 
-def pack(place, kept, counts, gate_w, up_w, down_w, mask_gain):
+def pack(me, kept, counts, gate_w, up_w, down_w, mask_gain):
     rows, units = gate_w.shape
-    blocks = units // BLOCK
-
-    def pick(k, kept, place):
-        return jnp.clip(kept[place[0], k], 0, blocks - 1)
-
-    cols = [
-        pl.BlockSpec((rows, BLOCK), lambda i, p, b, n, k=k: (0, pick(k, b, p)))
-        for k in (0, 1)
-    ]
-    down = [
-        pl.BlockSpec((BLOCK, rows), lambda i, p, b, n, k=k: (pick(k, b, p), 0))
-        for k in (0, 1)
-    ]
-    gain = [
-        pl.BlockSpec((1, 1, BLOCK), lambda i, p, b, n, k=k: (pick(k, b, p), 0, 0))
-        for k in (0, 1)
-    ]
-    gains = mask_gain.reshape(blocks, 1, BLOCK)
+
+    def block(kept, me, k):
+        return jnp.clip(kept[me[0], k], 0, units // BLOCK - 1)
+
+    cols = [pl.BlockSpec((rows, BLOCK), lambda i, m, b, n, k=k: (0, block(b, m, k))) for k in (0, 1)]
+    down = [pl.BlockSpec((BLOCK, rows), lambda i, m, b, n, k=k: (block(b, m, k), 0)) for k in (0, 1)]
+    gain = [pl.BlockSpec((1, 1, BLOCK), lambda i, m, b, n, k=k: (block(b, m, k), 0, 0)) for k in (0, 1)]
+    gains = mask_gain.reshape(units // BLOCK, 1, BLOCK)
     shape = (SHARDS, BLOCK + EXTRA, 3 * BLOCK)
     return pl.pallas_call(
         pack_kernel,
@@ -71,7 +55,7 @@
             out_specs=pl.BlockSpec(shape, lambda i, *_: (0, 0, 0)),
         ),
         name="pack_slots",
-    )(place, kept, counts, gate_w, gate_w, up_w, up_w, down_w, down_w, gains, gains)
+    )(me, kept, counts, gate_w, gate_w, up_w, up_w, down_w, down_w, gains, gains)
 
 
 def ffn_kernel(scale, layout, place, normed, cot, gain, *refs):
@@ -81,7 +65,7 @@
     n_buf, c_buf = refs[2 * count + 2 : 2 * count + 4]
     a_buf, b_buf = refs[2 * count + 4 : 3 * count + 4], refs[3 * count + 4 : 4 * count + 4]
     sems = refs[-1]
-    z, core = place[1], place[2]
+    z, core = place[0], place[1]
     copies, work = [], []
 
     def copy(source, target):
@@ -104,7 +88,7 @@
                 copy(mine[i].at[rows, :], a_buf[i].at[rows, :]),
                 copy(theirs[i].at[rows, :], b_buf[i].at[rows, :]),
             ]
-            zz = shift[0] if isinstance(shift, tuple) else lax.rem(z + shift + Z, Z)
+            zz = lax.rem(z + shift + Z, Z)
             for k in range(length):
                 at = (zz * YH + yh0 + k) * (CORE * BLOCK)
                 near = pl.multiple_of(at + core * BLOCK, BLOCK)
@@ -152,7 +136,7 @@
         functools.partial(ffn_kernel, scale, layout),
         out_shape=(
             jax.ShapeDtypeStruct((SHARDS, rows, BLOCK), BF),
-            jax.ShapeDtypeStruct(UNITS + (BLOCK,), F32),
+            jax.ShapeDtypeStruct((8, BLOCK), F32),
         ),
         in_specs=[pl.BlockSpec(memory_space=pltpu.SMEM), anyw, anyw, vmem] + [anyw] * (2 * len(mine)),
         out_specs=(vmem, vmem),
@@ -199,58 +183,58 @@
     )(place, act, gain.reshape(1, -1), parts)
 
 
-def whole(x, yh0):
-    length = x.shape[0] // BLOCK
-    return lax.all_gather(x, "z", axis=0, tiled=True), tuple(((i,), yh0, length) for i in range(Z))
-
-
-def swapped(x, axis, size, distance):
-    return lax.ppermute(x, axis, [(i, i ^ distance) for i in range(size)])
-
-
-def summed_over_dp(x):
-    for axis, size in (("core", CORE), ("yh", YH), ("z", Z)):
-        distance = 1
-        while distance < size:
-            x = x + swapped(x, axis, size, distance)
-            distance *= 2
-    return x
+def ring(x):
+    up = [(i, (i + 1) % Z) for i in range(Z)]
+    down = [(i, (i - 1) % Z) for i in range(Z)]
+    chunks, order, a, b = [x], [(0, 0, YH)], x, x
+    for step in (1, 2, 3):
+        a, b = lax.ppermute(a, "z", up), lax.ppermute(b, "z", down)
+        chunks += [a, b]
+        order += [(-step, 0, YH), (step, 0, YH)]
+    half = x.shape[0] // 2
+    far = [lax.ppermute(a[:half], "z", up), lax.ppermute(b[half:], "z", down)]
+    arrays = [jnp.concatenate(chunks, axis=0), jnp.concatenate(far, axis=0)]
+    return arrays, (tuple(order), ((Z // 2, 0, YH),)), chunks[1]
 
 
 def per_device(
     activations, norm_gain, gate_w, up_w, down_w, mask_gain, kept_blocks, kept_counts, cotangent
 ):
     me = lax.axis_index(TENSOR)
-    place = jnp.stack([me, lax.axis_index("z"), lax.axis_index("core")]).astype(jnp.int32)
-
-    sent = pack(place, kept_blocks, kept_counts, gate_w, up_w, down_w, mask_gain)
+    sent = pack(me.reshape(1), kept_blocks, kept_counts, gate_w, up_w, down_w, mask_gain)
+    copies = jnp.broadcast_to(cotangent[None], (SHARDS,) + cotangent.shape)
     got = lax.all_to_all(sent, TENSOR, split_axis=0, concat_axis=0, tiled=True)
     ends = jnp.cumsum(kept_counts)
-    source = jnp.sum((ends <= me).astype(jnp.int32))
+    source = jnp.minimum(jnp.sum((ends <= me).astype(jnp.int32)), SHARDS - 1)
     slot = lax.dynamic_index_in_dim(got, source, 0, keepdims=False)
     column = lax.all_gather(slot[:BLOCK], "yh", axis=0, tiled=True)
-    weights, order = whole(column, 0)
-
-    cotangent, activations_late, slot, _ = lax.optimization_barrier((cotangent, activations, slot, column))
-    unit_gain = slot[BLOCK:, :BLOCK]
-    wide = jnp.broadcast_to(cotangent[None], (SHARDS,) + cotangent.shape)
-    cot = lax.all_to_all(wide, TENSOR, split_axis=0, concat_axis=0, tiled=True).reshape(-1, cotangent.shape[1])
-    act = activations_late.astype(F32)
+    weights, layout, early = ring(column)
+    others = [lax.ppermute(one, "core", [(0, 1), (1, 0)]) for one in weights]
+
+    late, _ = lax.optimization_barrier(((copies, activations, slot), early))
+    copies, act, slot = late
+    cot = lax.all_to_all(copies, TENSOR, split_axis=0, concat_axis=0, tiled=True)
+    cot = cot.reshape(-1, cotangent.shape[1])
+    act = act.astype(F32)
     inv_rms = lax.rsqrt(jnp.mean(act * act, axis=-1, keepdims=True) + 1e-05)
     normed = (act * inv_rms * norm_gain.astype(F32)).astype(BF)
-
-    other = lax.ppermute(weights, "core", [(0, 1), (1, 0)])
-    parts, unit = ffn(place, normed, cot, unit_gain, (order,), [weights], [other])
+    place = jnp.stack([lax.axis_index("z"), lax.axis_index("core")]).astype(jnp.int32)
+
+    parts, unit = ffn(place, normed, cot, slot[BLOCK:, :BLOCK], layout, weights, others)
     got = lax.all_to_all(parts, TENSOR, split_axis=0, concat_axis=0, tiled=True)
-    input_grad = final(place, activations, norm_gain, got)
-
-    units = lax.all_gather(summed_over_dp(unit)[:1], TENSOR, axis=0, tiled=True)
+    unit = unit + lax.ppermute(unit, "core", [(0, 1), (1, 0)])
+    unit = jnp.sum(lax.all_gather(unit[:1], "z", axis=0, tiled=True), axis=0, keepdims=True)
+    unit = jnp.sum(lax.all_gather(unit, "yh", axis=0, tiled=True), axis=0)
+    unit, got = lax.optimization_barrier((unit, got))
+    wide = jnp.broadcast_to(unit[None, None], (SHARDS, 1, BLOCK))
+    units = lax.all_to_all(wide, TENSOR, split_axis=0, concat_axis=0, tiled=True)
+    input_grad = final(me.reshape(1), activations, norm_gain, got)
     width = BLOCK // (Z * YH * CORE)
+    units = lax.dynamic_slice_in_dim(units.reshape(SHARDS, BLOCK), lax.axis_index(DP) * width, width, 1)
+    shards, k = jnp.arange(SHARDS), jnp.arange(2)
     count = kept_counts[me]
-    slots = ends[me] - count + jnp.arange(2)
-    mine_units = lax.dynamic_slice_in_dim(units, lax.axis_index(DP) * width, width, 1)
-    picked = jnp.take(mine_units, jnp.minimum(slots, SHARDS - 1), axis=0)
-    gain_grad = jnp.where((jnp.arange(2) < count)[:, None], picked, 0.0)
+    wanted = (shards[None] == ends[me] - count + k[:, None]) & (k < count)[:, None]
+    gain_grad = jnp.sum(jnp.where(wanted[:, :, None], units[None], 0.0), axis=1)
     return input_grad, gain_grad
 
 

time: 207 us -> 167 us (0.81)
  waiting for transfers between devices: 78.8 us -> 17.9 us
  starting transfers between devices: 46.6 us -> 66.5 us
  between operations: 17.4 us -> 2.86 us
  blocking collectives: 34.3 us -> 43.3 us
  local copies, waits for them, and re-layouts: 6.65 us -> 15.2 us
    all_gather x1 -> x0, waiting for transfers between devices: 43.6 us -> none  [whole(): lax.all_gather(x, 'z', axis=0, tiled=True)]
    ppermute x7 -> x11, waiting for transfers between devices: 29.7 us -> 10.1 us  [the longest x2 4.76 us: ring(): far = [lax.ppermute(a[:half], 'z', up), lax.ppermute(b[half:], 'z', down)]]
    ppermute x7 -> x11, starting transfers between devices: 26 us -> 40.1 us  [the longest x6 26.9 us: ring(): a, b = (lax.ppermute(a, 'z', up), lax.ppermute(b, 'z', down))]
    all_gather x1 -> x2, blocking collectives: 16.8 us -> 26.6 us  [the longest x1 16.9 us: per_device(): lax.all_gather(unit[:1], 'z', axis=0, tiled=True)]
    unnamed x14 -> x23, local copies, waits for them, and re-layouts: 1.38 us -> 8.86 us
    all_to_all x0 -> x1, starting transfers between devices: none -> 5.69 us  [per_device(): lax.all_to_all(copies, TENSOR, split_axis=0, concat_axis=0, tiled=True)]
  transfers between devices with their start and end apart: 11 -> 15, of which waited for: 9 -> 7; matrix products, arithmetic and copies ran while one was open for 4% -> 10% of each run, Pallas kernels for 0% -> 2%
where the time goes in v6:
time: 167 us; the launch traced here: 165 us
  starting transfers between devices  66.5 us (40%)
  blocking collectives  43.3 us (26%)
  waiting for transfers between devices  17.9 us (11%)
  local copies, waits for them, and re-layouts  15.2 us (9%)
  Pallas kernels  13.8 us (8%)
  other arithmetic  5.27 us (3%)
  between operations  2.86 us (2%)
    ppermute x6, starting transfers between devices, ring(): a, b = (lax.ppermute(a, 'z', up), lax.ppermute(b, 'z', down))  26.9 us
    all_gather x1, blocking collectives, per_device(): lax.all_gather(unit[:1], 'z', axis=0, tiled=True)  16.9 us
    all_gather x1, blocking collectives, per_device(): column = lax.all_gather(slot[:BLOCK], 'yh', axis=0, tiled=True)  16.7 us
    all_gather x1, blocking collectives, per_device(): unit = jnp.sum(lax.all_gather(unit, 'yh', axis=0, tiled=True), axis=0)  9.77 us
    all_to_all x1, starting transfers between devices, per_device(): got = lax.all_to_all(sent, TENSOR, split_axis=0, concat_axis=0, tiled=True)  9.32 us
    unnamed x23, local copies, waits for them, and re-layouts  8.86 us
    pallas_call x1, Pallas kernels, ffn(): pl.pallas_call(functools.partial(ffn_kernel, scale, layout), out_shape=(j...  8.2 us
    ppermute x2, starting transfers between devices, ring(): far = [lax.ppermute(a[:half], 'z', up), lax.ppermute(b[half:], 'z', down)]  7.42 us
  transfers between devices with their start and end apart: 15, of which 7 were waited for; matrix products, arithmetic and copies ran while one was open for 10% of the time, Pallas kernels for 2%

profile of v6, /device:TPU:6, one launch (start us, length us, event | category | flops | bytes accessed | tf_op | source)
XLA Modules:
  0.0 164.9 jit_solution(3956587639565661517)
XLA Ops:
  0.6 1.3 copy.22.kept
  2.0 1.3 copy.23.m0.m1
  3.3 2.8 %pack_slots.1 = bf16[8,144,384]{2,1,0:T(8,128)(2,1)} custom-call(s32[1]{0:T(128)} %bitcast.me.place, s32[8,2]{1,0:T(8,128)} %copy.22.kept, s32[8]{0:T(128)} %counts.1, bf16[128,1792]{1,0:T(8,128)(2,1)} %g1.1, bf16[128,1792]{1,0:T(8,128)(2,1)} %g1.1, bf16[128,1792]{1,0:T(8,128)(2,1)} %u1_.1, bf16[128,1792]{1,0:T(8,128)(2,1)} %u1_.1, bf16[1792,128]{1,0:T(8,128)(2,1)} %d1.1, ...), custom_call_target="tpu_custom_call" | custom-call | tf_op jit(solution)/shard_map/pack_slots/pallas_call | solution.py:48
  6.0 9.3 %all-to-all-start = ((bf16[8,144,384]{2,1,0:T(8,128)(2,1)}), bf16[8,144,384]{2,1,0:T(8,128)(2,1)S(1)}, u32[]{:S(2)}, u32[]{:S(2)}) async-start(bf16[8,144,384]{2,1,0:T(8,128)(2,1)} %pack_slots.1), calls=%async_computation | async-start | bytes 1769472 | tf_op jit(solution)/shard_map/all_to_all | solution.py:206
  16.8 6.8 %all-to-all-done = bf16[8,144,384]{2,1,0:T(8,128)(2,1)S(1)} async-done(((bf16[8,144,384]{2,1,0:T(8,128)(2,1)}), bf16[8,144,384]{2,1,0:T(8,128)(2,1)S(1)}, u32[]{:S(2)}, u32[]{:S(2)}) %all-to-all-start) | async-done | bytes 884768 | tf_op jit(solution)/shard_map/all_to_all | solution.py:206
  23.6 16.7 %all-gather = bf16[1,512,384]{2,1,0:T(8,128)(2,1)S(1)} all-gather(bf16[1,128,384]{2,1,0:T(8,128)(2,1)S(1)} %constant_dynamic-slice_fusion), channel_id=2, replica_groups=mesh['z'=8,'yh'=4,'core'=2,'yl'=2,'x'=4] {'yh'}, dimensions={1}, use_global_device_ids=true | all-gather | bytes 491520 | tf_op jit(solution)/shard_map/all_gather | solution.py:210
  40.3 4.3 %collective-permute-start = (bf16[512,384]{1,0:T(8,128)(2,1)S(1)}, bf16[512,384]{1,0:T(8,128)(2,1)S(1)}, u32[]{:S(2)}, u32[]{:S(2)}) collective-permute-start(bf16[512,384]{1,0:T(8,128)(2,1)S(1)} %bitcast.16), channel_id=1, source_target_pairs={{0,64},{64,128},{128,192},{192,256},{256,320},{320,384},{384,448},... | collective-permute-start | bytes 1179656 | tf_op jit(solution)/shard_map/ppermute | solution.py:191
  44.6 8.6 %collective-permute-start.1 = (bf16[512,384]{1,0:T(8,128)(2,1)S(1)}, bf16[512,384]{1,0:T(8,128)(2,1)S(1)}, u32[]{:S(2)}, u32[]{:S(2)}) collective-permute-start(bf16[512,384]{1,0:T(8,128)(2,1)S(1)} %bitcast.17), channel_id=1, source_target_pairs={{0,448},{64,0},{128,64},{192,128},{256,192},{320,256},{384,320},{4... | collective-permute-start | bytes 1179656 | tf_op jit(solution)/shard_map/ppermute | solution.py:191
  53.2 3.8 %collective-permute-done = bf16[512,384]{1,0:T(8,128)(2,1)S(1)} collective-permute-done((bf16[512,384]{1,0:T(8,128)(2,1)S(1)}, bf16[512,384]{1,0:T(8,128)(2,1)S(1)}, u32[]{:S(2)}, u32[]{:S(2)}) %collective-permute-start) | collective-permute-done | bytes 393248 | tf_op jit(solution)/shard_map/ppermute | solution.py:191
  57.0 1.9 %collective-permute-start.2 = (bf16[512,384]{1,0:T(8,128)(2,1)S(1)}, bf16[512,384]{1,0:T(8,128)(2,1)}, u32[]{:S(2)}, u32[]{:S(2)}) collective-permute-start(bf16[512,384]{1,0:T(8,128)(2,1)S(1)} %collective-permute-done), channel_id=1, source_target_pairs={{0,64},{64,128},{128,192},{192,256},{256,320},{320,384},{384,448},... | collective-permute-start | bytes 1179656 | tf_op jit(solution)/shard_map/ppermute | solution.py:191
  58.9 5.1 %collective-permute-start.3 = (bf16[512,384]{1,0:T(8,128)(2,1)S(1)}, bf16[512,384]{1,0:T(8,128)(2,1)}, u32[]{:S(2)}, u32[]{:S(2)}) collective-permute-start(bf16[512,384]{1,0:T(8,128)(2,1)S(1)} %collective-permute-done.1), channel_id=1, source_target_pairs={{0,448},{64,0},{128,64},{192,128},{256,192},{320,256},{384,320},{4... | collective-permute-start | bytes 1179656 | tf_op jit(solution)/shard_map/ppermute | solution.py:191
  64.1 1.6 broadcast_in_dim.21
  65.7 5.7 %all-to-all-start.1 = ((bf16[8,16,8192]{2,1,0:T(8,128)(2,1)}), bf16[8,16,8192]{2,1,0:T(8,128)(2,1)}, u32[]{:S(2)}, u32[]{:S(2)}) async-start(bf16[8,16,8192]{2,1,0:T(8,128)(2,1)} %broadcast_in_dim.21), calls=%async_computation.1 | async-start | bytes 4194304 | tf_op jit(solution)/shard_map/all_to_all | solution.py:216
  72.2 1.9 %collective-permute-start.4 = (bf16[512,384]{1,0:T(8,128)(2,1)}, bf16[512,384]{1,0:T(8,128)(2,1)S(1)}, u32[]{:S(2)}, u32[]{:S(2)}) collective-permute-start(bf16[512,384]{1,0:T(8,128)(2,1)} %collective-permute-done.2), channel_id=1, source_target_pairs={{0,64},{64,128},{128,192},{192,256},{256,320},{320,384},{384,448},... | collective-permute-start | bytes 1179656 | tf_op jit(solution)/shard_map/ppermute | solution.py:191
  74.9 5.1 %collective-permute-start.5 = (bf16[512,384]{1,0:T(8,128)(2,1)}, bf16[512,384]{1,0:T(8,128)(2,1)S(1)}, u32[]{:S(2)}, u32[]{:S(2)}) collective-permute-start(bf16[512,384]{1,0:T(8,128)(2,1)} %collective-permute-done.3), channel_id=1, source_target_pairs={{0,448},{64,0},{128,64},{192,128},{256,192},{320,256},{384,320},{4... | collective-permute-start | bytes 1179656 | tf_op jit(solution)/shard_map/ppermute | solution.py:191
  80.8 1.8 %constant_dynamic-update-slice_fusion.3 = bf16[3584,384]{1,0:T(8,128)(2,1)} fusion(bf16[3584,384]{1,0:T(8,128)(2,1)} %constant_dynamic-update-slice_fusion.4, bf16[512,384]{1,0:T(8,128)(2,1)} %collective-permute-done.2), kind=kLoop, calls=%fused_computation.9 | loop fusion | bytes 786432
  82.6 1.8 %constant_dynamic-update-slice_fusion.2 = bf16[3584,384]{1,0:T(8,128)(2,1)} fusion(bf16[3584,384]{1,0:T(8,128)(2,1)} %constant_dynamic-update-slice_fusion.3, bf16[512,384]{1,0:T(8,128)(2,1)} %collective-permute-done.3), kind=kLoop, calls=%fused_computation.8 | loop fusion | bytes 786432
  86.4 1.9 %collective-permute-start.8 = (bf16[3584,384]{1,0:T(8,128)(2,1)}, bf16[3584,384]{1,0:T(8,128)(2,1)}, u32[]{:S(2)}, u32[]{:S(2)}) collective-permute-start(bf16[3584,384]{1,0:T(8,128)(2,1)} %constant_dynamic-update-slice_fusion.refs_0_), channel_id=1, source_target_pairs={{0,8},{8,0},{1,9},{9,1},{2,10},{10,2},{3,11},{11,3},{4,12},{12,4},... | collective-permute-start | bytes 8257544 | tf_op jit(solution)/shard_map/ppermute | solution.py:212
  89.5 1.9 %collective-permute-start.6 = (bf16[256,384]{1,0:T(8,128)(2,1)S(1)}, bf16[256,384]{1,0:T(8,128)(2,1)S(1)}, u32[]{:S(2)}, u32[]{:S(2)}) collective-permute-start(bf16[256,384]{1,0:T(8,128)(2,1)S(1)} %slice.24), channel_id=1, source_target_pairs={{0,64},{64,128},{128,192},{192,256},{256,320},{320,384},{384,448},... | collective-permute-start | bytes 589832 | tf_op jit(solution)/shard_map/ppermute | solution.py:195
  91.5 5.5 %collective-permute-start.7 = (bf16[256,384]{1,0:T(8,128)(2,1)S(1)}, bf16[256,384]{1,0:T(8,128)(2,1)S(1)}, u32[]{:S(2)}, u32[]{:S(2)}) collective-permute-start(bf16[256,384]{1,0:T(8,128)(2,1)S(1)} %slice.25), channel_id=1, source_target_pairs={{0,448},{64,0},{128,64},{192,128},{256,192},{320,256},{384,320},{4... | collective-permute-start | bytes 589832 | tf_op jit(solution)/shard_map/ppermute | solution.py:195
  97.0 3.6 %collective-permute-done.6 = bf16[256,384]{1,0:T(8,128)(2,1)S(1)} collective-permute-done((bf16[256,384]{1,0:T(8,128)(2,1)S(1)}, bf16[256,384]{1,0:T(8,128)(2,1)S(1)}, u32[]{:S(2)}, u32[]{:S(2)}) %collective-permute-start.6) | collective-permute-done | bytes 196640 | tf_op jit(solution)/shard_map/ppermute | solution.py:195
  100.6 1.2 collective-permute-done.7
  101.8 1.9 %collective-permute-start.9 = (bf16[512,384]{1,0:T(8,128)(2,1)S(1)}, bf16[512,384]{1,0:T(8,128)(2,1)S(1)}, u32[]{:S(2)}, u32[]{:S(2)}) collective-permute-start(bf16[512,384]{1,0:T(8,128)(2,1)S(1)} %constant_dynamic-update-slice_fusion.7.refs_1_), channel_id=1, source_target_pairs={{0,8},{8,0},{1,9},{9,1},{2,10},{10,2},{3,11},{11,3},{4,12},{12,4},... | collective-permute-start | bytes 1179656 | tf_op jit(solution)/shard_map/ppermute | solution.py:212
  103.8 1.9 %fusion.2.normed = bf16[128,8192]{1,0:T(8,128)(2,1)} fusion(bf16[128,8192]{1,0:T(8,128)(2,1)S(1)} %copy-done, f32[8192]{0:T(1024)S(1)} %convert_element_type.15, f32[128]{0:T(128)S(1)} %add_rsqrt_fusion), kind=kLoop, calls=%fused_computation.4 | loop fusion | flops 4194304 | bytes 4227584 | tf_op jit(solution)/shard_map/convert_element_type | solution.py:220
  107.0 8.2 %pruned_ffn.1 = (bf16[8,1024,128]{2,1,0:T(8,128)(2,1)}, f32[8,128]{1,0:T(8,128)}) custom-call(s32[2]{0:T(128)} %pad_add_fusion.place, bf16[128,8192]{1,0:T(8,128)(2,1)} %fusion.2.normed, bf16[128,8192]{1,0:T(8,128)(2,1)} %bitcast.7.cot, bf16[16,128]{1,0:T(8,128)(2,1)} %slice.20.gain, bf16[3584,384]{1,0:T(8,128)(2,1)} %constant_dynamic-update-slice_fusion.refs_0_, ...), custom_call_target="tpu_custom_call" | custom-call | tf_op jit(solution)/shard_map/pruned_ffn/pallas_call | solution.py:135
  115.2 5.7 %all-to-all-start.2 = ((bf16[8,1024,128]{2,1,0:T(8,128)(2,1)}), bf16[8,1024,128]{2,1,0:T(8,128)(2,1)}, u32[]{:S(2)}, u32[]{:S(2)}) async-start(bf16[8,1024,128]{2,1,0:T(8,128)(2,1)} %get-tuple-element.13), calls=%async_computation.2 | async-start | bytes 4194304 | tf_op jit(solution)/shard_map/all_to_all | solution.py:224
  124.1 1.9 %collective-permute-start.10 = (f32[8,128]{1,0:T(8,128)S(1)}, f32[8,128]{1,0:T(8,128)S(1)}, u32[]{:S(2)}, u32[]{:S(2)}) collective-permute-start(f32[8,128]{1,0:T(8,128)S(1)} %copy-done.5), channel_id=1, source_target_pairs={{0,8},{8,0},{1,9},{9,1},{2,10},{10,2},{3,11},{11,3},{4,12},{12,4},... | collective-permute-start | bytes 12296 | tf_op jit(solution)/shard_map/ppermute | solution.py:225
  126.0 1.1 collective-permute-done.10
  127.2 16.9 %all-gather.2 = f32[8,1,128]{2,1,0:T(1,128)S(1)} all-gather(f32[1,1,128]{2,1,0:T(1,128)S(1)} %slice_bitcast_fusion), channel_id=1, replica_groups=mesh['z'=8,'yh'=4,'core'=2,'yl'=2,'x'=4] {'z'}, dimensions={0}, use_global_device_ids=true | all-gather | bytes 4608 | tf_op jit(solution)/shard_map/all_gather | solution.py:226
  144.0 9.8 %all-gather.3 = f32[4,1,128]{2,1,0:T(1,128)S(1)} all-gather(f32[1,1,128]{2,1,0:T(1,128)S(1)} %bitcast.20), channel_id=3, replica_groups=mesh['z'=8,'yh'=4,'core'=2,'yl'=2,'x'=4] {'yh'}, dimensions={0}, use_global_device_ids=true | all-gather | bytes 2560 | tf_op jit(solution)/shard_map/all_gather | solution.py:227
  154.4 5.7 %all-to-all-start.3 = ((f32[8,1,128]{2,1,0:T(1,128)}), f32[8,1,128]{2,1,0:T(1,128)S(1)}, u32[]{:S(2)}, u32[]{:S(2)}) async-start(f32[8,1,128]{2,1,0:T(1,128)} %broadcast_in_dim.47), calls=%async_computation.3 | async-start | bytes 8192 | tf_op jit(solution)/shard_map/all_to_all | solution.py:230
  160.3 2.9 %input_grad.1 = bf16[16,8192]{1,0:T(8,128)(2,1)} custom-call(s32[1]{0:T(128)} %bitcast.me.place, bf16[128,8192]{1,0:T(8,128)(2,1)S(1)} %copy-done, bf16[1,8192]{1,0:T(2,128)(2,1)S(1)} %reshape.89.gain, bf16[8,1024,128]{2,1,0:T(8,128)(2,1)} %all-to-all-done.2.parts), custom_call_target="tpu_custom_call" | custom-call | tf_op jit(solution)/shard_map/input_grad/pallas_call | solution.py:168
  (56 shorter events, 12.2 us)
Async XLA Ops:
  0.6 14.7 %copy-start.6 = (s32[8]{0:T(128)S(1)}, s32[8]{0:T(128)}, u32[]{:S(2)}) copy-start(s32[8]{0:T(128)} %counts.1) | copy-start | bytes 100
  3.3 60.8 %copy-start.3 = (bf16[16,8192]{1,0:T(8,128)(2,1)S(1)}, bf16[16,8192]{1,0:T(8,128)(2,1)}, u32[]{:S(2)}) copy-start(bf16[16,8192]{1,0:T(8,128)(2,1)} %param.17) | copy-start | bytes 786436
  6.0 17.6 %all-to-all-start = ((bf16[8,144,384]{2,1,0:T(8,128)(2,1)}), bf16[8,144,384]{2,1,0:T(8,128)(2,1)S(1)}, u32[]{:S(2)}, u32[]{:S(2)}) async-start(bf16[8,144,384]{2,1,0:T(8,128)(2,1)} %pack_slots.1), calls=%async_computation | async-start | bytes 1769472 | tf_op jit(solution)/shard_map/all_to_all | solution.py:206
  40.3 16.7 %collective-permute-start = (bf16[512,384]{1,0:T(8,128)(2,1)S(1)}, bf16[512,384]{1,0:T(8,128)(2,1)S(1)}, u32[]{:S(2)}, u32[]{:S(2)}) collective-permute-start(bf16[512,384]{1,0:T(8,128)(2,1)S(1)} %bitcast.16), channel_id=1, source_target_pairs={{0,64},{64,128},{128,192},{192,256},{256,320},{320,384},{384,448},... | collective-permute-start | bytes 1179656 | tf_op jit(solution)/shard_map/ppermute | solution.py:191
  44.6 14.3 %collective-permute-start.1 = (bf16[512,384]{1,0:T(8,128)(2,1)S(1)}, bf16[512,384]{1,0:T(8,128)(2,1)S(1)}, u32[]{:S(2)}, u32[]{:S(2)}) collective-permute-start(bf16[512,384]{1,0:T(8,128)(2,1)S(1)} %bitcast.17), channel_id=1, source_target_pairs={{0,448},{64,0},{128,64},{192,128},{256,192},{320,256},{384,320},{4... | collective-permute-start | bytes 1179656 | tf_op jit(solution)/shard_map/ppermute | solution.py:191
  57.0 15.2 %collective-permute-start.2 = (bf16[512,384]{1,0:T(8,128)(2,1)S(1)}, bf16[512,384]{1,0:T(8,128)(2,1)}, u32[]{:S(2)}, u32[]{:S(2)}) collective-permute-start(bf16[512,384]{1,0:T(8,128)(2,1)S(1)} %collective-permute-done), channel_id=1, source_target_pairs={{0,64},{64,128},{128,192},{192,256},{256,320},{320,384},{384,448},... | collective-permute-start | bytes 1179656 | tf_op jit(solution)/shard_map/ppermute | solution.py:191
  58.9 16.0 %collective-permute-start.3 = (bf16[512,384]{1,0:T(8,128)(2,1)S(1)}, bf16[512,384]{1,0:T(8,128)(2,1)}, u32[]{:S(2)}, u32[]{:S(2)}) collective-permute-start(bf16[512,384]{1,0:T(8,128)(2,1)S(1)} %collective-permute-done.1), channel_id=1, source_target_pairs={{0,448},{64,0},{128,64},{192,128},{256,192},{320,256},{384,320},{4... | collective-permute-start | bytes 1179656 | tf_op jit(solution)/shard_map/ppermute | solution.py:191
  65.7 40.5 %all-to-all-start.1 = ((bf16[8,16,8192]{2,1,0:T(8,128)(2,1)}), bf16[8,16,8192]{2,1,0:T(8,128)(2,1)}, u32[]{:S(2)}, u32[]{:S(2)}) async-start(bf16[8,16,8192]{2,1,0:T(8,128)(2,1)} %broadcast_in_dim.21), calls=%async_computation.1 | async-start | bytes 4194304 | tf_op jit(solution)/shard_map/all_to_all | solution.py:216
  71.4 17.0 %copy-start.4 = (bf16[8192]{0:T(1024)(128)(2,1)S(1)}, bf16[8192]{0:T(1024)(128)(2,1)}, u32[]{:S(2)}) copy-start(bf16[8192]{0:T(1024)(128)(2,1)} %param.10) | copy-start | bytes 49156
  71.4 17.6 %copy-start = (bf16[128,8192]{1,0:T(8,128)(2,1)S(1)}, bf16[128,8192]{1,0:T(8,128)(2,1)}, u32[]{:S(2)}) copy-start(bf16[128,8192]{1,0:T(8,128)(2,1)} %act.1) | copy-start | bytes 6291460
  72.2 12.2 %collective-permute-start.4 = (bf16[512,384]{1,0:T(8,128)(2,1)}, bf16[512,384]{1,0:T(8,128)(2,1)S(1)}, u32[]{:S(2)}, u32[]{:S(2)}) collective-permute-start(bf16[512,384]{1,0:T(8,128)(2,1)} %collective-permute-done.2), channel_id=1, source_target_pairs={{0,64},{64,128},{128,192},{192,256},{256,320},{320,384},{384,448},... | collective-permute-start | bytes 1179656 | tf_op jit(solution)/shard_map/ppermute | solution.py:191
  74.9 10.7 %collective-permute-start.5 = (bf16[512,384]{1,0:T(8,128)(2,1)}, bf16[512,384]{1,0:T(8,128)(2,1)S(1)}, u32[]{:S(2)}, u32[]{:S(2)}) collective-permute-start(bf16[512,384]{1,0:T(8,128)(2,1)} %collective-permute-done.3), channel_id=1, source_target_pairs={{0,448},{64,0},{128,64},{192,128},{256,192},{320,256},{384,320},{4... | collective-permute-start | bytes 1179656 | tf_op jit(solution)/shard_map/ppermute | solution.py:191
  86.4 19.8 %collective-permute-start.8 = (bf16[3584,384]{1,0:T(8,128)(2,1)}, bf16[3584,384]{1,0:T(8,128)(2,1)}, u32[]{:S(2)}, u32[]{:S(2)}) collective-permute-start(bf16[3584,384]{1,0:T(8,128)(2,1)} %constant_dynamic-update-slice_fusion.refs_0_), channel_id=1, source_target_pairs={{0,8},{8,0},{1,9},{9,1},{2,10},{10,2},{3,11},{11,3},{4,12},{12,4},... | collective-permute-start | bytes 8257544 | tf_op jit(solution)/shard_map/ppermute | solution.py:212
  89.5 11.1 %collective-permute-start.6 = (bf16[256,384]{1,0:T(8,128)(2,1)S(1)}, bf16[256,384]{1,0:T(8,128)(2,1)S(1)}, u32[]{:S(2)}, u32[]{:S(2)}) collective-permute-start(bf16[256,384]{1,0:T(8,128)(2,1)S(1)} %slice.24), channel_id=1, source_target_pairs={{0,64},{64,128},{128,192},{192,256},{256,320},{320,384},{384,448},... | collective-permute-start | bytes 589832 | tf_op jit(solution)/shard_map/ppermute | solution.py:195
  91.5 10.3 %collective-permute-start.7 = (bf16[256,384]{1,0:T(8,128)(2,1)S(1)}, bf16[256,384]{1,0:T(8,128)(2,1)S(1)}, u32[]{:S(2)}, u32[]{:S(2)}) collective-permute-start(bf16[256,384]{1,0:T(8,128)(2,1)S(1)} %slice.25), channel_id=1, source_target_pairs={{0,448},{64,0},{128,64},{192,128},{256,192},{320,256},{384,320},{4... | collective-permute-start | bytes 589832 | tf_op jit(solution)/shard_map/ppermute | solution.py:195
  101.8 4.5 %copy-start.1 = (bf16[512,384]{1,0:T(8,128)(2,1)}, bf16[512,384]{1,0:T(8,128)(2,1)S(1)}, u32[]{:S(2)}) copy-start(bf16[512,384]{1,0:T(8,128)(2,1)S(1)} %constant_dynamic-update-slice_fusion.7.refs_1_) | copy-start | bytes 1179652
  101.8 4.4 %collective-permute-start.9 = (bf16[512,384]{1,0:T(8,128)(2,1)S(1)}, bf16[512,384]{1,0:T(8,128)(2,1)S(1)}, u32[]{:S(2)}, u32[]{:S(2)}) collective-permute-start(bf16[512,384]{1,0:T(8,128)(2,1)S(1)} %constant_dynamic-update-slice_fusion.7.refs_1_), channel_id=1, source_target_pairs={{0,8},{8,0},{1,9},{9,1},{2,10},{10,2},{3,11},{11,3},{4,12},{12,4},... | collective-permute-start | bytes 1179656 | tf_op jit(solution)/shard_map/ppermute | solution.py:212
  106.2 0.8 copy-start.2
  115.2 8.9 %copy-start.5 = (f32[8,128]{1,0:T(8,128)S(1)}, f32[8,128]{1,0:T(8,128)}, u32[]{:S(2)}) copy-start(f32[8,128]{1,0:T(8,128)} %get-tuple-element.12) | copy-start | bytes 12292
  115.2 38.6 %all-to-all-start.2 = ((bf16[8,1024,128]{2,1,0:T(8,128)(2,1)}), bf16[8,1024,128]{2,1,0:T(8,128)(2,1)}, u32[]{:S(2)}, u32[]{:S(2)}) async-start(bf16[8,1024,128]{2,1,0:T(8,128)(2,1)} %get-tuple-element.13), calls=%async_computation.2 | async-start | bytes 4194304 | tf_op jit(solution)/shard_map/all_to_all | solution.py:224
  124.1 3.1 %collective-permute-start.10 = (f32[8,128]{1,0:T(8,128)S(1)}, f32[8,128]{1,0:T(8,128)S(1)}, u32[]{:S(2)}, u32[]{:S(2)}) collective-permute-start(f32[8,128]{1,0:T(8,128)S(1)} %copy-done.5), channel_id=1, source_target_pairs={{0,8},{8,0},{1,9},{9,1},{2,10},{10,2},{3,11},{11,3},{4,12},{12,4},... | collective-permute-start | bytes 12296 | tf_op jit(solution)/shard_map/ppermute | solution.py:225
  154.4 9.6 %all-to-all-start.3 = ((f32[8,1,128]{2,1,0:T(1,128)}), f32[8,1,128]{2,1,0:T(1,128)S(1)}, u32[]{:S(2)}, u32[]{:S(2)}) async-start(f32[8,1,128]{2,1,0:T(1,128)} %broadcast_in_dim.47), calls=%async_computation.3 | async-start | bytes 8192 | tf_op jit(solution)/shard_map/all_to_all | solution.py:230

commit v7 on v5

--- a/solution.py
+++ b/solution.py
@@ -153,11 +153,41 @@
     )(place, act, gain.reshape(1, -1), parts)
 
 
+def pick_kernel(counts, units, out):
+    me = lax.axis_index("yl") * X + lax.axis_index("x")
+    dp = (lax.axis_index("z") * YH + lax.axis_index("yh")) * CORE + lax.axis_index("core")
+    first, count = jnp.int32(0), jnp.int32(0)
+    for shard in range(SHARDS):
+        first += jnp.where(shard < me, counts[shard], 0)
+        count += jnp.where(shard == me, counts[shard], 0)
+    lane = lax.broadcasted_iota(jnp.int32, (1, BLOCK), 1)
+    width = out.shape[1]
+    for k in range(out.shape[0]):
+        total = jnp.zeros((1, BLOCK), F32)
+        for source in range(SHARDS):
+            wanted = (source == first + k) & (k < count)
+            total = jnp.where(wanted, units[source], total)
+        for i in range(width):
+            value = jnp.where(lane == dp * width + i, total, 0.0)
+            out[k : k + 1, i : i + 1] = jnp.sum(value, axis=1, keepdims=True)
+
+
+def pick(counts, units):
+    vmem = pl.BlockSpec(memory_space=pltpu.VMEM)
+    return pl.pallas_call(
+        pick_kernel,
+        out_shape=jax.ShapeDtypeStruct((2, BLOCK // (Z * YH * CORE)), F32),
+        in_specs=[pl.BlockSpec(memory_space=pltpu.SMEM), vmem],
+        out_specs=vmem,
+        name="gain_grad",
+    )(counts, units)
+
+
 def per_device(
     activations, norm_gain, gate_w, up_w, down_w, mask_gain, kept_blocks, kept_counts, cotangent
 ):
     me = lax.axis_index(TENSOR)
-    shards, k = jnp.arange(SHARDS), jnp.arange(2)
+    shards = jnp.arange(SHARDS)
     blocks = mask_gain.shape[0] // BLOCK
     sent = pack(me.reshape(1), kept_blocks, kept_counts, gate_w, up_w, down_w)
     got = lax.all_to_all(sent, TENSOR, split_axis=0, concat_axis=0, tiled=True)
@@ -170,7 +200,6 @@
     late, _ = lax.optimization_barrier(((cotangent, activations, mask_gain, kept_blocks, kept_counts), column))
     cotangent, act, mask_gain, kept_blocks, kept_counts = late
     kept = jnp.clip(kept_blocks[me], 0, blocks - 1)
-    first = jnp.sum(jnp.where(shards < me, kept_counts, 0))
     copies = jnp.broadcast_to(cotangent[None], (SHARDS,) + cotangent.shape)
     cot = lax.all_to_all(copies, TENSOR, split_axis=0, concat_axis=0, tiled=True)
     cot = cot.reshape(-1, cotangent.shape[1])
@@ -183,19 +212,16 @@
     unit_gain = lax.dynamic_slice_in_dim(gains, source * 2 + jnp.clip(which, 0, 1), 1, 0)
 
     parts, unit = ffn(normed, cot, unit_gain, weights)
+    unit = unit + lax.ppermute(unit, "core", [(0, 1), (1, 0)])
+    parts, unit = lax.optimization_barrier((parts, unit))
     got = lax.all_to_all(parts, TENSOR, split_axis=0, concat_axis=0, tiled=True)
-    unit = unit + lax.ppermute(unit, "core", [(0, 1), (1, 0)])
-    unit = jnp.sum(lax.all_gather(unit[:1], "z", axis=0, tiled=True), axis=0)
-    unit, got = lax.optimization_barrier((unit, got))
-    copies = jnp.broadcast_to(unit[None, None], (YH * SHARDS, 1, BLOCK))
-    units = lax.all_to_all(copies, ("yh",) + TENSOR, split_axis=0, concat_axis=0, tiled=True)
+    unit = jnp.sum(lax.all_gather(unit[:1], "z", axis=0, tiled=True), axis=0, keepdims=True)
+    unit = jnp.sum(lax.all_gather(unit, "yh", axis=0, tiled=True), axis=0)
+    copies = jnp.broadcast_to(unit[None, None], (SHARDS, 1, BLOCK))
+    copies, got = lax.optimization_barrier((copies, got))
+    units = lax.all_to_all(copies, TENSOR, split_axis=0, concat_axis=0, tiled=True)
     input_grad = final(me.reshape(1), activations, norm_gain, got)
-    width = BLOCK // (Z * YH * CORE)
-    units = lax.dynamic_slice_in_dim(units.reshape(YH * SHARDS, BLOCK), lax.axis_index(DP) * width, width, 1)
-    count = kept_counts[me]
-    owner = jnp.tile(shards, YH)
-    wanted = (owner[None] == first + k[:, None]) & (k < count)[:, None]
-    gain_grad = jnp.sum(jnp.where(wanted[:, :, None], units[None], 0.0), axis=1)
+    gain_grad = pick(kept_counts, units)
     return input_grad, gain_grad
 
 

time: 162 us -> 165 us (1.019)
  blocking collectives: 59.7 us -> 75.5 us
  waiting for transfers between devices: 29 us -> 19.8 us
  starting transfers between devices: 31.8 us -> 27.6 us
    all_gather x1 -> x2, blocking collectives: 14.8 us -> 30.5 us  [the longest x1 15.7 us: per_device(): unit = jnp.sum(lax.all_gather(unit, 'yh', axis=0, tiled=True), axis=0)]
    all_to_all x1 -> x0, starting transfers between devices: 8.92 us -> none  [per_device(): lax.all_to_all(copies, ('yh',) + TENSOR, split_axis=0, concat_axis=0, til...]
    all_to_all x1, waiting for transfers between devices: 6.1 us -> 0.01 us  [per_device(): got = lax.all_to_all(parts, TENSOR, split_axis=0, concat_axis=0, tiled=True)]
    all_to_all x1 -> x0, waiting for transfers between devices: 4.99 us -> none  [per_device(): lax.all_to_all(copies, ('yh',) + TENSOR, split_axis=0, concat_axis=0, til...]
    all_to_all x1 -> x2, starting transfers between devices: 5.76 us -> 10.3 us  [per_device(): lax.all_to_all(copies, TENSOR, split_axis=0, concat_axis=0, tiled=True)]
  transfers between devices with their start and end apart: 6 -> 6, of which waited for: 5 -> 4; matrix products, arithmetic and copies ran while one was open for 6% -> 4% of each run, Pallas kernels for 2% -> 2%
where the time goes in v7:
time: 165 us; the launch traced here: 163 us
  blocking collectives  75.5 us (46%)
  starting transfers between devices  27.6 us (17%)
  waiting for transfers between devices  19.8 us (12%)
  between operations  15.5 us (9%)
  Pallas kernels  14.8 us (9%)
  local copies, waits for them, and re-layouts  5.24 us (3%)
  other arithmetic  4.96 us (3%)
    all_gather x1, blocking collectives, per_device(): gains = lax.all_gather(gains, TENSOR, axis=0, tiled=True)  27.9 us
    all_gather x1, blocking collectives, per_device(): column = lax.all_gather(slot, 'yh', axis=0, tiled=True)  17.1 us
    all_gather x1, blocking collectives, per_device(): unit = jnp.sum(lax.all_gather(unit, 'yh', axis=0, tiled=True), axis=0)  15.7 us
    all_gather x1, blocking collectives, per_device(): lax.all_gather(unit[:1], 'z', axis=0, tiled=True)  14.8 us
    all_gather x1, waiting for transfers between devices, per_device(): weights = lax.all_gather(column, ('z', 'core'), axis=0, tiled=True)  11.4 us
    all_to_all x2, starting transfers between devices, per_device(): lax.all_to_all(copies, TENSOR, split_axis=0, concat_axis=0, tiled=True)  10.3 us
    all_to_all x1, starting transfers between devices, per_device(): got = lax.all_to_all(sent, TENSOR, split_axis=0, concat_axis=0, tiled=True)  9.44 us
    pallas_call x1, Pallas kernels, ffn(): pl.pallas_call(functools.partial(ffn_kernel, scale), out_shape=(jax.Shape...  7.87 us
  transfers between devices with their start and end apart: 6, of which 4 were waited for; matrix products, arithmetic and copies ran while one was open for 4% of the time, Pallas kernels for 2%

profile of v7, /device:TPU:6, one launch (start us, length us, event | category | flops | bytes accessed | tf_op | source)
XLA Modules:
  0.0 163.3 jit_solution(1529536270703965293)
XLA Ops:
  7.2 1.3 copy.12.kept
  8.5 2.7 %pack_slots.1 = bf16[8,128,384]{2,1,0:T(8,128)(2,1)} custom-call(s32[1]{0:T(128)} %bitcast.me.place, s32[8,2]{1,0:T(8,128)} %copy.12.kept, s32[8]{0:T(128)} %counts.2, bf16[128,1792]{1,0:T(8,128)(2,1)} %g1.1, bf16[128,1792]{1,0:T(8,128)(2,1)} %g1.1, bf16[128,1792]{1,0:T(8,128)(2,1)} %u1_.1, bf16[128,1792]{1,0:T(8,128)(2,1)} %u1_.1, bf16[1792,128]{1,0:T(8,128)(2,1)} %d1.1, ...), custom_call_target="tpu_custom_call" | custom-call | tf_op jit(solution)/shard_map/pack_slots/pallas_call | solution.py:42
  11.2 9.4 %all-to-all-start = ((bf16[8,128,384]{2,1,0:T(8,128)(2,1)}), bf16[8,128,384]{2,1,0:T(8,128)(2,1)S(1)}, u32[]{:S(2)}, u32[]{:S(2)}) async-start(bf16[8,128,384]{2,1,0:T(8,128)(2,1)} %pack_slots.1), calls=%async_computation | async-start | bytes 1572864 | tf_op jit(solution)/shard_map/all_to_all | solution.py:193
  20.7 0.2 reduce-window.9
  20.9 0.6 fusion.3
  22.1 6.1 %all-to-all-done = bf16[8,128,384]{2,1,0:T(8,128)(2,1)S(1)} async-done(((bf16[8,128,384]{2,1,0:T(8,128)(2,1)}), bf16[8,128,384]{2,1,0:T(8,128)(2,1)S(1)}, u32[]{:S(2)}, u32[]{:S(2)}) %all-to-all-start) | async-done | bytes 786464 | tf_op jit(solution)/shard_map/all_to_all | solution.py:193
  28.3 17.1 %all-gather = bf16[1,512,384]{2,1,0:T(8,128)(2,1)} all-gather(bf16[1,128,384]{2,1,0:T(8,128)(2,1)S(1)} %constant_dynamic-slice_fusion.1), channel_id=2, replica_groups=mesh['z'=8,'yh'=4,'core'=2,'yl'=2,'x'=4] {'yh'}, dimensions={1}, use_global_device_ids=true | all-gather | bytes 491520 | tf_op jit(solution)/shard_map/all_gather | solution.py:197
  45.3 0.0 all-gather.8.cloned.1.call-update
  45.4 1.5 broadcast_in_dim.31
  46.9 5.8 %all-to-all-start.1 = ((bf16[8,16,8192]{2,1,0:T(8,128)(2,1)}), bf16[8,16,8192]{2,1,0:T(8,128)(2,1)}, u32[]{:S(2)}, u32[]{:S(2)}) async-start(bf16[8,16,8192]{2,1,0:T(8,128)(2,1)} %broadcast_in_dim.31), calls=%async_computation.1 | async-start | bytes 4194304 | tf_op jit(solution)/shard_map/all_to_all | solution.py:204
  52.6 0.6 fusion.4
  54.0 0.2 clamp_reduce_fusion
  54.2 0.6 gather_fusion
  54.7 0.1 fusion.6
  54.8 27.9 %all-gather.3 = bf16[8,2,128]{2,1,0:T(2,128)(2,1)S(1)} all-gather(bf16[1,2,128]{2,1,0:T(2,128)(2,1)S(1)} %fusion.6), channel_id=1, replica_groups=mesh['z'=8,'yh'=4,'core'=2,'yl'=2,'x'=4] {'yl','x'}, dimensions={0}, use_global_device_ids=true | all-gather | bytes 4608 | tf_op jit(solution)/shard_map/all_gather | solution.py:210
  82.7 0.6 constant_dynamic-slice_fusion.gain
  83.3 0.5 fusion
  83.8 2.0 %fusion.2.normed = bf16[128,8192]{1,0:T(8,128)(2,1)} fusion(bf16[128,8192]{1,0:T(8,128)(2,1)S(1)} %copy-done.1, f32[8192]{0:T(1024)S(1)} %convert_element_type.14, f32[128]{0:T(128)S(1)} %add_rsqrt_fusion), kind=kLoop, calls=%fused_computation.5 | loop fusion | flops 4194304 | bytes 4227584 | tf_op jit(solution)/shard_map/convert_element_type | solution.py:208
  85.8 11.4 %all-gather.8.cloned.1.call-done = bf16[1,8192,384]{2,1,0:T(8,128)(2,1)} async-done(((bf16[1,512,384]{2,1,0:T(8,128)(2,1)}), bf16[1,8192,384]{2,1,0:T(8,128)(2,1)}) %all-gather.8.cloned.1.call-update) | async-done | bytes 6291472 | tf_op jit(solution)/shard_map/all_gather | solution.py:198
  97.2 7.9 %pruned_ffn.1 = (bf16[8,1024,128]{2,1,0:T(8,128)(2,1)}, f32[8,128]{1,0:T(8,128)}) custom-call(bf16[128,8192]{1,0:T(8,128)(2,1)} %fusion.2.normed, bf16[128,8192]{1,0:T(8,128)(2,1)} %bitcast.1.cot, bf16[1,128]{1,0:T(2,128)(2,1)} %constant_dynamic-slice_fusion.gain, bf16[8192,384]{1,0:T(8,128)(2,1)} %bitcast.21), custom_call_target="tpu_custom_call" | custom-call | tf_op jit(solution)/shard_map/pruned_ffn/pallas_call | solution.py:105
  105.1 2.2 %collective-permute-start = (f32[8,128]{1,0:T(8,128)}, f32[8,128]{1,0:T(8,128)S(1)}, u32[]{:S(2)}, u32[]{:S(2)}) collective-permute-start(f32[8,128]{1,0:T(8,128)} %get-tuple-element.19), channel_id=1, source_target_pairs={{0,8},{8,0},{1,9},{9,1},{2,10},{10,2},{3,11},{11,3},{4,12},{12,4},... | collective-permute-start | bytes 12296 | tf_op jit(solution)/shard_map/ppermute | solution.py:215
  107.2 1.1 collective-permute-done
  108.3 0.7 add.54
  109.0 5.7 %all-to-all-start.2 = ((bf16[8,1024,128]{2,1,0:T(8,128)(2,1)}), bf16[8,1024,128]{2,1,0:T(8,128)(2,1)}, u32[]{:S(2)}, u32[]{:S(2)}) async-start(bf16[8,1024,128]{2,1,0:T(8,128)(2,1)} %get-tuple-element.21), calls=%async_computation.2 | async-start | bytes 4194304 | tf_op jit(solution)/shard_map/all_to_all | solution.py:217
  114.7 14.8 %all-gather.4 = f32[8,1,128]{2,1,0:T(1,128)S(1)} all-gather(f32[1,1,128]{2,1,0:T(1,128)S(1)} %slice_bitcast_fusion), channel_id=1, replica_groups=mesh['z'=8,'yh'=4,'core'=2,'yl'=2,'x'=4] {'z'}, dimensions={0}, use_global_device_ids=true | all-gather | bytes 4608 | tf_op jit(solution)/shard_map/all_gather | solution.py:218
  129.6 15.7 %all-gather.5 = f32[4,1,128]{2,1,0:T(1,128)S(1)} all-gather(f32[1,1,128]{2,1,0:T(1,128)S(1)} %bitcast.24), channel_id=4, replica_groups=mesh['z'=8,'yh'=4,'core'=2,'yl'=2,'x'=4] {'yh'}, dimensions={0}, use_global_device_ids=true | all-gather | bytes 2560 | tf_op jit(solution)/shard_map/all_gather | solution.py:219
  145.3 0.6 broadcast_in_dim.36
  145.9 4.5 %all-to-all-start.3 = ((f32[8,1,128]{2,1,0:T(1,128)}), f32[8,1,128]{2,1,0:T(1,128)S(1)}, u32[]{:S(2)}, u32[]{:S(2)}) async-start(f32[8,1,128]{2,1,0:T(1,128)} %broadcast_in_dim.36), calls=%async_computation.3 | async-start | bytes 8192 | tf_op jit(solution)/shard_map/all_to_all | solution.py:222
  150.4 2.9 %input_grad.1 = bf16[16,8192]{1,0:T(8,128)(2,1)} custom-call(s32[1]{0:T(128)} %bitcast.me.place, bf16[128,8192]{1,0:T(8,128)(2,1)S(1)} %copy-done.1, bf16[1,8192]{1,0:T(2,128)(2,1)S(1)} %reshape.88.gain, bf16[8,1024,128]{2,1,0:T(8,128)(2,1)} %all-to-all-done.2.parts), custom_call_target="tpu_custom_call" | custom-call | tf_op jit(solution)/shard_map/input_grad/pallas_call | solution.py:138
  153.3 1.2 all-to-all-done.3.units
  154.5 0.6 copy-done.4
  155.1 1.4 gain_grad.1
  (26 shorter events, 0.2 us)
Async XLA Ops:
  7.2 47.0 %copy-start = (bf16[1792]{0:T(1024)(128)(2,1)S(1)}, bf16[1792]{0:T(1024)(128)(2,1)}, u32[]{:S(2)}) copy-start(bf16[1792]{0:T(1024)(128)(2,1)} %param.14) | copy-start | bytes 10756
  8.5 12.1 %copy-start.5 = (s32[8]{0:T(128)S(1)}, s32[8]{0:T(128)}, u32[]{:S(2)}) copy-start(s32[8]{0:T(128)} %counts.2) | copy-start | bytes 100
  11.2 34.1 %copy-start.2 = (bf16[16,8192]{1,0:T(8,128)(2,1)S(1)}, bf16[16,8192]{1,0:T(8,128)(2,1)}, u32[]{:S(2)}) copy-start(bf16[16,8192]{1,0:T(8,128)(2,1)} %param.17) | copy-start | bytes 786436
  11.2 17.0 %all-to-all-start = ((bf16[8,128,384]{2,1,0:T(8,128)(2,1)}), bf16[8,128,384]{2,1,0:T(8,128)(2,1)S(1)}, u32[]{:S(2)}, u32[]{:S(2)}) async-start(bf16[8,128,384]{2,1,0:T(8,128)(2,1)} %pack_slots.1), calls=%async_computation | async-start | bytes 1572864 | tf_op jit(solution)/shard_map/all_to_all | solution.py:193
  20.7 76.5 %all-gather.8.cloned.1.call-start = ((), (), s32[]{:S(2)}) async-start(), calls=%async_computation.4 | async-start | bytes 6684672 | tf_op jit(solution)/shard_map/all_gather | solution.py:198
  46.9 7.1 %copy-start.3 = (bf16[8192]{0:T(1024)(128)(2,1)S(1)}, bf16[8192]{0:T(1024)(128)(2,1)}, u32[]{:S(2)}) copy-start(bf16[8192]{0:T(1024)(128)(2,1)} %param.10) | copy-start | bytes 49156
  46.9 7.1 %copy-start.6 = (s32[8,2]{0,1:T(2,128)S(1)}, s32[8,2]{0,1:T(2,128)}, u32[]{:S(2)}) copy-start(s32[8,2]{0,1:T(2,128)} %param.15) | copy-start | bytes 196
  46.9 36.5 %copy-start.1 = (bf16[128,8192]{1,0:T(8,128)(2,1)S(1)}, bf16[128,8192]{1,0:T(8,128)(2,1)}, u32[]{:S(2)}) copy-start(bf16[128,8192]{1,0:T(8,128)(2,1)} %act.1) | copy-start | bytes 6291460
  46.9 38.9 %all-to-all-start.1 = ((bf16[8,16,8192]{2,1,0:T(8,128)(2,1)}), bf16[8,16,8192]{2,1,0:T(8,128)(2,1)}, u32[]{:S(2)}, u32[]{:S(2)}) async-start(bf16[8,16,8192]{2,1,0:T(8,128)(2,1)} %broadcast_in_dim.31), calls=%async_computation.1 | async-start | bytes 4194304 | tf_op jit(solution)/shard_map/all_to_all | solution.py:204
  105.1 3.3 %collective-permute-start = (f32[8,128]{1,0:T(8,128)}, f32[8,128]{1,0:T(8,128)S(1)}, u32[]{:S(2)}, u32[]{:S(2)}) collective-permute-start(f32[8,128]{1,0:T(8,128)} %get-tuple-element.19), channel_id=1, source_target_pairs={{0,8},{8,0},{1,9},{9,1},{2,10},{10,2},{3,11},{11,3},{4,12},{12,4},... | collective-permute-start | bytes 12296 | tf_op jit(solution)/shard_map/ppermute | solution.py:215
  109.0 36.3 %all-to-all-start.2 = ((bf16[8,1024,128]{2,1,0:T(8,128)(2,1)}), bf16[8,1024,128]{2,1,0:T(8,128)(2,1)}, u32[]{:S(2)}, u32[]{:S(2)}) async-start(bf16[8,1024,128]{2,1,0:T(8,128)(2,1)} %get-tuple-element.21), calls=%async_computation.2 | async-start | bytes 4194304 | tf_op jit(solution)/shard_map/all_to_all | solution.py:217
  145.9 8.6 %all-to-all-start.3 = ((f32[8,1,128]{2,1,0:T(1,128)}), f32[8,1,128]{2,1,0:T(1,128)S(1)}, u32[]{:S(2)}, u32[]{:S(2)}) async-start(f32[8,1,128]{2,1,0:T(1,128)} %broadcast_in_dim.36), calls=%async_computation.3 | async-start | bytes 8192 | tf_op jit(solution)/shard_map/all_to_all | solution.py:222
  154.5 0.6 copy-start.4
Sparse Core Ops, SparseCore 0:
  45.5 51.6 all-gather.7

commit v8 on v6

--- a/solution.py
+++ b/solution.py
@@ -58,14 +58,14 @@
     )(me, kept, counts, gate_w, gate_w, up_w, up_w, down_w, down_w, gains, gains)
 
 
-def ffn_kernel(scale, layout, place, normed, cot, gain, *refs):
+def ffn_kernel(scale, layout, normed, cot, gain, *refs):
     count = len(layout)
     mine, theirs = refs[:count], refs[count : 2 * count]
     out, unit_out = refs[2 * count : 2 * count + 2]
     n_buf, c_buf = refs[2 * count + 2 : 2 * count + 4]
     a_buf, b_buf = refs[2 * count + 4 : 3 * count + 4], refs[3 * count + 4 : 4 * count + 4]
     sems = refs[-1]
-    z, core = place[0], place[1]
+    z, core = lax.axis_index("z"), lax.axis_index("core")
     copies, work = [], []
 
     def copy(source, target):
@@ -124,7 +124,7 @@
             out[:, pl.ds(first, share), :] = part.astype(BF).reshape(SHARDS, share, BLOCK)
 
 
-def ffn(place, normed, cot, gain, layout, mine, theirs):
+def ffn(normed, cot, gain, layout, mine, theirs):
     tokens, width = normed.shape
     rows = width // BLOCK * (tokens // SHARDS)
     vmem = pl.BlockSpec(memory_space=pltpu.VMEM)
@@ -138,12 +138,12 @@
             jax.ShapeDtypeStruct((SHARDS, rows, BLOCK), BF),
             jax.ShapeDtypeStruct((8, BLOCK), F32),
         ),
-        in_specs=[pl.BlockSpec(memory_space=pltpu.SMEM), anyw, anyw, vmem] + [anyw] * (2 * len(mine)),
+        in_specs=[anyw, anyw, vmem] + [anyw] * (2 * len(mine)),
         out_specs=(vmem, vmem),
         scratch_shapes=buffers + [pltpu.SemaphoreType.DMA((copies,))],
         compiler_params=pltpu.CompilerParams(vmem_limit_bytes=56 << 20),
         name="pruned_ffn",
-    )(place, normed, cot, gain, *mine, *theirs)
+    )(normed, cot, gain, *mine, *theirs)
 
 
 def final_kernel(place, act, gain, parts, grad):
@@ -183,6 +183,36 @@
     )(place, act, gain.reshape(1, -1), parts)
 
 
+def pick_kernel(counts, units, out):
+    me = lax.axis_index("yl") * X + lax.axis_index("x")
+    dp = (lax.axis_index("z") * YH + lax.axis_index("yh")) * CORE + lax.axis_index("core")
+    first, count = jnp.int32(0), jnp.int32(0)
+    for shard in range(SHARDS):
+        first += jnp.where(shard < me, counts[shard], 0)
+        count += jnp.where(shard == me, counts[shard], 0)
+    lane = lax.broadcasted_iota(jnp.int32, (1, BLOCK), 1)
+    width = out.shape[1]
+    for k in range(out.shape[0]):
+        total = jnp.zeros((1, BLOCK), F32)
+        for source in range(SHARDS):
+            wanted = (source == first + k) & (k < count)
+            total = jnp.where(wanted, units[source], total)
+        for i in range(width):
+            value = jnp.where(lane == dp * width + i, total, 0.0)
+            out[k : k + 1, i : i + 1] = jnp.sum(value, axis=1, keepdims=True)
+
+
+def pick(counts, units):
+    vmem = pl.BlockSpec(memory_space=pltpu.VMEM)
+    return pl.pallas_call(
+        pick_kernel,
+        out_shape=jax.ShapeDtypeStruct((2, BLOCK // (Z * YH * CORE)), F32),
+        in_specs=[pl.BlockSpec(memory_space=pltpu.SMEM), vmem],
+        out_specs=vmem,
+        name="gain_grad",
+    )(counts, units)
+
+
 def ring(x):
     up = [(i, (i + 1) % Z) for i in range(Z)]
     down = [(i, (i - 1) % Z) for i in range(Z)]
@@ -191,10 +221,8 @@
         a, b = lax.ppermute(a, "z", up), lax.ppermute(b, "z", down)
         chunks += [a, b]
         order += [(-step, 0, YH), (step, 0, YH)]
-    half = x.shape[0] // 2
-    far = [lax.ppermute(a[:half], "z", up), lax.ppermute(b[half:], "z", down)]
-    arrays = [jnp.concatenate(chunks, axis=0), jnp.concatenate(far, axis=0)]
-    return arrays, (tuple(order), ((Z // 2, 0, YH),)), chunks[1]
+    far = lax.ppermute(a, "z", up)
+    return [jnp.concatenate(chunks, axis=0), far], (tuple(order), ((-4, 0, YH),)), chunks[1]
 
 
 def per_device(
@@ -207,6 +235,7 @@
     ends = jnp.cumsum(kept_counts)
     source = jnp.minimum(jnp.sum((ends <= me).astype(jnp.int32)), SHARDS - 1)
     slot = lax.dynamic_index_in_dim(got, source, 0, keepdims=False)
+    slot, copies = lax.optimization_barrier((slot, copies))
     column = lax.all_gather(slot[:BLOCK], "yh", axis=0, tiled=True)
     weights, layout, early = ring(column)
     others = [lax.ppermute(one, "core", [(0, 1), (1, 0)]) for one in weights]
@@ -218,23 +247,17 @@
     act = act.astype(F32)
     inv_rms = lax.rsqrt(jnp.mean(act * act, axis=-1, keepdims=True) + 1e-05)
     normed = (act * inv_rms * norm_gain.astype(F32)).astype(BF)
-    place = jnp.stack([lax.axis_index("z"), lax.axis_index("core")]).astype(jnp.int32)
-
-    parts, unit = ffn(place, normed, cot, slot[BLOCK:, :BLOCK], layout, weights, others)
+
+    parts, unit = ffn(normed, cot, slot[BLOCK:, :BLOCK], layout, weights, others)
     got = lax.all_to_all(parts, TENSOR, split_axis=0, concat_axis=0, tiled=True)
     unit = unit + lax.ppermute(unit, "core", [(0, 1), (1, 0)])
     unit = jnp.sum(lax.all_gather(unit[:1], "z", axis=0, tiled=True), axis=0, keepdims=True)
     unit = jnp.sum(lax.all_gather(unit, "yh", axis=0, tiled=True), axis=0)
-    unit, got = lax.optimization_barrier((unit, got))
     wide = jnp.broadcast_to(unit[None, None], (SHARDS, 1, BLOCK))
+    wide, got = lax.optimization_barrier((wide, got))
     units = lax.all_to_all(wide, TENSOR, split_axis=0, concat_axis=0, tiled=True)
     input_grad = final(me.reshape(1), activations, norm_gain, got)
-    width = BLOCK // (Z * YH * CORE)
-    units = lax.dynamic_slice_in_dim(units.reshape(SHARDS, BLOCK), lax.axis_index(DP) * width, width, 1)
-    shards, k = jnp.arange(SHARDS), jnp.arange(2)
-    count = kept_counts[me]
-    wanted = (shards[None] == ends[me] - count + k[:, None]) & (k < count)[:, None]
-    gain_grad = jnp.sum(jnp.where(wanted[:, :, None], units[None], 0.0), axis=1)
+    gain_grad = pick(kept_counts, units)
     return input_grad, gain_grad
 
 

time: 167 us -> 165 us (0.988)
  waiting for transfers between devices: 17.9 us -> 30.2 us
  local copies, waits for them, and re-layouts: 15.2 us -> 9.23 us
  starting transfers between devices: 66.5 us -> 60.9 us
  other arithmetic: 5.27 us -> 3.25 us
    ppermute x2 -> x1, waiting for transfers between devices: 4.76 us -> 12.8 us  [ring(): far = lax.ppermute(a, 'z', up)]
    ppermute x2 -> x1, starting transfers between devices: 7.42 us -> 1.92 us  [ring(): far = lax.ppermute(a, 'z', up)]
    ppermute x6, waiting for transfers between devices: 4.25 us -> 8.24 us  [ring(): a, b = (lax.ppermute(a, 'z', up), lax.ppermute(b, 'z', down))]
    unnamed x23 -> x26, local copies, waits for them, and re-layouts: 8.86 us -> 5.04 us
    all_gather x1, blocking collectives: 16.9 us -> 14.9 us  [per_device(): lax.all_gather(unit[:1], 'z', axis=0, tiled=True)]
    all_gather x1, blocking collectives: 9.77 us -> 11.6 us  [per_device(): unit = jnp.sum(lax.all_gather(unit, 'yh', axis=0, tiled=True), axis=0)]
  transfers between devices with their start and end apart: 15 -> 14, of which waited for: 7 -> 7; matrix products, arithmetic and copies ran while one was open for 10% -> 4% of each run, Pallas kernels for 2% -> 2%
where the time goes in v8:
time: 165 us; the launch traced here: 163 us
  starting transfers between devices  60.9 us (37%)
  blocking collectives  43.1 us (26%)
  waiting for transfers between devices  30.2 us (18%)
  Pallas kernels  15.1 us (9%)
  local copies, waits for them, and re-layouts  9.23 us (6%)
  other arithmetic  3.25 us (2%)
    ppermute x6, starting transfers between devices, ring(): a, b = (lax.ppermute(a, 'z', up), lax.ppermute(b, 'z', down))  27.1 us
    all_gather x1, blocking collectives, per_device(): column = lax.all_gather(slot[:BLOCK], 'yh', axis=0, tiled=True)  16.7 us
    all_gather x1, blocking collectives, per_device(): lax.all_gather(unit[:1], 'z', axis=0, tiled=True)  14.9 us
    ppermute x1, waiting for transfers between devices, ring(): far = lax.ppermute(a, 'z', up)  12.8 us
    all_gather x1, blocking collectives, per_device(): unit = jnp.sum(lax.all_gather(unit, 'yh', axis=0, tiled=True), axis=0)  11.6 us
    all_to_all x1, starting transfers between devices, per_device(): got = lax.all_to_all(sent, TENSOR, split_axis=0, concat_axis=0, tiled=True)  9.36 us
    ppermute x6, waiting for transfers between devices, ring(): a, b = (lax.ppermute(a, 'z', up), lax.ppermute(b, 'z', down))  8.24 us
    pallas_call x1, Pallas kernels, ffn(): pl.pallas_call(functools.partial(ffn_kernel, scale, layout), out_shape=(j...  8.17 us
  transfers between devices with their start and end apart: 14, of which 7 were waited for; matrix products, arithmetic and copies ran while one was open for 4% of the time, Pallas kernels for 2%

profile of v8, /device:TPU:6, one launch (start us, length us, event | category | flops | bytes accessed | tf_op | source)
XLA Modules:
  0.0 163.4 jit_solution(13741784782599944128)
XLA Ops:
  0.6 1.3 copy.16.m0.m1
  1.9 1.3 copy.15.kept
  3.3 2.7 %pack_slots.1 = bf16[8,144,384]{2,1,0:T(8,128)(2,1)} custom-call(s32[1]{0:T(128)} %bitcast.me.place, s32[8,2]{1,0:T(8,128)} %copy.15.kept, s32[8]{0:T(128)} %counts.3, bf16[128,1792]{1,0:T(8,128)(2,1)} %g1.1, bf16[128,1792]{1,0:T(8,128)(2,1)} %g1.1, bf16[128,1792]{1,0:T(8,128)(2,1)} %u1_.1, bf16[128,1792]{1,0:T(8,128)(2,1)} %u1_.1, bf16[1792,128]{1,0:T(8,128)(2,1)} %d1.1, ...), custom_call_target="tpu_custom_call" | custom-call | tf_op jit(solution)/shard_map/pack_slots/pallas_call | solution.py:48
  6.0 9.4 %all-to-all-start = ((bf16[8,144,384]{2,1,0:T(8,128)(2,1)}), bf16[8,144,384]{2,1,0:T(8,128)(2,1)S(1)}, u32[]{:S(2)}, u32[]{:S(2)}) async-start(bf16[8,144,384]{2,1,0:T(8,128)(2,1)} %pack_slots.1), calls=%async_computation | async-start | bytes 1769472 | tf_op jit(solution)/shard_map/all_to_all | solution.py:234
  16.8 6.7 %all-to-all-done = bf16[8,144,384]{2,1,0:T(8,128)(2,1)S(1)} async-done(((bf16[8,144,384]{2,1,0:T(8,128)(2,1)}), bf16[8,144,384]{2,1,0:T(8,128)(2,1)S(1)}, u32[]{:S(2)}, u32[]{:S(2)}) %all-to-all-start) | async-done | bytes 884768 | tf_op jit(solution)/shard_map/all_to_all | solution.py:234
  23.6 1.6 broadcast_in_dim.6
  25.2 16.7 %all_gather.9 = bf16[512,384]{1,0:T(8,128)(2,1)S(1)} all-gather(bf16[128,384]{1,0:T(8,128)(2,1)S(1)} %slice.9), channel_id=1, replica_groups=mesh['z'=8,'yh'=4,'core'=2,'yl'=2,'x'=4] {'yh'}, dimensions={0}, use_global_device_ids=true | all-gather | bytes 491520 | tf_op jit(solution)/shard_map/all_gather | solution.py:239
  41.9 4.3 %collective-permute-start = (bf16[512,384]{1,0:T(8,128)(2,1)S(1)}, bf16[512,384]{1,0:T(8,128)(2,1)}, u32[]{:S(2)}, u32[]{:S(2)}) collective-permute-start(bf16[512,384]{1,0:T(8,128)(2,1)S(1)} %all_gather.9), channel_id=1, source_target_pairs={{0,64},{64,128},{128,192},{192,256},{256,320},{320,384},{384,448},... | collective-permute-start | bytes 1179656 | tf_op jit(solution)/shard_map/ppermute | solution.py:221
  46.2 8.6 %collective-permute-start.1 = (bf16[512,384]{1,0:T(8,128)(2,1)S(1)}, bf16[512,384]{1,0:T(8,128)(2,1)S(1)}, u32[]{:S(2)}, u32[]{:S(2)}) collective-permute-start(bf16[512,384]{1,0:T(8,128)(2,1)S(1)} %all_gather.9), channel_id=1, source_target_pairs={{0,448},{64,0},{128,64},{192,128},{256,192},{320,256},{384,320},{4... | collective-permute-start | bytes 1179656 | tf_op jit(solution)/shard_map/ppermute | solution.py:221
  54.8 3.9 %collective-permute-done = bf16[512,384]{1,0:T(8,128)(2,1)} collective-permute-done((bf16[512,384]{1,0:T(8,128)(2,1)S(1)}, bf16[512,384]{1,0:T(8,128)(2,1)}, u32[]{:S(2)}, u32[]{:S(2)}) %collective-permute-start) | collective-permute-done | bytes 393248 | tf_op jit(solution)/shard_map/ppermute | solution.py:221
  58.7 1.9 %collective-permute-start.2 = (bf16[512,384]{1,0:T(8,128)(2,1)}, bf16[512,384]{1,0:T(8,128)(2,1)S(1)}, u32[]{:S(2)}, u32[]{:S(2)}) collective-permute-start(bf16[512,384]{1,0:T(8,128)(2,1)} %collective-permute-done), channel_id=1, source_target_pairs={{0,64},{64,128},{128,192},{192,256},{256,320},{320,384},{384,448},... | collective-permute-start | bytes 1179656 | tf_op jit(solution)/shard_map/ppermute | solution.py:221
  60.6 5.1 %collective-permute-start.3 = (bf16[512,384]{1,0:T(8,128)(2,1)S(1)}, bf16[512,384]{1,0:T(8,128)(2,1)}, u32[]{:S(2)}, u32[]{:S(2)}) collective-permute-start(bf16[512,384]{1,0:T(8,128)(2,1)S(1)} %collective-permute-done.1), channel_id=1, source_target_pairs={{0,448},{64,0},{128,64},{192,128},{256,192},{320,256},{384,320},{4... | collective-permute-start | bytes 1179656 | tf_op jit(solution)/shard_map/ppermute | solution.py:221
  65.8 5.7 %all-to-all-start.1 = ((bf16[8,16,8192]{2,1,0:T(8,128)(2,1)}), bf16[8,16,8192]{2,1,0:T(8,128)(2,1)}, u32[]{:S(2)}, u32[]{:S(2)}) async-start(bf16[8,16,8192]{2,1,0:T(8,128)(2,1)} %broadcast_in_dim.6), calls=%async_computation.1 | async-start | bytes 4194304 | tf_op jit(solution)/shard_map/all_to_all | solution.py:245
  71.5 2.1 %collective-permute-start.4 = (bf16[512,384]{1,0:T(8,128)(2,1)S(1)}, bf16[512,384]{1,0:T(8,128)(2,1)S(1)}, u32[]{:S(2)}, u32[]{:S(2)}) collective-permute-start(bf16[512,384]{1,0:T(8,128)(2,1)S(1)} %collective-permute-done.2), channel_id=1, source_target_pairs={{0,64},{64,128},{128,192},{192,256},{256,320},{320,384},{384,448},... | collective-permute-start | bytes 1179656 | tf_op jit(solution)/shard_map/ppermute | solution.py:221
  74.7 5.1 %collective-permute-start.5 = (bf16[512,384]{1,0:T(8,128)(2,1)}, bf16[512,384]{1,0:T(8,128)(2,1)S(1)}, u32[]{:S(2)}, u32[]{:S(2)}) collective-permute-start(bf16[512,384]{1,0:T(8,128)(2,1)} %collective-permute-done.3), channel_id=1, source_target_pairs={{0,448},{64,0},{128,64},{192,128},{256,192},{320,256},{384,320},{4... | collective-permute-start | bytes 1179656 | tf_op jit(solution)/shard_map/ppermute | solution.py:221
  81.0 1.5 collective-permute-done.4
  82.6 2.8 %collective-permute-done.5 = bf16[512,384]{1,0:T(8,128)(2,1)S(1)} collective-permute-done((bf16[512,384]{1,0:T(8,128)(2,1)}, bf16[512,384]{1,0:T(8,128)(2,1)S(1)}, u32[]{:S(2)}, u32[]{:S(2)}) %collective-permute-start.5) | collective-permute-done | bytes 393248 | tf_op jit(solution)/shard_map/ppermute | solution.py:221
  85.5 1.9 %collective-permute-start.7 = (bf16[3584,384]{1,0:T(8,128)(2,1)S(1)}, bf16[3584,384]{1,0:T(8,128)(2,1)}, u32[]{:S(2)}, u32[]{:S(2)}) collective-permute-start(bf16[3584,384]{1,0:T(8,128)(2,1)S(1)} %constant_dynamic-update-slice_fusion.refs_0_), channel_id=1, source_target_pairs={{0,8},{8,0},{1,9},{9,1},{2,10},{10,2},{3,11},{11,3},{4,12},{12,4},... | collective-permute-start | bytes 8257544 | tf_op jit(solution)/shard_map/ppermute | solution.py:241
  87.4 1.9 %collective-permute-start.6 = (bf16[512,384]{1,0:T(8,128)(2,1)S(1)}, bf16[512,384]{1,0:T(8,128)(2,1)S(1)}, u32[]{:S(2)}, u32[]{:S(2)}) collective-permute-start(bf16[512,384]{1,0:T(8,128)(2,1)S(1)} %collective-permute-done.4), channel_id=1, source_target_pairs={{0,64},{64,128},{128,192},{192,256},{256,320},{320,384},{384,448},... | collective-permute-start | bytes 1179656 | tf_op jit(solution)/shard_map/ppermute | solution.py:224
  89.9 12.8 %collective-permute-done.6.refs_1_ = bf16[512,384]{1,0:T(8,128)(2,1)S(1)} collective-permute-done((bf16[512,384]{1,0:T(8,128)(2,1)S(1)}, bf16[512,384]{1,0:T(8,128)(2,1)S(1)}, u32[]{:S(2)}, u32[]{:S(2)}) %collective-permute-start.6) | collective-permute-done | bytes 393248 | tf_op jit(solution)/shard_map/ppermute | solution.py:224
  102.7 1.9 %collective-permute-start.8 = (bf16[512,384]{1,0:T(8,128)(2,1)S(1)}, bf16[512,384]{1,0:T(8,128)(2,1)S(1)}, u32[]{:S(2)}, u32[]{:S(2)}) collective-permute-start(bf16[512,384]{1,0:T(8,128)(2,1)S(1)} %collective-permute-done.6.refs_1_), channel_id=1, source_target_pairs={{0,8},{8,0},{1,9},{9,1},{2,10},{10,2},{3,11},{11,3},{4,12},{12,4},... | collective-permute-start | bytes 1179656 | tf_op jit(solution)/shard_map/ppermute | solution.py:241
  104.6 1.9 %fusion.2.normed = bf16[128,8192]{1,0:T(8,128)(2,1)} fusion(bf16[128,8192]{1,0:T(8,128)(2,1)S(1)} %copy-done, f32[8192]{0:T(1024)S(1)} %convert_element_type.15, f32[128]{0:T(128)S(1)} %add_rsqrt_fusion), kind=kLoop, calls=%fused_computation.4 | loop fusion | flops 4194304 | bytes 4227584 | tf_op jit(solution)/shard_map/convert_element_type | solution.py:249
  107.8 8.2 %pruned_ffn.1 = (bf16[8,1024,128]{2,1,0:T(8,128)(2,1)}, f32[8,128]{1,0:T(8,128)}) custom-call(bf16[128,8192]{1,0:T(8,128)(2,1)} %fusion.2.normed, bf16[128,8192]{1,0:T(8,128)(2,1)} %bitcast.4.cot, bf16[16,128]{1,0:T(8,128)(2,1)} %slice.10.gain, bf16[3584,384]{1,0:T(8,128)(2,1)} %copy-done.1, bf16[512,384]{1,0:T(8,128)(2,1)} %copy-done.2, ...), custom_call_target="tpu_custom_call" | custom-call | tf_op jit(solution)/shard_map/pruned_ffn/pallas_call | solution.py:135
  116.0 5.7 %all-to-all-start.2 = ((bf16[8,1024,128]{2,1,0:T(8,128)(2,1)}), bf16[8,1024,128]{2,1,0:T(8,128)(2,1)}, u32[]{:S(2)}, u32[]{:S(2)}) async-start(bf16[8,1024,128]{2,1,0:T(8,128)(2,1)} %get-tuple-element.17), calls=%async_computation.2 | async-start | bytes 4194304 | tf_op jit(solution)/shard_map/all_to_all | solution.py:252
  121.8 1.9 %collective-permute-start.9 = (f32[8,128]{1,0:T(8,128)S(1)}, f32[8,128]{1,0:T(8,128)S(1)}, u32[]{:S(2)}, u32[]{:S(2)}) collective-permute-start(f32[8,128]{1,0:T(8,128)S(1)} %copy-done.7), channel_id=1, source_target_pairs={{0,8},{8,0},{1,9},{9,1},{2,10},{10,2},{3,11},{11,3},{4,12},{12,4},... | collective-permute-start | bytes 12296 | tf_op jit(solution)/shard_map/ppermute | solution.py:253
  123.7 1.1 collective-permute-done.9
  124.8 14.9 %all-gather.1 = f32[8,1,128]{2,1,0:T(1,128)S(1)} all-gather(f32[1,1,128]{2,1,0:T(1,128)S(1)} %slice_bitcast_fusion), channel_id=1, replica_groups=mesh['z'=8,'yh'=4,'core'=2,'yl'=2,'x'=4] {'z'}, dimensions={0}, use_global_device_ids=true | all-gather | bytes 4608 | tf_op jit(solution)/shard_map/all_gather | solution.py:254
  139.7 11.6 %all-gather.2 = f32[4,1,128]{2,1,0:T(1,128)S(1)} all-gather(f32[1,1,128]{2,1,0:T(1,128)S(1)} %bitcast.10), channel_id=2, replica_groups=mesh['z'=8,'yh'=4,'core'=2,'yl'=2,'x'=4] {'yh'}, dimensions={0}, use_global_device_ids=true | all-gather | bytes 2560 | tf_op jit(solution)/shard_map/all_gather | solution.py:255
  151.9 5.4 %all-to-all-start.3 = ((f32[8,1,128]{2,1,0:T(1,128)}), f32[8,1,128]{2,1,0:T(1,128)S(1)}, u32[]{:S(2)}, u32[]{:S(2)}) async-start(f32[8,1,128]{2,1,0:T(1,128)} %broadcast_in_dim.8), calls=%async_computation.3 | async-start | bytes 8192 | tf_op jit(solution)/shard_map/all_to_all | solution.py:258
  157.4 2.9 %input_grad.1 = bf16[16,8192]{1,0:T(8,128)(2,1)} custom-call(s32[1]{0:T(128)} %bitcast.me.place, bf16[128,8192]{1,0:T(8,128)(2,1)S(1)} %copy-done, bf16[1,8192]{1,0:T(2,128)(2,1)S(1)} %reshape.58.gain, bf16[8,1024,128]{2,1,0:T(8,128)(2,1)} %all-to-all-done.2.parts), custom_call_target="tpu_custom_call" | custom-call | tf_op jit(solution)/shard_map/input_grad/pallas_call | solution.py:168
  160.2 1.2 all-to-all-done.3.units
  162.0 1.4 gain_grad.1
  (46 shorter events, 6.4 us)
Async XLA Ops:
  0.6 14.7 %copy-start.8 = (s32[8]{0:T(128)S(1)}, s32[8]{0:T(128)}, u32[]{:S(2)}) copy-start(s32[8]{0:T(128)} %counts.3) | copy-start | bytes 100
  3.3 20.3 %copy-start.4 = (bf16[16,8192]{1,0:T(8,128)(2,1)S(1)}, bf16[16,8192]{1,0:T(8,128)(2,1)}, u32[]{:S(2)}) copy-start(bf16[16,8192]{1,0:T(8,128)(2,1)} %param.17) | copy-start | bytes 786436
  6.0 17.6 %all-to-all-start = ((bf16[8,144,384]{2,1,0:T(8,128)(2,1)}), bf16[8,144,384]{2,1,0:T(8,128)(2,1)S(1)}, u32[]{:S(2)}, u32[]{:S(2)}) async-start(bf16[8,144,384]{2,1,0:T(8,128)(2,1)} %pack_slots.1), calls=%async_computation | async-start | bytes 1769472 | tf_op jit(solution)/shard_map/all_to_all | solution.py:234
  41.9 16.8 %collective-permute-start = (bf16[512,384]{1,0:T(8,128)(2,1)S(1)}, bf16[512,384]{1,0:T(8,128)(2,1)}, u32[]{:S(2)}, u32[]{:S(2)}) collective-permute-start(bf16[512,384]{1,0:T(8,128)(2,1)S(1)} %all_gather.9), channel_id=1, source_target_pairs={{0,64},{64,128},{128,192},{192,256},{256,320},{320,384},{384,448},... | collective-permute-start | bytes 1179656 | tf_op jit(solution)/shard_map/ppermute | solution.py:221
  46.2 14.4 %collective-permute-start.1 = (bf16[512,384]{1,0:T(8,128)(2,1)S(1)}, bf16[512,384]{1,0:T(8,128)(2,1)S(1)}, u32[]{:S(2)}, u32[]{:S(2)}) collective-permute-start(bf16[512,384]{1,0:T(8,128)(2,1)S(1)} %all_gather.9), channel_id=1, source_target_pairs={{0,448},{64,0},{128,64},{192,128},{256,192},{320,256},{384,320},{4... | collective-permute-start | bytes 1179656 | tf_op jit(solution)/shard_map/ppermute | solution.py:221
  58.7 12.8 %collective-permute-start.2 = (bf16[512,384]{1,0:T(8,128)(2,1)}, bf16[512,384]{1,0:T(8,128)(2,1)S(1)}, u32[]{:S(2)}, u32[]{:S(2)}) collective-permute-start(bf16[512,384]{1,0:T(8,128)(2,1)} %collective-permute-done), channel_id=1, source_target_pairs={{0,64},{64,128},{128,192},{192,256},{256,320},{320,384},{384,448},... | collective-permute-start | bytes 1179656 | tf_op jit(solution)/shard_map/ppermute | solution.py:221
  60.6 14.0 %collective-permute-start.3 = (bf16[512,384]{1,0:T(8,128)(2,1)S(1)}, bf16[512,384]{1,0:T(8,128)(2,1)}, u32[]{:S(2)}, u32[]{:S(2)}) collective-permute-start(bf16[512,384]{1,0:T(8,128)(2,1)S(1)} %collective-permute-done.1), channel_id=1, source_target_pairs={{0,448},{64,0},{128,64},{192,128},{256,192},{320,256},{384,320},{4... | collective-permute-start | bytes 1179656 | tf_op jit(solution)/shard_map/ppermute | solution.py:221
  65.8 41.3 %all-to-all-start.1 = ((bf16[8,16,8192]{2,1,0:T(8,128)(2,1)}), bf16[8,16,8192]{2,1,0:T(8,128)(2,1)}, u32[]{:S(2)}, u32[]{:S(2)}) async-start(bf16[8,16,8192]{2,1,0:T(8,128)(2,1)} %broadcast_in_dim.6), calls=%async_computation.1 | async-start | bytes 4194304 | tf_op jit(solution)/shard_map/all_to_all | solution.py:245
  71.5 15.9 %copy-start.5 = (bf16[8192]{0:T(1024)(128)(2,1)S(1)}, bf16[8192]{0:T(1024)(128)(2,1)}, u32[]{:S(2)}) copy-start(bf16[8192]{0:T(1024)(128)(2,1)} %param.10) | copy-start | bytes 49156
  71.5 17.9 %copy-start = (bf16[128,8192]{1,0:T(8,128)(2,1)S(1)}, bf16[128,8192]{1,0:T(8,128)(2,1)}, u32[]{:S(2)}) copy-start(bf16[128,8192]{1,0:T(8,128)(2,1)} %act.1) | copy-start | bytes 6291460
  71.5 11.0 %collective-permute-start.4 = (bf16[512,384]{1,0:T(8,128)(2,1)S(1)}, bf16[512,384]{1,0:T(8,128)(2,1)S(1)}, u32[]{:S(2)}, u32[]{:S(2)}) collective-permute-start(bf16[512,384]{1,0:T(8,128)(2,1)S(1)} %collective-permute-done.2), channel_id=1, source_target_pairs={{0,64},{64,128},{128,192},{192,256},{256,320},{320,384},{384,448},... | collective-permute-start | bytes 1179656 | tf_op jit(solution)/shard_map/ppermute | solution.py:221
  74.7 10.7 %collective-permute-start.5 = (bf16[512,384]{1,0:T(8,128)(2,1)}, bf16[512,384]{1,0:T(8,128)(2,1)S(1)}, u32[]{:S(2)}, u32[]{:S(2)}) collective-permute-start(bf16[512,384]{1,0:T(8,128)(2,1)} %collective-permute-done.3), channel_id=1, source_target_pairs={{0,448},{64,0},{128,64},{192,128},{256,192},{320,256},{384,320},{4... | collective-permute-start | bytes 1179656 | tf_op jit(solution)/shard_map/ppermute | solution.py:221
  85.5 21.0 %copy-start.1 = (bf16[3584,384]{1,0:T(8,128)(2,1)}, bf16[3584,384]{1,0:T(8,128)(2,1)S(1)}, u32[]{:S(2)}) copy-start(bf16[3584,384]{1,0:T(8,128)(2,1)S(1)} %constant_dynamic-update-slice_fusion.refs_0_) | copy-start | bytes 8257540
  85.5 21.6 %collective-permute-start.7 = (bf16[3584,384]{1,0:T(8,128)(2,1)S(1)}, bf16[3584,384]{1,0:T(8,128)(2,1)}, u32[]{:S(2)}, u32[]{:S(2)}) collective-permute-start(bf16[3584,384]{1,0:T(8,128)(2,1)S(1)} %constant_dynamic-update-slice_fusion.refs_0_), channel_id=1, source_target_pairs={{0,8},{8,0},{1,9},{9,1},{2,10},{10,2},{3,11},{11,3},{4,12},{12,4},... | collective-permute-start | bytes 8257544 | tf_op jit(solution)/shard_map/ppermute | solution.py:241
  87.4 15.3 %collective-permute-start.6 = (bf16[512,384]{1,0:T(8,128)(2,1)S(1)}, bf16[512,384]{1,0:T(8,128)(2,1)S(1)}, u32[]{:S(2)}, u32[]{:S(2)}) collective-permute-start(bf16[512,384]{1,0:T(8,128)(2,1)S(1)} %collective-permute-done.4), channel_id=1, source_target_pairs={{0,64},{64,128},{128,192},{192,256},{256,320},{320,384},{384,448},... | collective-permute-start | bytes 1179656 | tf_op jit(solution)/shard_map/ppermute | solution.py:224
  102.7 4.4 %copy-start.2 = (bf16[512,384]{1,0:T(8,128)(2,1)}, bf16[512,384]{1,0:T(8,128)(2,1)S(1)}, u32[]{:S(2)}) copy-start(bf16[512,384]{1,0:T(8,128)(2,1)S(1)} %collective-permute-done.6.refs_1_) | copy-start | bytes 1179652
  102.7 4.4 %collective-permute-start.8 = (bf16[512,384]{1,0:T(8,128)(2,1)S(1)}, bf16[512,384]{1,0:T(8,128)(2,1)S(1)}, u32[]{:S(2)}, u32[]{:S(2)}) collective-permute-start(bf16[512,384]{1,0:T(8,128)(2,1)S(1)} %collective-permute-done.6.refs_1_), channel_id=1, source_target_pairs={{0,8},{8,0},{1,9},{9,1},{2,10},{10,2},{3,11},{11,3},{4,12},{12,4},... | collective-permute-start | bytes 1179656 | tf_op jit(solution)/shard_map/ppermute | solution.py:241
  107.1 0.8 copy-start.3
  116.0 5.7 %copy-start.7 = (f32[8,128]{1,0:T(8,128)S(1)}, f32[8,128]{1,0:T(8,128)}, u32[]{:S(2)}) copy-start(f32[8,128]{1,0:T(8,128)} %get-tuple-element.16) | copy-start | bytes 12292
  116.0 35.3 %all-to-all-start.2 = ((bf16[8,1024,128]{2,1,0:T(8,128)(2,1)}), bf16[8,1024,128]{2,1,0:T(8,128)(2,1)}, u32[]{:S(2)}, u32[]{:S(2)}) async-start(bf16[8,1024,128]{2,1,0:T(8,128)(2,1)} %get-tuple-element.17), calls=%async_computation.2 | async-start | bytes 4194304 | tf_op jit(solution)/shard_map/all_to_all | solution.py:252
  121.8 3.0 %collective-permute-start.9 = (f32[8,128]{1,0:T(8,128)S(1)}, f32[8,128]{1,0:T(8,128)S(1)}, u32[]{:S(2)}, u32[]{:S(2)}) collective-permute-start(f32[8,128]{1,0:T(8,128)S(1)} %copy-done.7), channel_id=1, source_target_pairs={{0,8},{8,0},{1,9},{9,1},{2,10},{10,2},{3,11},{11,3},{4,12},{12,4},... | collective-permute-start | bytes 12296 | tf_op jit(solution)/shard_map/ppermute | solution.py:253
  151.9 9.5 %all-to-all-start.3 = ((f32[8,1,128]{2,1,0:T(1,128)}), f32[8,1,128]{2,1,0:T(1,128)S(1)}, u32[]{:S(2)}, u32[]{:S(2)}) async-start(f32[8,1,128]{2,1,0:T(1,128)} %broadcast_in_dim.8), calls=%async_computation.3 | async-start | bytes 8192 | tf_op jit(solution)/shard_map/all_to_all | solution.py:258
  161.4 0.6 copy-start.6

commit v9 on v5

--- a/solution.py
+++ b/solution.py
@@ -116,7 +116,7 @@
     )(normed, cot, gain, weights)
 
 
-def final_kernel(place, act, gain, parts, grad):
+def final_kernel(place, counts, act, gain, parts, units, grad, shares):
     share, width = act.shape
     x = act[...].astype(F32)
     inv = lax.rsqrt(jnp.mean(x * x, axis=-1, keepdims=True) + 1e-05)
@@ -130,34 +130,59 @@
     normalized = x * inv
     mean = jnp.mean(scaled * normalized, axis=-1, keepdims=True)
     grad[...] = (inv * (scaled - normalized * mean)).astype(BF)
-
-
-def final(place, act, gain, parts):
+    me = place[0]
+    dp = (lax.axis_index("z") * YH + lax.axis_index("yh")) * CORE + lax.axis_index("core")
+    first, count = jnp.int32(0), jnp.int32(0)
+    for shard in range(SHARDS):
+        first += jnp.where(shard < me, counts[shard], 0)
+        count += jnp.where(shard == me, counts[shard], 0)
+    lane = lax.broadcasted_iota(jnp.int32, (1, BLOCK), 1)
+    wide = shares.shape[1]
+    for k in range(shares.shape[0]):
+        total = jnp.zeros((1, BLOCK), F32)
+        for source in range(SHARDS):
+            row = source % X * YL + source // X
+            wanted = (source == first + k) & (k < count)
+            total = jnp.where(wanted, units[row : row + 1, :], total)
+        for i in range(wide):
+            value = jnp.where(lane == dp * wide + i, total, 0.0)
+            shares[k : k + 1, i : i + 1] = jnp.sum(value, axis=1, keepdims=True)
+
+
+def final(place, counts, act, gain, parts, units):
     tokens, width = act.shape
     share = tokens // SHARDS
+    wide = BLOCK // (Z * YH * CORE)
     return pl.pallas_call(
         final_kernel,
-        out_shape=jax.ShapeDtypeStruct((share, width), BF),
+        out_shape=(
+            jax.ShapeDtypeStruct((share, width), BF),
+            jax.ShapeDtypeStruct((2, wide), F32),
+        ),
         grid_spec=pltpu.PrefetchScalarGridSpec(
-            num_scalar_prefetch=1,
+            num_scalar_prefetch=2,
             grid=(1,),
             in_specs=[
-                pl.BlockSpec((share, width), lambda i, p: (p[0], 0)),
-                pl.BlockSpec((1, width), lambda i, p: (0, 0)),
-                pl.BlockSpec(parts.shape, lambda i, p: (0, 0, 0)),
+                pl.BlockSpec((share, width), lambda i, p, n: (p[0], 0)),
+                pl.BlockSpec((1, width), lambda i, p, n: (0, 0)),
+                pl.BlockSpec(parts.shape, lambda i, p, n: (0, 0, 0)),
+                pl.BlockSpec(units.shape, lambda i, p, n: (0, 0)),
             ],
-            out_specs=pl.BlockSpec((share, width), lambda i, p: (0, 0)),
+            out_specs=(
+                pl.BlockSpec((share, width), lambda i, p, n: (0, 0)),
+                pl.BlockSpec((2, wide), lambda i, p, n: (0, 0)),
+            ),
         ),
         compiler_params=pltpu.CompilerParams(vmem_limit_bytes=12 << 20),
         name="input_grad",
-    )(place, act, gain.reshape(1, -1), parts)
+    )(place, counts, act, gain.reshape(1, -1), parts, units)
 
 
 def per_device(
     activations, norm_gain, gate_w, up_w, down_w, mask_gain, kept_blocks, kept_counts, cotangent
 ):
     me = lax.axis_index(TENSOR)
-    shards, k = jnp.arange(SHARDS), jnp.arange(2)
+    shards = jnp.arange(SHARDS)
     blocks = mask_gain.shape[0] // BLOCK
     sent = pack(me.reshape(1), kept_blocks, kept_counts, gate_w, up_w, down_w)
     got = lax.all_to_all(sent, TENSOR, split_axis=0, concat_axis=0, tiled=True)
@@ -170,7 +195,6 @@
     late, _ = lax.optimization_barrier(((cotangent, activations, mask_gain, kept_blocks, kept_counts), column))
     cotangent, act, mask_gain, kept_blocks, kept_counts = late
     kept = jnp.clip(kept_blocks[me], 0, blocks - 1)
-    first = jnp.sum(jnp.where(shards < me, kept_counts, 0))
     copies = jnp.broadcast_to(cotangent[None], (SHARDS,) + cotangent.shape)
     cot = lax.all_to_all(copies, TENSOR, split_axis=0, concat_axis=0, tiled=True)
     cot = cot.reshape(-1, cotangent.shape[1])
@@ -185,17 +209,11 @@
     parts, unit = ffn(normed, cot, unit_gain, weights)
     got = lax.all_to_all(parts, TENSOR, split_axis=0, concat_axis=0, tiled=True)
     unit = unit + lax.ppermute(unit, "core", [(0, 1), (1, 0)])
-    unit = jnp.sum(lax.all_gather(unit[:1], "z", axis=0, tiled=True), axis=0)
-    unit, got = lax.optimization_barrier((unit, got))
-    copies = jnp.broadcast_to(unit[None, None], (YH * SHARDS, 1, BLOCK))
-    units = lax.all_to_all(copies, ("yh",) + TENSOR, split_axis=0, concat_axis=0, tiled=True)
-    input_grad = final(me.reshape(1), activations, norm_gain, got)
-    width = BLOCK // (Z * YH * CORE)
-    units = lax.dynamic_slice_in_dim(units.reshape(YH * SHARDS, BLOCK), lax.axis_index(DP) * width, width, 1)
-    count = kept_counts[me]
-    owner = jnp.tile(shards, YH)
-    wanted = (owner[None] == first + k[:, None]) & (k < count)[:, None]
-    gain_grad = jnp.sum(jnp.where(wanted[:, :, None], units[None], 0.0), axis=1)
+    unit = jnp.sum(lax.all_gather(unit[:1], "z", axis=0, tiled=True), axis=0, keepdims=True)
+    unit = lax.all_gather(unit, ("yh", "yl"), axis=0, tiled=True)
+    unit = jnp.sum(unit.reshape(YH, YL, BLOCK), axis=0)
+    units = lax.all_gather(unit, "x", axis=0, tiled=True)
+    input_grad, gain_grad = final(me.reshape(1), kept_counts, activations, norm_gain, got, units)
     return input_grad, gain_grad
 
 

time: 162 us -> 165 us (1.019)
  blocking collectives: 59.7 us -> 83.7 us
  waiting for transfers between devices: 29 us -> 18.7 us
  starting transfers between devices: 31.8 us -> 22.9 us
  other arithmetic: 6.24 us -> 4.26 us
    all_gather x1 -> x3, blocking collectives: 14.8 us -> 38.8 us  [the longest x1 17.3 us: per_device(): unit = lax.all_gather(unit, ('yh', 'yl'), axis=0, tiled=True)]
    all_to_all x1 -> x0, starting transfers between devices: 8.92 us -> none  [per_device(): lax.all_to_all(copies, ('yh',) + TENSOR, split_axis=0, concat_axis=0, til...]
    all_to_all x1, waiting for transfers between devices: 6.1 us -> 0.01 us  [per_device(): got = lax.all_to_all(parts, TENSOR, split_axis=0, concat_axis=0, tiled=True)]
    all_to_all x1 -> x0, waiting for transfers between devices: 4.99 us -> none  [per_device(): lax.all_to_all(copies, ('yh',) + TENSOR, split_axis=0, concat_axis=0, til...]
  transfers between devices with their start and end apart: 6 -> 5, of which waited for: 5 -> 3; matrix products, arithmetic and copies ran while one was open for 6% -> 4% of each run, Pallas kernels for 2% -> 0%
where the time goes in v9:
time: 165 us; the launch traced here: 163 us
  blocking collectives  83.7 us (51%)
  starting transfers between devices  22.9 us (14%)
  waiting for transfers between devices  18.7 us (11%)
  between operations  15.5 us (9%)
  Pallas kernels  14 us (8%)
  other arithmetic  4.26 us (3%)
  local copies, waits for them, and re-layouts  4 us (2%)
    all_gather x1, blocking collectives, per_device(): gains = lax.all_gather(gains, TENSOR, axis=0, tiled=True)  27.9 us
    all_gather x1, blocking collectives, per_device(): unit = lax.all_gather(unit, ('yh', 'yl'), axis=0, tiled=True)  17.3 us
    all_gather x1, blocking collectives, per_device(): column = lax.all_gather(slot, 'yh', axis=0, tiled=True)  17.1 us
    all_gather x1, blocking collectives, per_device(): lax.all_gather(unit[:1], 'z', axis=0, tiled=True)  14.8 us
    all_gather x1, waiting for transfers between devices, per_device(): weights = lax.all_gather(column, ('z', 'core'), axis=0, tiled=True)  11.4 us
    all_to_all x1, starting transfers between devices, per_device(): got = lax.all_to_all(sent, TENSOR, split_axis=0, concat_axis=0, tiled=True)  9.46 us
    pallas_call x1, Pallas kernels, ffn(): pl.pallas_call(functools.partial(ffn_kernel, scale), out_shape=(jax.Shape...  7.86 us
    all_gather x1, blocking collectives, per_device(): units = lax.all_gather(unit, 'x', axis=0, tiled=True)  6.71 us
  transfers between devices with their start and end apart: 5, of which 3 were waited for; matrix products, arithmetic and copies ran while one was open for 4% of the time, Pallas kernels for 0%

profile of v9, /device:TPU:6, one launch (start us, length us, event | category | flops | bytes accessed | tf_op | source)
XLA Modules:
  0.0 162.9 jit_solution(14499599214781906380)
XLA Ops:
  7.2 0.0 copy-start
  7.2 1.3 copy.12.kept
  8.5 2.7 %pack_slots.1 = bf16[8,128,384]{2,1,0:T(8,128)(2,1)} custom-call(s32[1]{0:T(128)} %bitcast.me.place, s32[8,2]{1,0:T(8,128)} %copy.12.kept, s32[8]{0:T(128)} %counts.2, bf16[128,1792]{1,0:T(8,128)(2,1)} %g1.1, bf16[128,1792]{1,0:T(8,128)(2,1)} %g1.1, bf16[128,1792]{1,0:T(8,128)(2,1)} %u1_.1, bf16[128,1792]{1,0:T(8,128)(2,1)} %u1_.1, bf16[1792,128]{1,0:T(8,128)(2,1)} %d1.1, ...), custom_call_target="tpu_custom_call" | custom-call | tf_op jit(solution)/shard_map/pack_slots/pallas_call | solution.py:42
  11.2 9.5 %all-to-all-start = ((bf16[8,128,384]{2,1,0:T(8,128)(2,1)}), bf16[8,128,384]{2,1,0:T(8,128)(2,1)S(1)}, u32[]{:S(2)}, u32[]{:S(2)}) async-start(bf16[8,128,384]{2,1,0:T(8,128)(2,1)} %pack_slots.1), calls=%async_computation | async-start | bytes 1572864 | tf_op jit(solution)/shard_map/all_to_all | solution.py:188
  20.7 0.0 copy-done.2
  20.7 0.2 reduce-window.9
  20.9 0.6 fusion.3
  22.2 6.1 %all-to-all-done = bf16[8,128,384]{2,1,0:T(8,128)(2,1)S(1)} async-done(((bf16[8,128,384]{2,1,0:T(8,128)(2,1)}), bf16[8,128,384]{2,1,0:T(8,128)(2,1)S(1)}, u32[]{:S(2)}, u32[]{:S(2)}) %all-to-all-start) | async-done | bytes 786464 | tf_op jit(solution)/shard_map/all_to_all | solution.py:188
  28.3 17.1 %all-gather = bf16[1,512,384]{2,1,0:T(8,128)(2,1)} all-gather(bf16[1,128,384]{2,1,0:T(8,128)(2,1)S(1)} %constant_dynamic-slice_fusion.1), channel_id=2, replica_groups=mesh['z'=8,'yh'=4,'core'=2,'yl'=2,'x'=4] {'yh'}, dimensions={1}, use_global_device_ids=true | all-gather | bytes 491520 | tf_op jit(solution)/shard_map/all_gather | solution.py:192
  45.3 0.0 all-gather.9.cloned.1.call-update
  45.4 1.5 broadcast_in_dim.25
  46.9 5.8 %all-to-all-start.1 = ((bf16[8,16,8192]{2,1,0:T(8,128)(2,1)}), bf16[8,16,8192]{2,1,0:T(8,128)(2,1)}, u32[]{:S(2)}, u32[]{:S(2)}) async-start(bf16[8,16,8192]{2,1,0:T(8,128)(2,1)} %broadcast_in_dim.25), calls=%async_computation.1 | async-start | bytes 4194304 | tf_op jit(solution)/shard_map/all_to_all | solution.py:199
  52.6 0.6 fusion.4
  54.0 0.2 clamp_reduce_fusion
  54.2 0.6 gather_fusion
  54.7 0.1 fusion.6
  54.8 27.9 %all-gather.3 = bf16[8,2,128]{2,1,0:T(2,128)(2,1)S(1)} all-gather(bf16[1,2,128]{2,1,0:T(2,128)(2,1)S(1)} %fusion.6), channel_id=1, replica_groups=mesh['z'=8,'yh'=4,'core'=2,'yl'=2,'x'=4] {'yl','x'}, dimensions={0}, use_global_device_ids=true | all-gather | bytes 4608 | tf_op jit(solution)/shard_map/all_gather | solution.py:205
  82.7 0.5 constant_dynamic-slice_fusion.gain
  83.3 0.5 fusion
  83.7 2.0 %fusion.2.normed = bf16[128,8192]{1,0:T(8,128)(2,1)} fusion(bf16[128,8192]{1,0:T(8,128)(2,1)S(1)} %copy-done.1, f32[8192]{0:T(1024)S(1)} %convert_element_type.14, f32[128]{0:T(128)S(1)} %add_rsqrt_fusion), kind=kLoop, calls=%fused_computation.5 | loop fusion | flops 4194304 | bytes 4227584 | tf_op jit(solution)/shard_map/convert_element_type | solution.py:203
  85.7 0.0 all-to-all-done.1
  85.7 11.4 %all-gather.9.cloned.1.call-done = bf16[1,8192,384]{2,1,0:T(8,128)(2,1)} async-done(((bf16[1,512,384]{2,1,0:T(8,128)(2,1)}), bf16[1,8192,384]{2,1,0:T(8,128)(2,1)}) %all-gather.9.cloned.1.call-update) | async-done | bytes 6291472 | tf_op jit(solution)/shard_map/all_gather | solution.py:193
  97.2 7.9 %pruned_ffn.1 = (bf16[8,1024,128]{2,1,0:T(8,128)(2,1)}, f32[8,128]{1,0:T(8,128)}) custom-call(bf16[128,8192]{1,0:T(8,128)(2,1)} %fusion.2.normed, bf16[128,8192]{1,0:T(8,128)(2,1)} %bitcast.1.cot, bf16[1,128]{1,0:T(2,128)(2,1)} %constant_dynamic-slice_fusion.gain, bf16[8192,384]{1,0:T(8,128)(2,1)} %bitcast.26), custom_call_target="tpu_custom_call" | custom-call | tf_op jit(solution)/shard_map/pruned_ffn/pallas_call | solution.py:105
  105.0 0.0 copy-start.5
  105.1 5.7 %all-to-all-start.2 = ((bf16[8,1024,128]{2,1,0:T(8,128)(2,1)}), bf16[8,1024,128]{2,1,0:T(8,128)(2,1)}, u32[]{:S(2)}, u32[]{:S(2)}) async-start(bf16[8,1024,128]{2,1,0:T(8,128)(2,1)} %get-tuple-element.14), calls=%async_computation.2 | async-start | bytes 4194304 | tf_op jit(solution)/shard_map/all_to_all | solution.py:210
  110.8 1.9 %collective-permute-start = (f32[8,128]{1,0:T(8,128)S(1)}, f32[8,128]{1,0:T(8,128)S(1)}, u32[]{:S(2)}, u32[]{:S(2)}) collective-permute-start(f32[8,128]{1,0:T(8,128)S(1)} %copy-done.5), channel_id=1, source_target_pairs={{0,8},{8,0},{1,9},{9,1},{2,10},{10,2},{3,11},{11,3},{4,12},{12,4},... | collective-permute-start | bytes 12296 | tf_op jit(solution)/shard_map/ppermute | solution.py:211
  112.7 1.1 collective-permute-done
  113.9 14.8 %all-gather.4 = f32[8,1,128]{2,1,0:T(1,128)S(1)} all-gather(f32[1,1,128]{2,1,0:T(1,128)S(1)} %slice_bitcast_fusion), channel_id=1, replica_groups=mesh['z'=8,'yh'=4,'core'=2,'yl'=2,'x'=4] {'z'}, dimensions={0}, use_global_device_ids=true | all-gather | bytes 4608 | tf_op jit(solution)/shard_map/all_gather | solution.py:212
  128.7 17.3 %all-gather.5 = f32[8,1,128]{2,1,0:T(1,128)S(1)} all-gather(f32[1,1,128]{2,1,0:T(1,128)S(1)} %bitcast.30), channel_id=4, replica_groups=mesh['z'=8,'yh'=4,'core'=2,'yl'=2,'x'=4] {'yh','yl'}, dimensions={0}, use_global_device_ids=true | all-gather | bytes 4608 | tf_op jit(solution)/shard_map/all_gather | solution.py:213
  146.0 6.7 %all-gather.6 = f32[4,2,128]{2,1,0:T(2,128)S(1)} all-gather(f32[1,2,128]{2,1,0:T(2,128)S(1)} %bitcast.29), channel_id=1, replica_groups=mesh['z'=8,'yh'=4,'core'=2,'yl'=2,'x'=4] {'x'}, dimensions={0}, use_global_device_ids=true | all-gather | bytes 5120 | tf_op jit(solution)/shard_map/all_gather | solution.py:215
  152.7 0.0 all-to-all-done.2.parts
  152.7 3.4 %input_grad.1 = (bf16[16,8192]{1,0:T(8,128)(2,1)}, f32[2,2]{1,0:T(2,128)}) custom-call(s32[1]{0:T(128)} %bitcast.me.place, s32[8]{0:T(128)S(1)} %copy-done.2, bf16[128,8192]{1,0:T(8,128)(2,1)S(1)} %copy-done.1, bf16[1,8192]{1,0:T(2,128)(2,1)S(1)} %reshape.90.gain, bf16[8,1024,128]{2,1,0:T(8,128)(2,1)} %all-to-all-done.2.parts, f32[8,128]{1,0:T(8,128)S(1)} %bitcast.24), custom_call_target="tpu_custom_call" | custom-call | tf_op jit(solution)/shard_map/input_grad/pallas_call | solution.py:156
  (23 shorter events, 0.1 us)
Async XLA Ops:
  7.2 47.0 %copy-start = (bf16[1792]{0:T(1024)(128)(2,1)S(1)}, bf16[1792]{0:T(1024)(128)(2,1)}, u32[]{:S(2)}) copy-start(bf16[1792]{0:T(1024)(128)(2,1)} %param.14) | copy-start | bytes 10756
  8.5 12.2 %copy-start.2 = (s32[8]{0:T(128)S(1)}, s32[8]{0:T(128)}, u32[]{:S(2)}) copy-start(s32[8]{0:T(128)} %counts.2) | copy-start | bytes 100
  11.2 34.1 %copy-start.3 = (bf16[16,8192]{1,0:T(8,128)(2,1)S(1)}, bf16[16,8192]{1,0:T(8,128)(2,1)}, u32[]{:S(2)}) copy-start(bf16[16,8192]{1,0:T(8,128)(2,1)} %param.17) | copy-start | bytes 786436
  11.2 17.0 %all-to-all-start = ((bf16[8,128,384]{2,1,0:T(8,128)(2,1)}), bf16[8,128,384]{2,1,0:T(8,128)(2,1)S(1)}, u32[]{:S(2)}, u32[]{:S(2)}) async-start(bf16[8,128,384]{2,1,0:T(8,128)(2,1)} %pack_slots.1), calls=%async_computation | async-start | bytes 1572864 | tf_op jit(solution)/shard_map/all_to_all | solution.py:188
  20.7 76.5 %all-gather.9.cloned.1.call-start = ((), (), s32[]{:S(2)}) async-start(), calls=%async_computation.3 | async-start | bytes 6684672 | tf_op jit(solution)/shard_map/all_gather | solution.py:193
  46.9 7.1 %copy-start.4 = (bf16[8192]{0:T(1024)(128)(2,1)S(1)}, bf16[8192]{0:T(1024)(128)(2,1)}, u32[]{:S(2)}) copy-start(bf16[8192]{0:T(1024)(128)(2,1)} %param.10) | copy-start | bytes 49156
  46.9 7.1 %copy-start.6 = (s32[8,2]{0,1:T(2,128)S(1)}, s32[8,2]{0,1:T(2,128)}, u32[]{:S(2)}) copy-start(s32[8,2]{0,1:T(2,128)} %param.15) | copy-start | bytes 196
  46.9 36.4 %copy-start.1 = (bf16[128,8192]{1,0:T(8,128)(2,1)S(1)}, bf16[128,8192]{1,0:T(8,128)(2,1)}, u32[]{:S(2)}) copy-start(bf16[128,8192]{1,0:T(8,128)(2,1)} %act.1) | copy-start | bytes 6291460
  46.9 38.9 %all-to-all-start.1 = ((bf16[8,16,8192]{2,1,0:T(8,128)(2,1)}), bf16[8,16,8192]{2,1,0:T(8,128)(2,1)}, u32[]{:S(2)}, u32[]{:S(2)}) async-start(bf16[8,16,8192]{2,1,0:T(8,128)(2,1)} %broadcast_in_dim.25), calls=%async_computation.1 | async-start | bytes 4194304 | tf_op jit(solution)/shard_map/all_to_all | solution.py:199
  105.0 5.8 %copy-start.5 = (f32[8,128]{1,0:T(8,128)S(1)}, f32[8,128]{1,0:T(8,128)}, u32[]{:S(2)}) copy-start(f32[8,128]{1,0:T(8,128)} %get-tuple-element.15) | copy-start | bytes 12292
  105.1 47.6 %all-to-all-start.2 = ((bf16[8,1024,128]{2,1,0:T(8,128)(2,1)}), bf16[8,1024,128]{2,1,0:T(8,128)(2,1)}, u32[]{:S(2)}, u32[]{:S(2)}) async-start(bf16[8,1024,128]{2,1,0:T(8,128)(2,1)} %get-tuple-element.14), calls=%async_computation.2 | async-start | bytes 4194304 | tf_op jit(solution)/shard_map/all_to_all | solution.py:210
  110.8 3.0 %collective-permute-start = (f32[8,128]{1,0:T(8,128)S(1)}, f32[8,128]{1,0:T(8,128)S(1)}, u32[]{:S(2)}, u32[]{:S(2)}) collective-permute-start(f32[8,128]{1,0:T(8,128)S(1)} %copy-done.5), channel_id=1, source_target_pairs={{0,8},{8,0},{1,9},{9,1},{2,10},{10,2},{3,11},{11,3},{4,12},{12,4},... | collective-permute-start | bytes 12296 | tf_op jit(solution)/shard_map/ppermute | solution.py:211
Sparse Core Ops, SparseCore 0:
  45.5 51.6 all-gather.8

commit v10 on v9

--- a/solution.py
+++ b/solution.py
@@ -207,11 +207,12 @@
     unit_gain = lax.dynamic_slice_in_dim(gains, source * 2 + jnp.clip(which, 0, 1), 1, 0)
 
     parts, unit = ffn(normed, cot, unit_gain, weights)
+    unit = lax.all_gather(unit[:1], ("yh", "yl"), axis=0, tiled=True)
+    unit = jnp.sum(unit.reshape(YH, YL, BLOCK), axis=0)
+    parts, unit = lax.optimization_barrier((parts, unit))
     got = lax.all_to_all(parts, TENSOR, split_axis=0, concat_axis=0, tiled=True)
     unit = unit + lax.ppermute(unit, "core", [(0, 1), (1, 0)])
-    unit = jnp.sum(lax.all_gather(unit[:1], "z", axis=0, tiled=True), axis=0, keepdims=True)
-    unit = lax.all_gather(unit, ("yh", "yl"), axis=0, tiled=True)
-    unit = jnp.sum(unit.reshape(YH, YL, BLOCK), axis=0)
+    unit = jnp.sum(lax.all_gather(unit, "z", axis=0, tiled=True).reshape(Z, YL, BLOCK), axis=0)
     units = lax.all_gather(unit, "x", axis=0, tiled=True)
     input_grad, gain_grad = final(me.reshape(1), kept_counts, activations, norm_gain, got, units)
     return input_grad, gain_grad

time: 165 us -> 165 us (level)
  the two profiles are of different devices: /device:TPU:6 before, /device:TPU:8 now
where the time goes in v10:
time: 165 us; the launch traced here: 164 us
  blocking collectives  86.5 us (52%)
  starting transfers between devices  21.8 us (13%)
  waiting for transfers between devices  17.7 us (11%)
  between operations  15.5 us (9%)
  Pallas kernels  14 us (8%)
  local copies, waits for them, and re-layouts  4.68 us (3%)
  other arithmetic  4.25 us (3%)
    all_gather x1, blocking collectives, per_device(): gains = lax.all_gather(gains, TENSOR, axis=0, tiled=True)  29.9 us
    all_gather x1, blocking collectives, per_device(): column = lax.all_gather(slot, 'yh', axis=0, tiled=True)  17.3 us
    all_gather x1, blocking collectives, per_device(): lax.all_gather(unit, 'z', axis=0, tiled=True).reshape(Z, YL, BLOCK)  14.9 us
    all_gather x1, blocking collectives, per_device(): unit = lax.all_gather(unit[:1], ('yh', 'yl'), axis=0, tiled=True)  14.7 us
    all_gather x1, blocking collectives, per_device(): units = lax.all_gather(unit, 'x', axis=0, tiled=True)  9.64 us
    all_to_all x1, starting transfers between devices, per_device(): got = lax.all_to_all(sent, TENSOR, split_axis=0, concat_axis=0, tiled=True)  9.42 us
    all_gather x1, waiting for transfers between devices, per_device(): weights = lax.all_gather(column, ('z', 'core'), axis=0, tiled=True)  9.42 us
    pallas_call x1, Pallas kernels, ffn(): pl.pallas_call(functools.partial(ffn_kernel, scale), out_shape=(jax.Shape...  7.87 us
  transfers between devices with their start and end apart: 5, of which 3 were waited for; matrix products, arithmetic and copies ran while one was open for 4% of the time, Pallas kernels for 0%

profile of v10, /device:TPU:8, one launch (start us, length us, event | category | flops | bytes accessed | tf_op | source)
XLA Modules:
  0.0 164.4 jit_solution(9823259638833266238)
XLA Ops:
  7.2 0.0 copy-start
  7.2 1.3 copy.12.kept
  8.5 2.7 %pack_slots.1 = bf16[8,128,384]{2,1,0:T(8,128)(2,1)} custom-call(s32[1]{0:T(128)} %bitcast.me.place, s32[8,2]{1,0:T(8,128)} %copy.12.kept, s32[8]{0:T(128)} %counts.2, bf16[128,1792]{1,0:T(8,128)(2,1)} %g1.1, bf16[128,1792]{1,0:T(8,128)(2,1)} %g1.1, bf16[128,1792]{1,0:T(8,128)(2,1)} %u1_.1, bf16[128,1792]{1,0:T(8,128)(2,1)} %u1_.1, bf16[1792,128]{1,0:T(8,128)(2,1)} %d1.1, ...), custom_call_target="tpu_custom_call" | custom-call | tf_op jit(solution)/shard_map/pack_slots/pallas_call | solution.py:42
  11.2 9.4 %all-to-all-start = ((bf16[8,128,384]{2,1,0:T(8,128)(2,1)}), bf16[8,128,384]{2,1,0:T(8,128)(2,1)S(1)}, u32[]{:S(2)}, u32[]{:S(2)}) async-start(bf16[8,128,384]{2,1,0:T(8,128)(2,1)} %pack_slots.1), calls=%async_computation | async-start | bytes 1572864 | tf_op jit(solution)/shard_map/all_to_all | solution.py:188
  20.6 0.0 copy-done.2
  20.6 0.2 reduce-window.9
  20.8 0.6 fusion.3
  22.1 7.2 %all-to-all-done = bf16[8,128,384]{2,1,0:T(8,128)(2,1)S(1)} async-done(((bf16[8,128,384]{2,1,0:T(8,128)(2,1)}), bf16[8,128,384]{2,1,0:T(8,128)(2,1)S(1)}, u32[]{:S(2)}, u32[]{:S(2)}) %all-to-all-start) | async-done | bytes 786464 | tf_op jit(solution)/shard_map/all_to_all | solution.py:188
  29.3 17.3 %all-gather = bf16[1,512,384]{2,1,0:T(8,128)(2,1)} all-gather(bf16[1,128,384]{2,1,0:T(8,128)(2,1)S(1)} %constant_dynamic-slice_fusion.1), channel_id=2, replica_groups=mesh['z'=8,'yh'=4,'core'=2,'yl'=2,'x'=4] {'yh'}, dimensions={1}, use_global_device_ids=true | all-gather | bytes 491520 | tf_op jit(solution)/shard_map/all_gather | solution.py:192
  46.6 0.0 all-gather.8.cloned.1.call-update
  46.6 1.5 broadcast_in_dim.22
  48.1 4.5 %all-to-all-start.1 = ((bf16[8,16,8192]{2,1,0:T(8,128)(2,1)}), bf16[8,16,8192]{2,1,0:T(8,128)(2,1)}, u32[]{:S(2)}, u32[]{:S(2)}) async-start(bf16[8,16,8192]{2,1,0:T(8,128)(2,1)} %broadcast_in_dim.22), calls=%async_computation.1 | async-start | bytes 4194304 | tf_op jit(solution)/shard_map/all_to_all | solution.py:199
  52.6 0.6 fusion.4
  53.9 0.2 clamp_reduce_fusion
  54.1 0.6 gather_fusion
  54.7 0.1 fusion.6
  54.8 29.9 %all-gather.2 = bf16[8,2,128]{2,1,0:T(2,128)(2,1)S(1)} all-gather(bf16[1,2,128]{2,1,0:T(2,128)(2,1)S(1)} %fusion.6), channel_id=1, replica_groups=mesh['z'=8,'yh'=4,'core'=2,'yl'=2,'x'=4] {'yl','x'}, dimensions={0}, use_global_device_ids=true | all-gather | bytes 4608 | tf_op jit(solution)/shard_map/all_gather | solution.py:205
  84.7 0.5 constant_dynamic-slice_fusion.gain
  85.3 0.5 fusion
  85.8 2.0 %fusion.2.normed = bf16[128,8192]{1,0:T(8,128)(2,1)} fusion(bf16[128,8192]{1,0:T(8,128)(2,1)S(1)} %copy-done.1, f32[8192]{0:T(1024)S(1)} %convert_element_type.14, f32[128]{0:T(128)S(1)} %add_rsqrt_fusion), kind=kLoop, calls=%fused_computation.5 | loop fusion | flops 4194304 | bytes 4227584 | tf_op jit(solution)/shard_map/convert_element_type | solution.py:203
  87.7 0.0 all-to-all-done.1
  87.7 9.4 %all-gather.8.cloned.1.call-done = bf16[1,8192,384]{2,1,0:T(8,128)(2,1)} async-done(((bf16[1,512,384]{2,1,0:T(8,128)(2,1)}), bf16[1,8192,384]{2,1,0:T(8,128)(2,1)}) %all-gather.8.cloned.1.call-update) | async-done | bytes 6291472 | tf_op jit(solution)/shard_map/all_gather | solution.py:193
  97.2 7.9 %pruned_ffn.1 = (bf16[8,1024,128]{2,1,0:T(8,128)(2,1)}, f32[8,128]{1,0:T(8,128)}) custom-call(bf16[128,8192]{1,0:T(8,128)(2,1)} %fusion.2.normed, bf16[128,8192]{1,0:T(8,128)(2,1)} %bitcast.1.cot, bf16[1,128]{1,0:T(2,128)(2,1)} %constant_dynamic-slice_fusion.gain, bf16[8192,384]{1,0:T(8,128)(2,1)} %bitcast.27), custom_call_target="tpu_custom_call" | custom-call | tf_op jit(solution)/shard_map/pruned_ffn/pallas_call | solution.py:105
  105.0 0.7 slice_bitcast_fusion
  105.7 14.7 %all-gather.3 = f32[8,1,128]{2,1,0:T(1,128)S(1)} all-gather(f32[1,1,128]{2,1,0:T(1,128)S(1)} %slice_bitcast_fusion), channel_id=1, replica_groups=mesh['z'=8,'yh'=4,'core'=2,'yl'=2,'x'=4] {'yh','yl'}, dimensions={0}, use_global_device_ids=true | all-gather | bytes 4608 | tf_op jit(solution)/shard_map/all_gather | solution.py:210
  120.5 6.0 %all-to-all-start.2 = ((bf16[8,1024,128]{2,1,0:T(8,128)(2,1)}), bf16[8,1024,128]{2,1,0:T(8,128)(2,1)}, u32[]{:S(2)}, u32[]{:S(2)}) async-start(bf16[8,1024,128]{2,1,0:T(8,128)(2,1)} %get-tuple-element.18), calls=%async_computation.2 | async-start | bytes 4194304 | tf_op jit(solution)/shard_map/all_to_all | solution.py:213
  126.5 1.9 %collective-permute-start = (f32[2,128]{1,0:T(2,128)S(1)}, f32[2,128]{1,0:T(2,128)S(1)}, u32[]{:S(2)}, u32[]{:S(2)}) collective-permute-start(f32[2,128]{1,0:T(2,128)S(1)} %reduce_sum.48), channel_id=1, source_target_pairs={{0,8},{8,0},{1,9},{9,1},{2,10},{10,2},{3,11},{11,3},{4,12},{12,4},... | collective-permute-start | bytes 3080 | tf_op jit(solution)/shard_map/ppermute | solution.py:214
  128.5 1.1 collective-permute-done
  129.5 14.9 %all-gather.4 = f32[8,2,128]{2,1,0:T(2,128)S(1)} all-gather(f32[1,2,128]{2,1,0:T(2,128)S(1)} %add_bitcast_fusion), channel_id=1, replica_groups=mesh['z'=8,'yh'=4,'core'=2,'yl'=2,'x'=4] {'z'}, dimensions={0}, use_global_device_ids=true | all-gather | bytes 9216 | tf_op jit(solution)/shard_map/all_gather | solution.py:215
  144.5 9.6 %all-gather.5 = f32[4,2,128]{2,1,0:T(2,128)S(1)} all-gather(f32[1,2,128]{2,1,0:T(2,128)S(1)} %bitcast.29), channel_id=1, replica_groups=mesh['z'=8,'yh'=4,'core'=2,'yl'=2,'x'=4] {'x'}, dimensions={0}, use_global_device_ids=true | all-gather | bytes 5120 | tf_op jit(solution)/shard_map/all_gather | solution.py:216
  154.1 0.0 all-to-all-done.2.parts
  154.1 3.4 %input_grad.1 = (bf16[16,8192]{1,0:T(8,128)(2,1)}, f32[2,2]{1,0:T(2,128)}) custom-call(s32[1]{0:T(128)} %bitcast.me.place, s32[8]{0:T(128)S(1)} %copy-done.2, bf16[128,8192]{1,0:T(8,128)(2,1)S(1)} %copy-done.1, bf16[1,8192]{1,0:T(2,128)(2,1)S(1)} %reshape.93.gain, bf16[8,1024,128]{2,1,0:T(8,128)(2,1)} %all-to-all-done.2.parts, f32[8,128]{1,0:T(8,128)S(1)} %bitcast.25), custom_call_target="tpu_custom_call" | custom-call | tf_op jit(solution)/shard_map/input_grad/pallas_call | solution.py:156
  (21 shorter events, 0.1 us)
Async XLA Ops:
  7.2 47.0 %copy-start = (bf16[1792]{0:T(1024)(128)(2,1)S(1)}, bf16[1792]{0:T(1024)(128)(2,1)}, u32[]{:S(2)}) copy-start(bf16[1792]{0:T(1024)(128)(2,1)} %param.14) | copy-start | bytes 10756
  8.5 12.1 %copy-start.2 = (s32[8]{0:T(128)S(1)}, s32[8]{0:T(128)}, u32[]{:S(2)}) copy-start(s32[8]{0:T(128)} %counts.2) | copy-start | bytes 100
  11.2 35.4 %copy-start.3 = (bf16[16,8192]{1,0:T(8,128)(2,1)S(1)}, bf16[16,8192]{1,0:T(8,128)(2,1)}, u32[]{:S(2)}) copy-start(bf16[16,8192]{1,0:T(8,128)(2,1)} %param.17) | copy-start | bytes 786436
  11.2 18.1 %all-to-all-start = ((bf16[8,128,384]{2,1,0:T(8,128)(2,1)}), bf16[8,128,384]{2,1,0:T(8,128)(2,1)S(1)}, u32[]{:S(2)}, u32[]{:S(2)}) async-start(bf16[8,128,384]{2,1,0:T(8,128)(2,1)} %pack_slots.1), calls=%async_computation | async-start | bytes 1572864 | tf_op jit(solution)/shard_map/all_to_all | solution.py:188
  20.6 76.5 %all-gather.8.cloned.1.call-start = ((), (), s32[]{:S(2)}) async-start(), calls=%async_computation.3 | async-start | bytes 6684672 | tf_op jit(solution)/shard_map/all_gather | solution.py:193
  48.1 5.8 %copy-start.4 = (bf16[8192]{0:T(1024)(128)(2,1)S(1)}, bf16[8192]{0:T(1024)(128)(2,1)}, u32[]{:S(2)}) copy-start(bf16[8192]{0:T(1024)(128)(2,1)} %param.10) | copy-start | bytes 49156
  48.1 5.8 %copy-start.5 = (s32[8,2]{0,1:T(2,128)S(1)}, s32[8,2]{0,1:T(2,128)}, u32[]{:S(2)}) copy-start(s32[8,2]{0,1:T(2,128)} %param.15) | copy-start | bytes 196
  48.1 37.1 %copy-start.1 = (bf16[128,8192]{1,0:T(8,128)(2,1)S(1)}, bf16[128,8192]{1,0:T(8,128)(2,1)}, u32[]{:S(2)}) copy-start(bf16[128,8192]{1,0:T(8,128)(2,1)} %act.1) | copy-start | bytes 6291460
  48.1 39.6 %all-to-all-start.1 = ((bf16[8,16,8192]{2,1,0:T(8,128)(2,1)}), bf16[8,16,8192]{2,1,0:T(8,128)(2,1)}, u32[]{:S(2)}, u32[]{:S(2)}) async-start(bf16[8,16,8192]{2,1,0:T(8,128)(2,1)} %broadcast_in_dim.22), calls=%async_computation.1 | async-start | bytes 4194304 | tf_op jit(solution)/shard_map/all_to_all | solution.py:199
  120.5 33.6 %all-to-all-start.2 = ((bf16[8,1024,128]{2,1,0:T(8,128)(2,1)}), bf16[8,1024,128]{2,1,0:T(8,128)(2,1)}, u32[]{:S(2)}, u32[]{:S(2)}) async-start(bf16[8,1024,128]{2,1,0:T(8,128)(2,1)} %get-tuple-element.18), calls=%async_computation.2 | async-start | bytes 4194304 | tf_op jit(solution)/shard_map/all_to_all | solution.py:213
  126.5 3.0 %collective-permute-start = (f32[2,128]{1,0:T(2,128)S(1)}, f32[2,128]{1,0:T(2,128)S(1)}, u32[]{:S(2)}, u32[]{:S(2)}) collective-permute-start(f32[2,128]{1,0:T(2,128)S(1)} %reduce_sum.48), channel_id=1, source_target_pairs={{0,8},{8,0},{1,9},{9,1},{2,10},{10,2},{3,11},{11,3},{4,12},{12,4},... | collective-permute-start | bytes 3080 | tf_op jit(solution)/shard_map/ppermute | solution.py:214
Sparse Core Ops, SparseCore 0:
  46.7 50.3 all-gather.7

commit v11 on v5

--- a/solution.py
+++ b/solution.py
@@ -66,17 +66,16 @@
     gate_up = jnp.zeros((tokens, 2 * BLOCK), F32)
     hidden = jnp.zeros((tokens, BLOCK), F32)
     rows = [
-        [((z * CORE + core) * YH + yh) * BLOCK for core in range(CORE)]
-        for z in range(Z) for yh in range(YH)
+        [((z * CORE + core) * YH + yh) * BLOCK for yh in range(YH) for core in range(CORE)]
+        for z in range(Z)
     ]
-    wide = CORE * BLOCK
-    for i, pair in enumerate(rows):
-        if i % YH == 0:
-            for one in copies[3 * (i // YH) : 3 * (i // YH) + 3]:
-                one.wait()
-        w2 = jnp.concatenate([w_buf[row : row + BLOCK, :] for row in pair], axis=0)
-        gate_up += jnp.dot(n_buf[:, i * wide : (i + 1) * wide], w2[:, : 2 * BLOCK], preferred_element_type=F32)
-        hidden += jnp.dot(c_buf[:, i * wide : (i + 1) * wide], w2[:, 2 * BLOCK :], preferred_element_type=F32)
+    for i, group in enumerate(rows):
+        for one in copies[3 * i : 3 * i + 3]:
+            one.wait()
+        w = jnp.concatenate([w_buf[row : row + BLOCK, :] for row in group], axis=0)
+        cols = slice(i * chunk, (i + 1) * chunk)
+        gate_up += jnp.dot(n_buf[:, cols], w[:, : 2 * BLOCK], preferred_element_type=F32)
+        hidden += jnp.dot(c_buf[:, cols], w[:, 2 * BLOCK :], preferred_element_type=F32)
     gate, up = gate_up[:, :BLOCK], gate_up[:, BLOCK:]
     sig = jax.nn.sigmoid(gate)
     unit = jnp.sum(gate * sig * up * hidden, axis=0, keepdims=True) * scale
@@ -86,12 +85,12 @@
     up_grad = (masked * gate * sig).astype(BF)
     grads = jnp.concatenate([gate_grad, up_grad], axis=1)
     share = tokens // SHARDS
-    for i, pair in enumerate(rows):
-        w2 = jnp.concatenate([w_buf[row : row + BLOCK, : 2 * BLOCK] for row in pair], axis=0)
-        part = lax.dot_general(grads, w2, NT, preferred_element_type=F32).astype(BF)
-        for core in range(CORE):
-            block = part[:, core * BLOCK : (core + 1) * BLOCK].reshape(SHARDS, share, BLOCK)
-            first = (i * CORE + core) * share
+    for i, group in enumerate(rows):
+        w = jnp.concatenate([w_buf[row : row + BLOCK, : 2 * BLOCK] for row in group], axis=0)
+        part = lax.dot_general(grads, w, NT, preferred_element_type=F32).astype(BF)
+        for j in range(len(group)):
+            block = part[:, j * BLOCK : (j + 1) * BLOCK].reshape(SHARDS, share, BLOCK)
+            first = (i * len(group) + j) * share
             out[:, first : first + share, :] = block
 
 

time: 162 us -> 162 us (level)
  no operation moved by 1% of the time
where the time goes in v11:
time: 162 us; the launch traced here: 161 us
  blocking collectives  59.7 us (37%)
  starting transfers between devices  31.8 us (20%)
  waiting for transfers between devices  29 us (18%)
  between operations  15.5 us (10%)
  Pallas kernels  13.4 us (8%)
  other arithmetic  6.24 us (4%)
  local copies, waits for them, and re-layouts  5.52 us (3%)
    all_gather x1, blocking collectives, per_device(): gains = lax.all_gather(gains, TENSOR, axis=0, tiled=True)  27.8 us
    all_gather x1, blocking collectives, per_device(): column = lax.all_gather(slot, 'yh', axis=0, tiled=True)  17.1 us
    all_gather x1, blocking collectives, per_device(): unit = jnp.sum(lax.all_gather(unit[:1], 'z', axis=0, tiled=True), axis=0)  14.8 us
    all_gather x1, waiting for transfers between devices, per_device(): weights = lax.all_gather(column, ('z', 'core'), axis=0, tiled=True)  11.5 us
    all_to_all x1, starting transfers between devices, per_device(): got = lax.all_to_all(sent, TENSOR, split_axis=0, concat_axis=0, tiled=True)  9.44 us
    all_to_all x1, starting transfers between devices, per_device(): lax.all_to_all(copies, ('yh',) + TENSOR, split_axis=0, concat_axis=0, til...  8.91 us
    pallas_call x1, Pallas kernels, ffn(): pl.pallas_call(functools.partial(ffn_kernel, scale), out_shape=(jax.Shape...  7.9 us
    all_to_all x1, waiting for transfers between devices, per_device(): got = lax.all_to_all(parts, TENSOR, split_axis=0, concat_axis=0, tiled=True)  6.11 us
  transfers between devices with their start and end apart: 6, of which 5 were waited for; matrix products, arithmetic and copies ran while one was open for 6% of the time, Pallas kernels for 2%

profile of v11, /device:TPU:6, one launch (start us, length us, event | category | flops | bytes accessed | tf_op | source)
XLA Modules:
  0.0 161.2 jit_solution(14744917738689015861)
XLA Ops:
  7.2 1.3 copy.16.kept
  8.5 2.7 %pack_slots.1 = bf16[8,128,384]{2,1,0:T(8,128)(2,1)} custom-call(s32[1]{0:T(128)} %bitcast.me.place, s32[8,2]{1,0:T(8,128)} %copy.16.kept, s32[8]{0:T(128)} %counts.1, bf16[128,1792]{1,0:T(8,128)(2,1)} %g1.1, bf16[128,1792]{1,0:T(8,128)(2,1)} %g1.1, bf16[128,1792]{1,0:T(8,128)(2,1)} %u1_.1, bf16[128,1792]{1,0:T(8,128)(2,1)} %u1_.1, bf16[1792,128]{1,0:T(8,128)(2,1)} %d1.1, ...), custom_call_target="tpu_custom_call" | custom-call | tf_op jit(solution)/shard_map/pack_slots/pallas_call | solution.py:42
  11.2 9.4 %all-to-all-start = ((bf16[8,128,384]{2,1,0:T(8,128)(2,1)}), bf16[8,128,384]{2,1,0:T(8,128)(2,1)S(1)}, u32[]{:S(2)}, u32[]{:S(2)}) async-start(bf16[8,128,384]{2,1,0:T(8,128)(2,1)} %pack_slots.1), calls=%async_computation | async-start | bytes 1572864 | tf_op jit(solution)/shard_map/all_to_all | solution.py:162
  20.7 0.2 reduce-window.9
  20.9 0.6 fusion.3
  22.1 6.1 %all-to-all-done = bf16[8,128,384]{2,1,0:T(8,128)(2,1)S(1)} async-done(((bf16[8,128,384]{2,1,0:T(8,128)(2,1)}), bf16[8,128,384]{2,1,0:T(8,128)(2,1)S(1)}, u32[]{:S(2)}, u32[]{:S(2)}) %all-to-all-start) | async-done | bytes 786464 | tf_op jit(solution)/shard_map/all_to_all | solution.py:162
  28.3 17.1 %all-gather = bf16[1,512,384]{2,1,0:T(8,128)(2,1)} all-gather(bf16[1,128,384]{2,1,0:T(8,128)(2,1)S(1)} %constant_dynamic-slice_fusion.2), channel_id=2, replica_groups=mesh['z'=8,'yh'=4,'core'=2,'yl'=2,'x'=4] {'yh'}, dimensions={1}, use_global_device_ids=true | all-gather | bytes 491520 | tf_op jit(solution)/shard_map/all_gather | solution.py:166
  45.4 1.5 broadcast_in_dim.55
  46.9 5.8 %all-to-all-start.1 = ((bf16[8,16,8192]{2,1,0:T(8,128)(2,1)}), bf16[8,16,8192]{2,1,0:T(8,128)(2,1)}, u32[]{:S(2)}, u32[]{:S(2)}) async-start(bf16[8,16,8192]{2,1,0:T(8,128)(2,1)} %broadcast_in_dim.55), calls=%async_computation.1 | async-start | bytes 4194304 | tf_op jit(solution)/shard_map/all_to_all | solution.py:174
  52.7 0.7 fusion.5
  54.1 0.2 clamp_reduce_fusion
  54.3 0.6 gather_fusion
  54.9 27.8 %all-gather.2 = bf16[8,2,128]{2,1,0:T(2,128)(2,1)S(1)} all-gather(bf16[1,2,128]{2,1,0:T(2,128)(2,1)S(1)} %fusion.7), channel_id=1, replica_groups=mesh['z'=8,'yh'=4,'core'=2,'yl'=2,'x'=4] {'yl','x'}, dimensions={0}, use_global_device_ids=true | all-gather | bytes 4608 | tf_op jit(solution)/shard_map/all_gather | solution.py:180
  82.8 0.5 constant_dynamic-slice_fusion.1.gain
  83.3 0.5 fusion
  83.8 1.9 %fusion.2.normed = bf16[128,8192]{1,0:T(8,128)(2,1)} fusion(bf16[128,8192]{1,0:T(8,128)(2,1)S(1)} %copy-done.1, f32[8192]{0:T(1024)S(1)} %convert_element_type.14, f32[128]{0:T(128)S(1)} %add_rsqrt_fusion), kind=kLoop, calls=%fused_computation.5 | loop fusion | flops 4194304 | bytes 4227584 | tf_op jit(solution)/shard_map/convert_element_type | solution.py:178
  85.7 11.5 %all-gather.6.cloned.1.call-done = bf16[1,8192,384]{2,1,0:T(8,128)(2,1)} async-done(((bf16[1,512,384]{2,1,0:T(8,128)(2,1)}), bf16[1,8192,384]{2,1,0:T(8,128)(2,1)}) %all-gather.6.cloned.1.call-update) | async-done | bytes 6291472 | tf_op jit(solution)/shard_map/all_gather | solution.py:167
  97.2 7.9 %pruned_ffn.1 = (bf16[8,1024,128]{2,1,0:T(8,128)(2,1)}, f32[8,128]{1,0:T(8,128)}) custom-call(bf16[128,8192]{1,0:T(8,128)(2,1)} %fusion.2.normed, bf16[128,8192]{1,0:T(8,128)(2,1)} %bitcast.1.cot, bf16[1,128]{1,0:T(2,128)(2,1)} %constant_dynamic-slice_fusion.1.gain, bf16[8192,384]{1,0:T(8,128)(2,1)} %bitcast.22), custom_call_target="tpu_custom_call" | custom-call | tf_op jit(solution)/shard_map/pruned_ffn/pallas_call | solution.py:104
  105.1 5.7 %all-to-all-start.2 = ((bf16[8,1024,128]{2,1,0:T(8,128)(2,1)}), bf16[8,1024,128]{2,1,0:T(8,128)(2,1)}, u32[]{:S(2)}, u32[]{:S(2)}) async-start(bf16[8,1024,128]{2,1,0:T(8,128)(2,1)} %get-tuple-element.17), calls=%async_computation.2 | async-start | bytes 4194304 | tf_op jit(solution)/shard_map/all_to_all | solution.py:185
  110.8 0.6 dynamic_slice.19
  111.4 0.6 iota_compare_fusion
  112.1 1.9 %collective-permute-start = (f32[8,128]{1,0:T(8,128)S(1)}, f32[8,128]{1,0:T(8,128)S(1)}, u32[]{:S(2)}, u32[]{:S(2)}) collective-permute-start(f32[8,128]{1,0:T(8,128)S(1)} %copy-done.4), channel_id=1, source_target_pairs={{0,8},{8,0},{1,9},{9,1},{2,10},{10,2},{3,11},{11,3},{4,12},{12,4},... | collective-permute-start | bytes 12296 | tf_op jit(solution)/shard_map/ppermute | solution.py:186
  114.0 0.7 iota_add_fusion
  114.8 0.4 collective-permute-done
  115.1 14.8 %all-gather.3 = f32[8,1,128]{2,1,0:T(1,128)S(1)} all-gather(f32[1,1,128]{2,1,0:T(1,128)S(1)} %slice_bitcast_fusion), channel_id=1, replica_groups=mesh['z'=8,'yh'=4,'core'=2,'yl'=2,'x'=4] {'z'}, dimensions={0}, use_global_device_ids=true | all-gather | bytes 4608 | tf_op jit(solution)/shard_map/all_gather | solution.py:187
  129.9 6.1 %all-to-all-done.2.parts = bf16[8,1024,128]{2,1,0:T(8,128)(2,1)} async-done(((bf16[8,1024,128]{2,1,0:T(8,128)(2,1)}), bf16[8,1024,128]{2,1,0:T(8,128)(2,1)}, u32[]{:S(2)}, u32[]{:S(2)}) %all-to-all-start.2) | async-done | bytes 2097184 | tf_op jit(solution)/shard_map/all_to_all | solution.py:185
  136.1 0.6 broadcast_in_dim.60
  136.7 8.9 %all-to-all-start.3 = ((f32[32,1,128]{2,1,0:T(1,128)}), f32[32,1,128]{2,1,0:T(1,128)S(1)}, u32[]{:S(2)}, u32[]{:S(2)}) async-start(f32[32,1,128]{2,1,0:T(1,128)} %broadcast_in_dim.60), calls=%async_computation.3 | async-start | bytes 32768 | tf_op jit(solution)/shard_map/all_to_all | solution.py:190
  145.7 2.9 %input_grad.1 = bf16[16,8192]{1,0:T(8,128)(2,1)} custom-call(s32[1]{0:T(128)} %bitcast.me.place, bf16[128,8192]{1,0:T(8,128)(2,1)S(1)} %copy-done.1, bf16[1,8192]{1,0:T(2,128)(2,1)S(1)} %reshape.145.gain, bf16[8,1024,128]{2,1,0:T(8,128)(2,1)} %all-to-all-done.2.parts), custom_call_target="tpu_custom_call" | custom-call | tf_op jit(solution)/shard_map/input_grad/pallas_call | solution.py:137
  148.5 5.0 %all-to-all-done.3 = f32[32,1,128]{2,1,0:T(1,128)S(1)} async-done(((f32[32,1,128]{2,1,0:T(1,128)}), f32[32,1,128]{2,1,0:T(1,128)S(1)}, u32[]{:S(2)}, u32[]{:S(2)}) %all-to-all-start.3) | async-done | bytes 16416 | tf_op jit(solution)/shard_map/all_to_all | solution.py:190
  153.5 0.1 constant_dynamic-slice_fusion
  153.7 0.7 select_reduce_fusion
  (32 shorter events, 0.5 us)
Async XLA Ops:
  7.2 47.1 %copy-start = (bf16[1792]{0:T(1024)(128)(2,1)S(1)}, bf16[1792]{0:T(1024)(128)(2,1)}, u32[]{:S(2)}) copy-start(bf16[1792]{0:T(1024)(128)(2,1)} %param.14) | copy-start | bytes 10756
  8.5 12.1 %copy-start.6 = (s32[8]{0:T(128)S(1)}, s32[8]{0:T(128)}, u32[]{:S(2)}) copy-start(s32[8]{0:T(128)} %counts.1) | copy-start | bytes 100
  11.2 34.1 %copy-start.2 = (bf16[16,8192]{1,0:T(8,128)(2,1)S(1)}, bf16[16,8192]{1,0:T(8,128)(2,1)}, u32[]{:S(2)}) copy-start(bf16[16,8192]{1,0:T(8,128)(2,1)} %param.17) | copy-start | bytes 786436
  11.2 17.0 %all-to-all-start = ((bf16[8,128,384]{2,1,0:T(8,128)(2,1)}), bf16[8,128,384]{2,1,0:T(8,128)(2,1)S(1)}, u32[]{:S(2)}, u32[]{:S(2)}) async-start(bf16[8,128,384]{2,1,0:T(8,128)(2,1)} %pack_slots.1), calls=%async_computation | async-start | bytes 1572864 | tf_op jit(solution)/shard_map/all_to_all | solution.py:162
  20.7 76.5 %all-gather.6.cloned.1.call-start = ((), (), s32[]{:S(2)}) async-start(), calls=%async_computation.4 | async-start | bytes 6684672 | tf_op jit(solution)/shard_map/all_gather | solution.py:167
  46.9 7.1 %copy-start.3 = (bf16[8192]{0:T(1024)(128)(2,1)S(1)}, bf16[8192]{0:T(1024)(128)(2,1)}, u32[]{:S(2)}) copy-start(bf16[8192]{0:T(1024)(128)(2,1)} %param.10) | copy-start | bytes 49156
  46.9 7.1 %copy-start.5 = (s32[8,2]{0,1:T(2,128)S(1)}, s32[8,2]{0,1:T(2,128)}, u32[]{:S(2)}) copy-start(s32[8,2]{0,1:T(2,128)} %param.15) | copy-start | bytes 196
  46.9 36.4 %copy-start.1 = (bf16[128,8192]{1,0:T(8,128)(2,1)S(1)}, bf16[128,8192]{1,0:T(8,128)(2,1)}, u32[]{:S(2)}) copy-start(bf16[128,8192]{1,0:T(8,128)(2,1)} %act.1) | copy-start | bytes 6291460
  46.9 38.8 %all-to-all-start.1 = ((bf16[8,16,8192]{2,1,0:T(8,128)(2,1)}), bf16[8,16,8192]{2,1,0:T(8,128)(2,1)}, u32[]{:S(2)}, u32[]{:S(2)}) async-start(bf16[8,16,8192]{2,1,0:T(8,128)(2,1)} %broadcast_in_dim.55), calls=%async_computation.1 | async-start | bytes 4194304 | tf_op jit(solution)/shard_map/all_to_all | solution.py:174
  105.1 7.0 %copy-start.4 = (f32[8,128]{1,0:T(8,128)S(1)}, f32[8,128]{1,0:T(8,128)}, u32[]{:S(2)}) copy-start(f32[8,128]{1,0:T(8,128)} %get-tuple-element.16) | copy-start | bytes 12292
  105.1 30.9 %all-to-all-start.2 = ((bf16[8,1024,128]{2,1,0:T(8,128)(2,1)}), bf16[8,1024,128]{2,1,0:T(8,128)(2,1)}, u32[]{:S(2)}, u32[]{:S(2)}) async-start(bf16[8,1024,128]{2,1,0:T(8,128)(2,1)} %get-tuple-element.17), calls=%async_computation.2 | async-start | bytes 4194304 | tf_op jit(solution)/shard_map/all_to_all | solution.py:185
  112.1 3.1 %collective-permute-start = (f32[8,128]{1,0:T(8,128)S(1)}, f32[8,128]{1,0:T(8,128)S(1)}, u32[]{:S(2)}, u32[]{:S(2)}) collective-permute-start(f32[8,128]{1,0:T(8,128)S(1)} %copy-done.4), channel_id=1, source_target_pairs={{0,8},{8,0},{1,9},{9,1},{2,10},{10,2},{3,11},{11,3},{4,12},{12,4},... | collective-permute-start | bytes 12296 | tf_op jit(solution)/shard_map/ppermute | solution.py:186
  136.7 16.9 %all-to-all-start.3 = ((f32[32,1,128]{2,1,0:T(1,128)}), f32[32,1,128]{2,1,0:T(1,128)S(1)}, u32[]{:S(2)}, u32[]{:S(2)}) async-start(f32[32,1,128]{2,1,0:T(1,128)} %broadcast_in_dim.60), calls=%async_computation.3 | async-start | bytes 32768 | tf_op jit(solution)/shard_map/all_to_all | solution.py:190
Sparse Core Ops, SparseCore 0:
  45.5 51.6 all-gather.5
